TPU v7x, 256 devices: a whole 4x4x8 slice. The times are simulated.
256 devices in a mesh: video: 4 (over y), tm: 64 (over x, z, core).
Axes of the slice: x: 4, y: 4, z: 8, core: 2. Of those that a mesh axis runs over, the one named last changes fastest.
Arguments:
- bin_grad: bfloat16 [16, 256, 16, 1024], P('video', 'tm'), may hold values from -0.046875 to 0.046875
- tap_weight: float32 [16, 256, 16, 2], P('video', 'tm'), may hold values from 0.05 to 1
- tap_index: int32 [16, 256, 16, 2], P('video', 'tm'), may hold values from 0 to 8191, as said below
- features: bfloat16 [16, 8192, 1024], P('video', 'tm'), may hold values from -6 to 6
- preact: bfloat16 [16, 8192, 1024], P('video', 'tm'), may hold values from -8 to 8
- filter_second: bfloat16 [3, 1024, 1024], replicated, may hold values from -0.109375 to 0.109375
Outputs:
- first_filter_grad: float32 [1024, 3, 1024], P('tm')
- second_filter_grad: float32 [1024, 3, 1024], P('tm')
Inputs may be any that keep to these rules, and one draw needn't show every extreme that they name: `tap_index`: each proposal spans the integer snippets a to a + L for a start a and a length L of 1 or more; the taps of bin b are a + ((2 b + 1) L) // 32 and that snippet plus one. For the proposals held by one device (its 4 videos and 4 proposals of each), at most 32 taps fall into any one block of 128 snippets (snippets 128 * m to 128 * m + 127, taken over its videos together), and exactly 32 into some block.
All inputs are finite; a program needn't handle non-finite values.
Results may differ from a plain program's by a relative error of at most 0.0048.
Values may be sent and summed in bfloat16 or wider, within the bound.
No kernel may reach another device: no remote copies, remote signals or barrier semaphores. Data moves between devices by JAX's collectives and lax.ppermute only.
A program may use at most 192 MiB of HBM per device.

v0:
```python
import jax
import jax.numpy as jnp
import numpy as np
from jax import lax
from jax.experimental import pallas as pl
from jax.experimental.pallas import tpu as pltpu
from jax.sharding import Mesh
from jax.sharding import PartitionSpec as P

TM = ("x", "z", "core")
TM_SIZES = (4, 8, 2)
META = 128


def silu_slope(values):
    sigma = jax.nn.sigmoid(values)
    return sigma * (1.0 + values * (1.0 - sigma))


def neighbours(value, forward):
    count = lax.axis_size(TM)
    pairs = [(i, i + 1) for i in range(count - 1)]
    if not forward:
        pairs = [(j, i) for i, j in pairs]
    return lax.ppermute(value, TM, pairs)


def ring_shift(value, axis, shift):
    count = lax.axis_size(axis)
    return lax.ppermute(value, axis, [(i, (i + shift) % count) for i in range(count)])


def exchange(value, axis):
    return lax.all_to_all(value, axis, split_axis=0, concat_axis=0, tiled=True)


def route(first_tap, snip_count, unit_axis):
    count = first_tap[0].shape[0]
    col, row = first_tap
    mine, other = (col, row) if unit_axis == 0 else (row, col)
    reduce_axis = 1 - unit_axis
    block, block_other = mine // snip_count, other // snip_count
    crossing = mine % snip_count == snip_count - 1
    crossing_other = other % snip_count == snip_count - 1
    earlier = lax.broadcasted_iota(jnp.int32, (count, count), reduce_axis) < lax.broadcasted_iota(
        jnp.int32, (count, count), unit_axis
    )
    rank = jnp.sum(
        ((block == block_other) & crossing_other & earlier).astype(jnp.int32),
        axis=reduce_axis,
        keepdims=True,
    )
    target = block + (crossing & (rank % 2 == 1)).astype(jnp.int32)
    return target, mine - target * snip_count


def halved(value):
    high = lax.reduce_precision(value, 8, 7)
    rest = value - high
    middle = lax.reduce_precision(rest, 8, 7)
    return high, middle, rest - middle


def send_slots(bin_grad, tap_weight, tap_index, snip_count, peers):
    video_count, prop_count, bin_count, tap_count = tap_index.shape
    channels = bin_grad.shape[-1]
    units = video_count * prop_count * bin_count
    capacity = bin_count * ((video_count * prop_count + peers - 1) // peers)
    first = tap_index[..., 0].reshape(units)
    taps = (first[:, None], first[None, :])
    target_col, local = route(taps, snip_count, 0)
    target_row, _ = route(taps, snip_count, 1)
    earlier = lax.broadcasted_iota(jnp.int32, (units, units), 0) < lax.broadcasted_iota(
        jnp.int32, (units, units), 1
    )
    position = jnp.sum(
        ((target_col == target_row) & earlier).astype(jnp.int32), axis=0, keepdims=True
    )
    slot = target_row * capacity + position
    matches = (
        lax.broadcasted_iota(jnp.int32, (peers * capacity, units), 0) == slot
    ).astype(jnp.bfloat16)
    video = lax.broadcasted_iota(jnp.int32, (units, 1), 0) // (prop_count * bin_count)
    main = video_count * snip_count

    def line(step):
        at = local + step
        inside = video * snip_count + at
        edge = main + video + jnp.where(at < 0, 0, video_count)
        return jnp.where((at < 0) | (at >= snip_count), edge, inside)

    weights = tap_weight.reshape(units, tap_count)
    columns = []
    for step in range(2):
        where_to = line(step)
        columns += [(where_to // 256).astype(jnp.float32), (where_to % 256).astype(jnp.float32)]
        columns += list(halved(weights[:, step : step + 1]))
    lane = lax.broadcasted_iota(jnp.int32, (units, META), 1)
    meta = jnp.zeros((units, META), jnp.float32)
    for index, column in enumerate(columns):
        meta = jnp.where(lane == index, column, meta)
    payload = jnp.concatenate([bin_grad.reshape(units, channels), meta.astype(jnp.bfloat16)], axis=1)
    rows = jnp.dot(matches, payload, preferred_element_type=jnp.float32).astype(jnp.bfloat16)
    return rows.reshape(peers, capacity, channels + META)


def collect(got, channels, row_count):
    rows = got.reshape(-1, channels + META)
    grads = rows[:, :channels].astype(jnp.float32)
    meta = rows[:, channels:].astype(jnp.float32)
    meta_t = meta[:, :16].T
    total = jnp.zeros((row_count, channels), jnp.float32)
    for step in range(2):
        base = 5 * step
        where_to = (meta_t[base : base + 1] * 256.0 + meta_t[base + 1 : base + 2]).astype(jnp.int32)
        weight = meta[:, base + 2 : base + 3] + meta[:, base + 3 : base + 4] + meta[:, base + 4 : base + 5]
        tap_rows = (weight * grads).astype(jnp.bfloat16)
        table = (
            lax.broadcasted_iota(jnp.int32, (row_count, rows.shape[0]), 0) == where_to
        ).astype(jnp.bfloat16)
        total = total + jnp.dot(table, tap_rows, preferred_element_type=jnp.float32)
    return total


def finish_kernel(part_ref, low_in_ref, high_in_ref, after_ref, main_ref, before_ref, share_ref):
    videos, quarters = low_in_ref.shape[1], share_ref.shape[0]
    rows = main_ref.shape[0] // videos
    width = share_ref.shape[2]
    edges = part_ref.shape[0] - 2 * videos
    row = lax.broadcasted_iota(jnp.int32, (rows, part_ref.shape[1]), 0)
    lows, highs = [], []
    for video in range(videos):
        span = slice(video * rows, (video + 1) * rows)
        main = part_ref[span, :]
        main = main + jnp.where(row == 0, low_in_ref[1, video : video + 1, :], 0.0)
        main = main + jnp.where(row == rows - 1, high_in_ref[0, video : video + 1, :], 0.0)
        low = part_ref[edges + video : edges + video + 1, :] + low_in_ref[0, video : video + 1, :]
        high_at = edges + videos + video
        high = part_ref[high_at : high_at + 1, :] + high_in_ref[1, video : video + 1, :]
        before_ref[span, :] = jnp.where(row == 0, low, pltpu.roll(main, 1, 0)).astype(jnp.bfloat16)
        after_ref[span, :] = jnp.where(row == rows - 1, high, pltpu.roll(main, rows - 1, 0)).astype(
            jnp.bfloat16
        )
        main = main.astype(jnp.bfloat16)
        main_ref[span, :] = main
        for quarter in range(quarters):
            share_ref[quarter, span, :] = main[:, quarter * width : (quarter + 1) * width]
        lows.append(low)
        highs.append(high)
    pad = share_ref.shape[1] - edges - 2 * videos
    edge = jnp.concatenate(lows + highs + [jnp.zeros((pad, part_ref.shape[1]), jnp.float32)], axis=0)
    edge = edge.astype(jnp.bfloat16)
    for quarter in range(quarters):
        share_ref[quarter, edges:, :] = edge[:, quarter * width : (quarter + 1) * width]


def finish(partial, from_low, from_high, main_rows, quarters):
    channels = partial.shape[1]
    full = jax.ShapeDtypeStruct((main_rows, channels), jnp.bfloat16)
    share = jax.ShapeDtypeStruct((quarters, main_rows + 16, channels // quarters), jnp.bfloat16)
    return pl.pallas_call(
        finish_kernel,
        out_shape=(full, full, full, share),
        compiler_params=pltpu.CompilerParams(vmem_limit_bytes=40 * 2**20),
        cost_estimate=pl.CostEstimate(flops=0, bytes_accessed=8 * 2**20, transcendentals=0),
    )(partial, from_low, from_high)


def lags_kernel(videos, halo, grad_ref, out_ref):
    sources, block, width = grad_ref.shape
    rows = (block if not halo else block - 16) // videos
    main = rows * videos
    row = lax.broadcasted_iota(jnp.int32, (rows, width), 0)
    for source in range(sources):
        edge_low, edge_high = [], []
        if halo:
            edges = grad_ref[source, main:, :].astype(jnp.float32)
        for video in range(videos):
            span = slice(video * rows, (video + 1) * rows)
            grad = grad_ref[source, span, :].astype(jnp.float32)
            if halo:
                low, high = edges[video : video + 1], edges[videos + video : videos + video + 1]
            else:
                low, high = 0.0, 0.0
                edge_low.append(grad[:1])
                edge_high.append(grad[rows - 1 :])
            after = jnp.where(row == rows - 1, high, pltpu.roll(grad, rows - 1, 0))
            before = jnp.where(row == 0, low, pltpu.roll(grad, 1, 0))
            for index, part in enumerate((after, grad, before)):
                out_ref[source, span, index * width : (index + 1) * width] = part.astype(jnp.bfloat16)
        if not halo:
            zero = jnp.zeros((videos, width), jnp.float32)
            rest = jnp.zeros((out_ref.shape[1] - main - 2 * videos, width), jnp.float32)
            parts = (edge_low + [zero, rest], [zero, zero, rest], [zero] + edge_high + [rest])
            for index, part in enumerate(parts):
                out_ref[source, main:, index * width : (index + 1) * width] = jnp.concatenate(
                    part, axis=0
                ).astype(jnp.bfloat16)


def lags(gradient, videos, halo, lag_count):
    sources, block, width = gradient.shape
    rows = block - 16 if halo else block + 16
    return pl.pallas_call(
        lambda *refs: lags_kernel(videos, halo, *refs),
        out_shape=jax.ShapeDtypeStruct((sources, rows, lag_count * width), jnp.bfloat16),
        compiler_params=pltpu.CompilerParams(vmem_limit_bytes=40 * 2**20),
        cost_estimate=pl.CostEstimate(flops=0, bytes_accessed=4 * 2**20, transcendentals=0),
    )(gradient)


def filter_terms(inputs, lagged):
    inputs = inputs.reshape(-1, inputs.shape[-1])
    lagged = lagged.reshape(-1, lagged.shape[-1])
    return lax.dot_general(
        inputs, lagged, (((0,), (0,)), ((), ())), preferred_element_type=jnp.float32
    )


def reduce_core_x(terms):
    x_total, z_total, cores = (lax.axis_size(name) for name in TM)
    channels, outs = terms.shape
    each = channels // (x_total * z_total * cores)
    parts = terms.reshape(x_total * z_total, cores, each, outs)
    core = lax.axis_index("core")
    keep = lax.dynamic_index_in_dim(parts, core, 1, keepdims=False)
    give = lax.dynamic_index_in_dim(parts, 1 - core, 1, keepdims=False).astype(jnp.bfloat16)
    got = ring_shift(give, "core", 1)
    share = (keep + got.astype(jnp.float32)).astype(jnp.bfloat16)
    share = exchange(share.reshape(x_total, z_total * each, outs), "x")
    return jnp.sum(share.astype(jnp.float32), axis=0).reshape(z_total, each, outs)


def on_device(bin_grad, tap_weight, tap_index, features, preact, filter_second):
    video_count, snip_count, channels = features.shape
    peers = lax.axis_size(TM)
    quarters = lax.axis_size("video")
    lag_count = filter_second.shape[0]
    main_rows = video_count * snip_count
    sent = send_slots(bin_grad, tap_weight, tap_index, snip_count, peers)
    got = exchange(sent, TM)

    pre_values = preact.astype(jnp.float32).reshape(main_rows, channels)
    activation = jax.nn.silu(pre_values).astype(jnp.bfloat16)
    act_all = lax.all_gather(activation, "video", axis=0, tiled=False)
    after_send = sent[0, 0, 0] * 0
    edge_low = neighbours(features[:, -1] + after_send, True)
    edge_high = neighbours(features[:, 0] + after_send, False)
    spare = jnp.zeros((16 - 2 * video_count, channels), features.dtype)
    feature_rows = jnp.concatenate(
        [features.reshape(main_rows, channels), edge_low, edge_high, spare], axis=0
    )
    feature_all = lax.all_gather(feature_rows, "video", axis=0, tiled=False)

    partial = collect(got, channels, main_rows + 2 * video_count)
    ends = partial[:main_rows].reshape(video_count, snip_count, channels)
    low = partial[main_rows : main_rows + video_count]
    high = partial[main_rows + video_count :]
    from_low = neighbours(jnp.stack([ends[:, -1], high]), True)
    from_high = neighbours(jnp.stack([low, ends[:, 0]]), False)
    *windows, snippet_share = finish(partial, from_low, from_high, main_rows, quarters)
    snippet_share = exchange(snippet_share, "video")

    act_grad = jnp.zeros((main_rows, channels), jnp.float32)
    for window, taps in zip(windows, filter_second):
        act_grad = act_grad + lax.dot_general(
            window, taps, (((1,), (1,)), ((), ())), preferred_element_type=jnp.float32
        )
    pre_grad = (act_grad * silu_slope(pre_values)).astype(jnp.bfloat16)
    width = channels // quarters
    pre_share = jnp.stack([pre_grad[:, q * width : (q + 1) * width] for q in range(quarters)])
    pre_share = exchange(pre_share, "video")

    second = reduce_core_x(filter_terms(act_all, lags(snippet_share, video_count, True, lag_count)))
    first = reduce_core_x(filter_terms(feature_all, lags(pre_share, video_count, False, lag_count)))
    both = jnp.stack([first, second], axis=1).astype(jnp.bfloat16)
    mine = jnp.sum(exchange(both, "z").astype(jnp.float32), axis=0)

    place = lax.axis_index("video")
    held = [mine] + [ring_shift(mine, "video", shift) for shift in range(1, quarters)]
    blocks = []
    for quarter in range(quarters):
        block = held[0]
        for shift in range(1, quarters):
            block = jnp.where((place - shift) % quarters == quarter, held[shift], block)
        blocks.append(block.reshape(2, -1, lag_count, width))
    whole = jnp.concatenate(blocks, axis=-1)
    return (whole[0], whole[1])


def solution(mesh):
    shape = (mesh.shape["video"],) + TM_SIZES
    fine = Mesh(np.asarray(mesh.devices).reshape(shape), ("video",) + TM)
    return jax.shard_map(
        on_device,
        mesh=fine,
        in_specs=(
            P("video", TM, None, None),
            P("video", TM, None, None),
            P("video", TM, None, None),
            P("video", TM, None),
            P("video", TM, None),
            P(),
        ),
        out_specs=(P(TM, None, None), P(TM, None, None)),
        check_vma=False,
    )
```

profile of v0, /device:TPU:2, one launch (start us, length us, event | category | flops | bytes accessed | tf_op | source)
XLA Modules:
  0.0 258.1 jit_solution(10141078807202542169)
XLA Ops:
  8.7 1.5 fusion.27
  11.5 2.3 convolution_convert_fusion
  13.8 12.2 %all-to-all-start = ((bf16[64,16,1152]{2,1,0:T(8,128)(2,1)}), bf16[64,16,1152]{2,1,0:T(8,128)(2,1)S(1)}, u32[]{:S(2)}, u32[]{:S(2)}) async-start(bf16[64,16,1152]{2,1,0:T(8,128)(2,1)} %bitcast.8), calls=%async_computation | async-start | bytes 4718592 | tf_op jit(solution)/shard_map/all_to_all | solution.py:34
  27.9 2.1 collective-permute-start
  30.0 5.6 %collective-permute-start.1 = (bf16[4,1024]{1,0:T(4,128)(2,1)S(1)}, bf16[4,1024]{1,0:T(4,128)(2,1)S(1)}, u32[]{:S(2)}, u32[]{:S(2)}) collective-permute-start(bf16[4,1024]{1,0:T(4,128)(2,1)S(1)} %bitcast.145), channel_id=1, source_target_pairs={{1,0},{2,1},{3,2},{4,3},{5,4},{6,5},{7,6},{8,7},{9,8},{10,9},{11,1... | collective-permute-start | bytes 24584 | tf_op jit(solution)/shard_map/ppermute | solution.py:25
  35.7 42.6 %collective-permute-done = bf16[4,1024]{1,0:T(4,128)(2,1)S(1)} collective-permute-done((bf16[4,1024]{1,0:T(4,128)(2,1)S(1)}, bf16[4,1024]{1,0:T(4,128)(2,1)S(1)}, u32[]{:S(2)}, u32[]{:S(2)}) %collective-permute-start) | collective-permute-done | bytes 8224 | tf_op jit(solution)/shard_map/ppermute | solution.py:25
  79.5 1.6 all-to-all-done
  86.2 3.3 %collective-permute-start.3 = (f32[2,4,1024]{2,1,0:T(4,128)S(1)}, f32[2,4,1024]{2,1,0:T(4,128)S(1)}, u32[]{:S(2)}, u32[]{:S(2)}) collective-permute-start(f32[2,4,1024]{2,1,0:T(4,128)S(1)} %pad_maximum_fusion.3), channel_id=1, source_target_pairs={{1,0},{2,1},{3,2},{4,3},{5,4},{6,5},{7,6},{8,7},{9,8},{10,9},{11,1... | collective-permute-start | bytes 98312 | tf_op jit(solution)/shard_map/ppermute | solution.py:25
  89.5 2.3 collective-permute-start.2
  91.9 5.0 %collective-permute-done.2.low_in_ref = f32[2,4,1024]{2,1,0:T(4,128)S(1)} collective-permute-done((f32[2,4,1024]{2,1,0:T(4,128)S(1)}, f32[2,4,1024]{2,1,0:T(4,128)S(1)}, u32[]{:S(2)}, u32[]{:S(2)}) %collective-permute-start.2) | collective-permute-done | bytes 32800 | tf_op jit(solution)/shard_map/ppermute | solution.py:25
  100.8 1.8 fusion.15
  102.8 30.8 %all_to_all.30.refs_0_ = bf16[4,512,256]{2,1,0:T(8,128)(2,1)S(1)} all-to-all(bf16[4,512,256]{2,1,0:T(8,128)(2,1)S(1)} %pad_maximum_fusion), channel_id=1, replica_groups=mesh['video'=4,'x'=4,'z'=8,'core'=2] {'video'}, dimensions={0} | all-to-all | bytes 2097152 | tf_op jit(solution)/shard_map/all_to_all | solution.py:34
  133.6 3.5 %all-to-all-start.3 = ((bf16[4,528,256]{2,1,0:T(8,128)(2,1)}), bf16[4,528,256]{2,1,0:T(8,128)(2,1)S(1)}, u32[]{:S(2)}, u32[]{:S(2)}) async-start(bf16[4,528,256]{2,1,0:T(8,128)(2,1)} %get-tuple-element.9), calls=%async_computation.3 | async-start | bytes 2162688 | tf_op jit(solution)/shard_map/all_to_all | solution.py:34
  137.6 1.6 copy-done
  139.2 15.9 %all-to-all-done.3.refs_0_ = bf16[4,528,256]{2,1,0:T(8,128)(2,1)S(1)} async-done(((bf16[4,528,256]{2,1,0:T(8,128)(2,1)}), bf16[4,528,256]{2,1,0:T(8,128)(2,1)S(1)}, u32[]{:S(2)}, u32[]{:S(2)}) %all-to-all-start.3) | async-done | bytes 1081376 | tf_op jit(solution)/shard_map/all_to_all | solution.py:34
  155.6 1.7 copy-done.2
  157.3 6.7 %copy.42 = bf16[2048,1024]{0,1:T(8,128)(2,1)} copy(bf16[2048,1024]{1,0:T(8,128)(2,1)} %bitcast.132) | data formatting | bytes 8388608 | tf_op jit(solution)/shard_map/reshape | solution.py:213
  164.0 5.2 %fusion.67 = f32[32,2,16,768]{3,2,1,0:T(8,128)S(1)} fusion(bf16[32,2,16,2048]{3,2,1,0:T(8,128)(2,1)} %bitcast.133, bf16[2048,768,1,1]{1,0,3,2:T(8,128)(2,1)S(1)} %bitcast.128), kind=kOutput, calls=%fused_computation.174 | convolution fusion | flops 3221225472 | bytes 10485760 | tf_op jit(solution)/shard_map/dot_general | solution.py:215
  169.2 1.6 copy-done.4
  171.8 6.7 %copy.39 = bf16[1024,2112]{1,0:T(8,128)(2,1)} copy(bf16[1024,2112]{0,1:T(8,128)(2,1)} %bitcast.131) | data formatting | bytes 8650752 | tf_op jit(solution)/shard_map/dot_general | solution.py:215
  178.5 5.6 %fusion.66 = f32[32,2,16,768]{3,2,1,0:T(8,128)S(1)} fusion(bf16[32,2,16,2112]{3,2,1,0:T(8,128)(2,1)} %bitcast.130, bf16[2112,768,1,1]{1,0,3,2:T(8,128)(2,1)S(1)} %bitcast.127), kind=kOutput, calls=%fused_computation.173 | convolution fusion | flops 3321888768 | bytes 10715136 | tf_op jit(solution)/shard_map/dot_general | solution.py:215
  184.2 1.6 copy-done.5
  186.5 2.8 %fusion.30 = bf16[32,16,768]{2,1,0:T(8,128)(2,1)} fusion(bf16[32,16,768]{2,1,0:T(8,128)(2,1)} %collective-permute-done.5, f32[32,2,16,768]{3,2,1,0:T(8,128)} %copy-done.4, s32[]{:T(128)S(6)} %select_n.393), kind=kLoop, calls=%fused_computation.38 | loop fusion | flops 1179648 | bytes 3145732 | tf_op jit(solution)/shard_map/convert_element_type | solution.py:229
  189.2 4.8 %all-to-all-start.4 = ((bf16[4,128,768]{2,1,0:T(8,128)(2,1)}), bf16[4,128,768]{2,1,0:T(8,128)(2,1)S(1)}, u32[]{:S(2)}, u32[]{:S(2)}) async-start(bf16[4,128,768]{2,1,0:T(8,128)(2,1)} %bitcast.43), calls=%async_computation.4 | async-start | bytes 1572864 | tf_op jit(solution)/shard_map/all_to_all | solution.py:34
  194.0 2.5 fusion.31
  196.6 8.5 %all-to-all-done.4 = bf16[4,128,768]{2,1,0:T(8,128)(2,1)S(1)} async-done(((bf16[4,128,768]{2,1,0:T(8,128)(2,1)}), bf16[4,128,768]{2,1,0:T(8,128)(2,1)S(1)}, u32[]{:S(2)}, u32[]{:S(2)}) %all-to-all-start.4) | async-done | bytes 786464 | tf_op jit(solution)/shard_map/all_to_all | solution.py:34
  205.1 4.9 %all-to-all-start.2 = ((bf16[4,128,768]{2,1,0:T(8,128)(2,1)}), bf16[4,128,768]{2,1,0:T(8,128)(2,1)S(1)}, u32[]{:S(2)}, u32[]{:S(2)}) async-start(bf16[4,128,768]{2,1,0:T(8,128)(2,1)} %bitcast.32), calls=%async_computation.2 | async-start | bytes 1572864 | tf_op jit(solution)/shard_map/all_to_all | solution.py:34
  210.1 10.0 %all-to-all-done.2 = bf16[4,128,768]{2,1,0:T(8,128)(2,1)S(1)} async-done(((bf16[4,128,768]{2,1,0:T(8,128)(2,1)}), bf16[4,128,768]{2,1,0:T(8,128)(2,1)S(1)}, u32[]{:S(2)}, u32[]{:S(2)}) %all-to-all-start.2) | async-done | bytes 786464 | tf_op jit(solution)/shard_map/all_to_all | solution.py:34
  220.3 19.3 %all_to_all.31 = bf16[8,2,16,768]{3,2,1,0:T(8,128)(2,1)S(1)} all-to-all(bf16[8,2,16,768]{3,2,1,0:T(8,128)(2,1)S(1)} %pad_maximum_fusion.1), channel_id=1, replica_groups=mesh['video'=4,'x'=4,'z'=8,'core'=2] {'z'}, dimensions={0} | all-to-all | bytes 786432 | tf_op jit(solution)/shard_map/all_to_all | solution.py:34
  239.7 2.1 collective-permute-start.6
  243.3 1.7 collective-permute-done.6
  245.0 2.9 %collective-permute-done.7 = f32[2,16,768]{2,1,0:T(8,128)S(1)} collective-permute-done((f32[2,16,768]{2,1,0:T(8,128)S(1)}, f32[2,16,768]{2,1,0:T(8,128)S(1)}, u32[]{:S(2)}, u32[]{:S(2)}) %collective-permute-start.7) | collective-permute-done | bytes 98336 | tf_op jit(solution)/shard_map/ppermute | solution.py:30
  (103 shorter events, 22.0 us)
Async XLA Ops:
  7.2 150.1 %all-gather.4.cloned.1.call-start = ((), (), s32[]{:S(2)}) async-start(), calls=%async_computation.6 | async-start | bytes 5242880 | tf_op jit(solution)/shard_map/all_gather | solution.py:245
  8.7 1.6 copy-start.10
  8.7 2.0 copy-start.9
  8.7 2.7 %copy-start.8 = (bf16[4,4,16,1024]{3,2,1,0:T(8,128)(2,1)S(1)}, bf16[4,4,16,1024]{3,2,1,0:T(8,128)(2,1)}, u32[]{:S(2)}) copy-start(bf16[4,4,16,1024]{3,2,1,0:T(8,128)(2,1)} %param.6) | copy-start | bytes 1572868
  13.7 14.1 %copy-start.6 = (bf16[4,128,1024]{2,1,0:T(8,128)(2,1)S(1)}, bf16[4,128,1024]{2,1,0:T(8,128)(2,1)}, u32[]{:S(2)}) copy-start(bf16[4,128,1024]{2,1,0:T(8,128)(2,1)} %param.9) | copy-start | bytes 3145732
  13.8 67.4 %all-to-all-start = ((bf16[64,16,1152]{2,1,0:T(8,128)(2,1)}), bf16[64,16,1152]{2,1,0:T(8,128)(2,1)S(1)}, u32[]{:S(2)}, u32[]{:S(2)}) async-start(bf16[64,16,1152]{2,1,0:T(8,128)(2,1)} %bitcast.8), calls=%async_computation | async-start | bytes 4718592 | tf_op jit(solution)/shard_map/all_to_all | solution.py:34
  25.9 145.9 %all-gather.6.cloned.1.call-start = ((), (), s32[]{:S(2)}) async-start(), calls=%async_computation.7 | async-start | bytes 5406720 | tf_op jit(solution)/shard_map/all_gather | solution.py:253
  27.9 50.4 %collective-permute-start = (bf16[4,1024]{1,0:T(4,128)(2,1)S(1)}, bf16[4,1024]{1,0:T(4,128)(2,1)S(1)}, u32[]{:S(2)}, u32[]{:S(2)}) collective-permute-start(bf16[4,1024]{1,0:T(4,128)(2,1)S(1)} %bitcast.144), channel_id=1, source_target_pairs={{0,1},{1,2},{2,3},{3,4},{4,5},{5,6},{6,7},{7,8},{8,9},{9,10},{10,1... | collective-permute-start | bytes 24584 | tf_op jit(solution)/shard_map/ppermute | solution.py:25
  30.0 48.3 %collective-permute-start.1 = (bf16[4,1024]{1,0:T(4,128)(2,1)S(1)}, bf16[4,1024]{1,0:T(4,128)(2,1)S(1)}, u32[]{:S(2)}, u32[]{:S(2)}) collective-permute-start(bf16[4,1024]{1,0:T(4,128)(2,1)S(1)} %bitcast.145), channel_id=1, source_target_pairs={{1,0},{2,1},{3,2},{4,3},{5,4},{6,5},{7,6},{8,7},{9,8},{10,9},{11,1... | collective-permute-start | bytes 24584 | tf_op jit(solution)/shard_map/ppermute | solution.py:25
  84.6 13.6 %slice-start = ((s8[6291456]{0:T(1024)(128)(4,1)}), s8[4194304]{0:T(1024)(128)(4,1)S(1)}, s32[]{:S(2)}) async-start(s8[6291456]{0:T(1024)(128)(4,1)} %bitcast.152), calls=%async_computation.8 | async-start | bytes 8388608
  84.6 13.6 %slice-start.1 = ((s8[6291456]{0:T(1024)(128)(4,1)}), s8[2097152]{0:T(1024)(128)(4,1)S(1)}, s32[]{:S(2)}) async-start(s8[6291456]{0:T(1024)(128)(4,1)} %bitcast.152), calls=%async_computation.9 | async-start | bytes 4194304
  86.2 5.7 %collective-permute-start.3 = (f32[2,4,1024]{2,1,0:T(4,128)S(1)}, f32[2,4,1024]{2,1,0:T(4,128)S(1)}, u32[]{:S(2)}, u32[]{:S(2)}) collective-permute-start(f32[2,4,1024]{2,1,0:T(4,128)S(1)} %pad_maximum_fusion.3), channel_id=1, source_target_pairs={{1,0},{2,1},{3,2},{4,3},{5,4},{6,5},{7,6},{8,7},{9,8},{10,9},{11,1... | collective-permute-start | bytes 98312 | tf_op jit(solution)/shard_map/ppermute | solution.py:25
  89.5 7.3 %collective-permute-start.2 = (f32[2,4,1024]{2,1,0:T(4,128)S(1)}, f32[2,4,1024]{2,1,0:T(4,128)S(1)}, u32[]{:S(2)}, u32[]{:S(2)}) collective-permute-start(f32[2,4,1024]{2,1,0:T(4,128)S(1)} %pad_maximum_fusion.2), channel_id=1, source_target_pairs={{0,1},{1,2},{2,3},{3,4},{4,5},{5,6},{6,7},{7,8},{8,9},{9,10},{10,1... | collective-permute-start | bytes 98312 | tf_op jit(solution)/shard_map/ppermute | solution.py:25
  99.5 1.3 copy-start.7
  133.6 21.6 %all-to-all-start.3 = ((bf16[4,528,256]{2,1,0:T(8,128)(2,1)}), bf16[4,528,256]{2,1,0:T(8,128)(2,1)S(1)}, u32[]{:S(2)}, u32[]{:S(2)}) async-start(bf16[4,528,256]{2,1,0:T(8,128)(2,1)} %get-tuple-element.9), calls=%async_computation.3 | async-start | bytes 2162688 | tf_op jit(solution)/shard_map/all_to_all | solution.py:34
  137.6 1.7 copy-start
  155.6 1.7 copy-start.2
  157.3 6.7 %copy-start.3 = (bf16[4,512,768]{2,1,0:T(8,128)(2,1)S(1)}, bf16[4,512,768]{2,1,0:T(8,128)(2,1)}, u32[]{:S(2)}) copy-start(bf16[4,512,768]{2,1,0:T(8,128)(2,1)} %copy-done.2) | copy-start | bytes 9437188
  169.2 1.6 copy-start.4
  171.8 14.7 %collective-permute-start.5 = (bf16[32,16,768]{2,1,0:T(8,128)(2,1)}, bf16[32,16,768]{2,1,0:T(8,128)(2,1)}, u32[]{:S(2)}, u32[]{:S(2)}) collective-permute-start(bf16[32,16,768]{2,1,0:T(8,128)(2,1)} %fusion.38), channel_id=1, source_target_pairs={{0,1},{1,0},{2,3},{3,2},{4,5},{5,4},{6,7},{7,6},{8,9},{9,8},{10,11... | collective-permute-start | bytes 2359304 | tf_op jit(solution)/shard_map/ppermute | solution.py:30
  171.8 6.7 %copy-start.1 = (bf16[4,528,768]{2,1,0:T(8,128)(2,1)S(1)}, bf16[4,528,768]{2,1,0:T(8,128)(2,1)}, u32[]{:S(2)}) copy-start(bf16[4,528,768]{2,1,0:T(8,128)(2,1)} %copy-done) | copy-start | bytes 9732100
  184.2 1.6 copy-start.5
  185.9 8.1 %collective-permute-start.4 = (bf16[32,16,768]{2,1,0:T(8,128)(2,1)S(1)}, bf16[32,16,768]{2,1,0:T(8,128)(2,1)S(1)}, u32[]{:S(2)}, u32[]{:S(2)}) collective-permute-start(bf16[32,16,768]{2,1,0:T(8,128)(2,1)S(1)} %fusion.37), channel_id=1, source_target_pairs={{0,1},{1,0},{2,3},{3,2},{4,5},{5,4},{6,7},{7,6},{8,9},{9,8},{10,11... | collective-permute-start | bytes 2359304 | tf_op jit(solution)/shard_map/ppermute | solution.py:30
  189.2 15.8 %all-to-all-start.4 = ((bf16[4,128,768]{2,1,0:T(8,128)(2,1)}), bf16[4,128,768]{2,1,0:T(8,128)(2,1)S(1)}, u32[]{:S(2)}, u32[]{:S(2)}) async-start(bf16[4,128,768]{2,1,0:T(8,128)(2,1)} %bitcast.43), calls=%async_computation.4 | async-start | bytes 1572864 | tf_op jit(solution)/shard_map/all_to_all | solution.py:34
  205.1 15.1 %all-to-all-start.2 = ((bf16[4,128,768]{2,1,0:T(8,128)(2,1)}), bf16[4,128,768]{2,1,0:T(8,128)(2,1)S(1)}, u32[]{:S(2)}, u32[]{:S(2)}) async-start(bf16[4,128,768]{2,1,0:T(8,128)(2,1)} %bitcast.32), calls=%async_computation.2 | async-start | bytes 1572864 | tf_op jit(solution)/shard_map/all_to_all | solution.py:34
  239.7 5.3 %collective-permute-start.6 = (f32[2,16,768]{2,1,0:T(8,128)S(1)}, f32[2,16,768]{2,1,0:T(8,128)S(1)}, u32[]{:S(2)}, u32[]{:S(2)}) collective-permute-start(f32[2,16,768]{2,1,0:T(8,128)S(1)} %convert_reduce_fusion), channel_id=1, source_target_pairs={{0,192},{64,0},{128,64},{192,128},{1,193},{65,1},{129,65},{193,129... | collective-permute-start | bytes 294920 | tf_op jit(solution)/shard_map/ppermute | solution.py:30
  241.7 6.1 %collective-permute-start.7 = (f32[2,16,768]{2,1,0:T(8,128)S(1)}, f32[2,16,768]{2,1,0:T(8,128)S(1)}, u32[]{:S(2)}, u32[]{:S(2)}) collective-permute-start(f32[2,16,768]{2,1,0:T(8,128)S(1)} %convert_reduce_fusion), channel_id=1, source_target_pairs={{0,128},{64,192},{128,0},{192,64},{1,129},{65,193},{129,1},{193,65... | collective-permute-start | bytes 294920 | tf_op jit(solution)/shard_map/ppermute | solution.py:30
  243.3 5.8 %collective-permute-start.8 = (f32[2,16,768]{2,1,0:T(8,128)S(1)}, f32[2,16,768]{2,1,0:T(8,128)S(1)}, u32[]{:S(2)}, u32[]{:S(2)}) collective-permute-start(f32[2,16,768]{2,1,0:T(8,128)S(1)} %convert_reduce_fusion), channel_id=1, source_target_pairs={{0,64},{64,128},{128,192},{192,0},{1,65},{65,129},{129,193},{193,1... | collective-permute-start | bytes 294920 | tf_op jit(solution)/shard_map/ppermute | solution.py:30
Sparse Core Ops, SparseCore 0:
  10.4 53.7 all-gather.3
  79.7 68.6 all-gather.5
where the time goes:
time: 259 us; the launch traced here: 258 us
  waiting for transfers between devices  89.5 us (35%)
  blocking collectives  50.1 us (19%)
  starting transfers between devices  42.9 us (17%)
  local copies, waits for them, and re-layouts  24.9 us (10%)
  matrix products  20.3 us (8%)
  between operations  15.3 us (6%)
  other arithmetic  12.9 us (5%)
    all_to_all x2, blocking collectives, exchange(): return lax.all_to_all(value, axis, split_axis=0, concat_axis=0, tiled=True)  50.1 us
    ppermute x4, waiting for transfers between devices, neighbours(): return lax.ppermute(value, TM, pairs)  47.6 us
    all_to_all x4, waiting for transfers between devices, exchange(): return lax.all_to_all(value, axis, split_axis=0, concat_axis=0, tiled=True)  36.1 us
    all_to_all x4, starting transfers between devices, exchange(): return lax.all_to_all(value, axis, split_axis=0, concat_axis=0, tiled=True)  25.4 us
    ppermute x4, starting transfers between devices, neighbours(): return lax.ppermute(value, TM, pairs)  13.3 us
    dot_general x2, matrix products, filter_terms(): lax.dot_general(inputs, lagged, (((0,), (0,)), ((), ())), preferred_eleme...  10.8 us
    unnamed x36, local copies, waits for them, and re-layouts  8.3 us
    reshape x1, local copies, waits for them, and re-layouts, filter_terms(): inputs = inputs.reshape(-1, inputs.shape[-1])  6.69 us
  transfers between devices with their start and end apart: 15, of which 9 were waited for; matrix products, arithmetic and copies ran while one was open for 18% of the time, Pallas kernels for 1%

commit v1 on v0

--- a/solution.py
+++ b/solution.py
@@ -124,39 +124,44 @@
 
 def finish_kernel(part_ref, low_in_ref, high_in_ref, after_ref, main_ref, before_ref, share_ref):
     videos, quarters = low_in_ref.shape[1], share_ref.shape[0]
-    rows = main_ref.shape[0] // videos
     width = share_ref.shape[2]
     edges = part_ref.shape[0] - 2 * videos
+    rows = edges // videos
     row = lax.broadcasted_iota(jnp.int32, (rows, part_ref.shape[1]), 0)
-    lows, highs = [], []
+    low_edges, high_edges = ([], [], []), ([], [], [])
     for video in range(videos):
         span = slice(video * rows, (video + 1) * rows)
         main = part_ref[span, :]
-        main = main + jnp.where(row == 0, low_in_ref[1, video : video + 1, :], 0.0)
+        main = main + jnp.where(row == 0, low_in_ref[2, video : video + 1, :], 0.0)
         main = main + jnp.where(row == rows - 1, high_in_ref[0, video : video + 1, :], 0.0)
-        low = part_ref[edges + video : edges + video + 1, :] + low_in_ref[0, video : video + 1, :]
+        low = part_ref[edges + video : edges + video + 1, :] + low_in_ref[1, video : video + 1, :]
         high_at = edges + videos + video
         high = part_ref[high_at : high_at + 1, :] + high_in_ref[1, video : video + 1, :]
         before_ref[span, :] = jnp.where(row == 0, low, pltpu.roll(main, 1, 0)).astype(jnp.bfloat16)
         after_ref[span, :] = jnp.where(row == rows - 1, high, pltpu.roll(main, rows - 1, 0)).astype(
             jnp.bfloat16
         )
+        for index, part in enumerate((main[:1], low, low_in_ref[0, video : video + 1, :])):
+            low_edges[index].append(part)
+        for index, part in enumerate((high_in_ref[2, video : video + 1, :], high, main[rows - 1 :])):
+            high_edges[index].append(part)
         main = main.astype(jnp.bfloat16)
         main_ref[span, :] = main
         for quarter in range(quarters):
             share_ref[quarter, span, :] = main[:, quarter * width : (quarter + 1) * width]
-        lows.append(low)
-        highs.append(high)
-    pad = share_ref.shape[1] - edges - 2 * videos
-    edge = jnp.concatenate(lows + highs + [jnp.zeros((pad, part_ref.shape[1]), jnp.float32)], axis=0)
-    edge = edge.astype(jnp.bfloat16)
-    for quarter in range(quarters):
-        share_ref[quarter, edges:, :] = edge[:, quarter * width : (quarter + 1) * width]
+    spare = [jnp.zeros((main_ref.shape[0] - edges - 2 * videos, part_ref.shape[1]), jnp.float32)]
+    for index, ref in enumerate((after_ref, main_ref, before_ref)):
+        edge = jnp.concatenate(low_edges[index] + high_edges[index] + spare, axis=0)
+        edge = edge.astype(jnp.bfloat16)
+        ref[edges:, :] = edge
+        if ref is main_ref:
+            for quarter in range(quarters):
+                share_ref[quarter, edges:, :] = edge[:, quarter * width : (quarter + 1) * width]
 
 
 def finish(partial, from_low, from_high, main_rows, quarters):
     channels = partial.shape[1]
-    full = jax.ShapeDtypeStruct((main_rows, channels), jnp.bfloat16)
+    full = jax.ShapeDtypeStruct((main_rows + 16, channels), jnp.bfloat16)
     share = jax.ShapeDtypeStruct((quarters, main_rows + 16, channels // quarters), jnp.bfloat16)
     return pl.pallas_call(
         finish_kernel,
@@ -166,65 +171,77 @@
     )(partial, from_low, from_high)
 
 
-def lags_kernel(videos, halo, grad_ref, out_ref):
-    sources, block, width = grad_ref.shape
-    rows = (block if not halo else block - 16) // videos
-    main = rows * videos
+def terms_kernel(videos, source_count, order_ref, grad_ref, *refs):
+    input_refs, (keep_ref, give_ref, lag_ref) = refs[:-3], refs[-3:]
+    width = grad_ref.shape[2]
+    main = grad_ref.shape[1] - 16
+    rows = main // videos
+    groups, each, outs = keep_ref.shape
+    core = order_ref[source_count]
     row = lax.broadcasted_iota(jnp.int32, (rows, width), 0)
-    for source in range(sources):
-        edge_low, edge_high = [], []
-        if halo:
-            edges = grad_ref[source, main:, :].astype(jnp.float32)
+    for source in range(source_count):
+        at = order_ref[source]
+        edges = grad_ref[at, main:, :].astype(jnp.float32)
         for video in range(videos):
             span = slice(video * rows, (video + 1) * rows)
-            grad = grad_ref[source, span, :].astype(jnp.float32)
-            if halo:
-                low, high = edges[video : video + 1], edges[videos + video : videos + video + 1]
-            else:
-                low, high = 0.0, 0.0
-                edge_low.append(grad[:1])
-                edge_high.append(grad[rows - 1 :])
+            grad = grad_ref[at, span, :].astype(jnp.float32)
+            low, high = edges[video : video + 1], edges[videos + video : videos + video + 1]
             after = jnp.where(row == rows - 1, high, pltpu.roll(grad, rows - 1, 0))
             before = jnp.where(row == 0, low, pltpu.roll(grad, 1, 0))
             for index, part in enumerate((after, grad, before)):
-                out_ref[source, span, index * width : (index + 1) * width] = part.astype(jnp.bfloat16)
-        if not halo:
-            zero = jnp.zeros((videos, width), jnp.float32)
-            rest = jnp.zeros((out_ref.shape[1] - main - 2 * videos, width), jnp.float32)
-            parts = (edge_low + [zero, rest], [zero, zero, rest], [zero] + edge_high + [rest])
-            for index, part in enumerate(parts):
-                out_ref[source, main:, index * width : (index + 1) * width] = jnp.concatenate(
-                    part, axis=0
-                ).astype(jnp.bfloat16)
-
-
-def lags(gradient, videos, halo, lag_count):
-    sources, block, width = gradient.shape
-    rows = block - 16 if halo else block + 16
+                lag_ref[
+                    source * main + video * rows : source * main + (video + 1) * rows,
+                    index * width : (index + 1) * width,
+                ] = part.astype(jnp.bfloat16)
+    channels = groups * 2 * each
+    step = min(256, channels)
+    for start in range(0, channels, step):
+        total = jnp.zeros((step, outs), jnp.float32)
+        for source in range(source_count):
+            if len(input_refs) == 1:
+                block = input_refs[0][source, :, start : start + step]
+            else:
+                block = input_refs[source][:, start : start + step]
+            total = total + lax.dot_general(
+                block,
+                lag_ref[source * main : (source + 1) * main, :],
+                (((0,), (0,)), ((), ())),
+                preferred_element_type=jnp.float32,
+            )
+        total = total.reshape(step // (2 * each), 2, each, outs)
+        first, second = total[:, 0], total[:, 1]
+        span = slice(start // (2 * each), (start + step) // (2 * each))
+        keep_ref[span] = jnp.where(core == 0, first, second)
+        give_ref[span] = jnp.where(core == 0, second, first).astype(jnp.bfloat16)
+
+
+def filter_terms(inputs, gradient, order, videos, lag_count, each):
+    source_count, block, width = gradient.shape
+    channels = inputs[0].shape[-1]
+    shape = (channels // (2 * each), each, lag_count * width)
+    rows = source_count * (block - 16)
+    vmem = pl.BlockSpec(memory_space=pltpu.VMEM)
     return pl.pallas_call(
-        lambda *refs: lags_kernel(videos, halo, *refs),
-        out_shape=jax.ShapeDtypeStruct((sources, rows, lag_count * width), jnp.bfloat16),
+        lambda *refs: terms_kernel(videos, source_count, *refs),
+        out_shape=(
+            jax.ShapeDtypeStruct(shape, jnp.float32),
+            jax.ShapeDtypeStruct(shape, jnp.bfloat16),
+        ),
+        in_specs=[pl.BlockSpec(memory_space=pltpu.SMEM)] + [vmem] * (1 + len(inputs)),
+        out_specs=(vmem, vmem),
+        scratch_shapes=[pltpu.VMEM((rows, lag_count * width), jnp.bfloat16)],
         compiler_params=pltpu.CompilerParams(vmem_limit_bytes=40 * 2**20),
-        cost_estimate=pl.CostEstimate(flops=0, bytes_accessed=4 * 2**20, transcendentals=0),
-    )(gradient)
-
-
-def filter_terms(inputs, lagged):
-    inputs = inputs.reshape(-1, inputs.shape[-1])
-    lagged = lagged.reshape(-1, lagged.shape[-1])
-    return lax.dot_general(
-        inputs, lagged, (((0,), (0,)), ((), ())), preferred_element_type=jnp.float32
-    )
-
-
-def reduce_core_x(terms):
-    x_total, z_total, cores = (lax.axis_size(name) for name in TM)
-    channels, outs = terms.shape
-    each = channels // (x_total * z_total * cores)
-    parts = terms.reshape(x_total * z_total, cores, each, outs)
-    core = lax.axis_index("core")
-    keep = lax.dynamic_index_in_dim(parts, core, 1, keepdims=False)
-    give = lax.dynamic_index_in_dim(parts, 1 - core, 1, keepdims=False).astype(jnp.bfloat16)
+        cost_estimate=pl.CostEstimate(
+            flops=2 * rows * channels * lag_count * width,
+            bytes_accessed=10 * 2**20,
+            transcendentals=0,
+        ),
+    )(order, gradient, *inputs)
+
+
+def reduce_core_x(keep, give):
+    x_total, z_total = lax.axis_size("x"), lax.axis_size("z")
+    groups, each, outs = keep.shape
     got = ring_shift(give, "core", 1)
     share = (keep + got.astype(jnp.float32)).astype(jnp.bfloat16)
     share = exchange(share.reshape(x_total, z_total * each, outs), "x")
@@ -235,8 +252,10 @@
     video_count, snip_count, channels = features.shape
     peers = lax.axis_size(TM)
     quarters = lax.axis_size("video")
+    place, core = lax.axis_index("video"), lax.axis_index("core")
     lag_count = filter_second.shape[0]
     main_rows = video_count * snip_count
+    each = channels // peers
     sent = send_slots(bin_grad, tap_weight, tap_index, snip_count, peers)
     got = exchange(sent, TM)
 
@@ -244,39 +263,55 @@
     activation = jax.nn.silu(pre_values).astype(jnp.bfloat16)
     act_all = lax.all_gather(activation, "video", axis=0, tiled=False)
     after_send = sent[0, 0, 0] * 0
-    edge_low = neighbours(features[:, -1] + after_send, True)
-    edge_high = neighbours(features[:, 0] + after_send, False)
-    spare = jnp.zeros((16 - 2 * video_count, channels), features.dtype)
-    feature_rows = jnp.concatenate(
-        [features.reshape(main_rows, channels), edge_low, edge_high, spare], axis=0
-    )
-    feature_all = lax.all_gather(feature_rows, "video", axis=0, tiled=False)
+    feature_rows = features.reshape(main_rows, channels) + after_send
+    feature_all = [feature_rows] + [
+        ring_shift(feature_rows, "video", shift) for shift in range(1, quarters)
+    ]
+    pre_low = neighbours(preact[:, -1] + after_send, True)
+    pre_high = neighbours(preact[:, 0] + after_send, False)
+    at = lax.axis_index(TM)
+    edge_slope = jnp.concatenate(
+        [
+            jnp.where(at > 0, silu_slope(pre_low.astype(jnp.float32)), 0.0),
+            jnp.where(at < peers - 1, silu_slope(pre_high.astype(jnp.float32)), 0.0),
+            jnp.zeros((16 - 2 * video_count, channels), jnp.float32),
+        ],
+        axis=0,
+    )
 
     partial = collect(got, channels, main_rows + 2 * video_count)
     ends = partial[:main_rows].reshape(video_count, snip_count, channels)
     low = partial[main_rows : main_rows + video_count]
     high = partial[main_rows + video_count :]
-    from_low = neighbours(jnp.stack([ends[:, -1], high]), True)
-    from_high = neighbours(jnp.stack([low, ends[:, 0]]), False)
+    from_low = neighbours(jnp.stack([ends[:, -2], ends[:, -1], high]), True)
+    from_high = neighbours(jnp.stack([low, ends[:, 0], ends[:, 1]]), False)
     *windows, snippet_share = finish(partial, from_low, from_high, main_rows, quarters)
     snippet_share = exchange(snippet_share, "video")
 
-    act_grad = jnp.zeros((main_rows, channels), jnp.float32)
+    act_grad = jnp.zeros((main_rows + 16, channels), jnp.float32)
     for window, taps in zip(windows, filter_second):
         act_grad = act_grad + lax.dot_general(
             window, taps, (((1,), (1,)), ((), ())), preferred_element_type=jnp.float32
         )
-    pre_grad = (act_grad * silu_slope(pre_values)).astype(jnp.bfloat16)
+    slope = jnp.concatenate([silu_slope(pre_values), edge_slope], axis=0)
+    pre_grad = (act_grad * slope).astype(jnp.bfloat16)
+    pre_grad = pre_grad + snippet_share[0, 0, 0] * 0
     width = channels // quarters
     pre_share = jnp.stack([pre_grad[:, q * width : (q + 1) * width] for q in range(quarters)])
     pre_share = exchange(pre_share, "video")
 
-    second = reduce_core_x(filter_terms(act_all, lags(snippet_share, video_count, True, lag_count)))
-    first = reduce_core_x(filter_terms(feature_all, lags(pre_share, video_count, False, lag_count)))
+    in_order = [jnp.int32(source) for source in range(quarters)]
+    around = [(place + quarters - source) % quarters for source in range(quarters)]
+    second = filter_terms(
+        [act_all], snippet_share, jnp.stack(in_order + [core]), video_count, lag_count, each
+    )
+    first = filter_terms(
+        feature_all, pre_share, jnp.stack(around + [core]), video_count, lag_count, each
+    )
+    second, first = reduce_core_x(*second), reduce_core_x(*first)
     both = jnp.stack([first, second], axis=1).astype(jnp.bfloat16)
     mine = jnp.sum(exchange(both, "z").astype(jnp.float32), axis=0)
 
-    place = lax.axis_index("video")
     held = [mine] + [ring_shift(mine, "video", shift) for shift in range(1, quarters)]
     blocks = []
     for quarter in range(quarters):

time: 259 us -> 236 us (0.911)
  blocking collectives: 50.1 us -> 18.9 us
  starting transfers between devices: 42.9 us -> 56.9 us
  local copies, waits for them, and re-layouts: 24.9 us -> 12.7 us
  Pallas kernels: 2.18 us -> 12.7 us
  waiting for transfers between devices: 89.5 us -> 83.9 us
    ppermute x4, waiting for transfers between devices: 47.6 us -> 2.33 us  [neighbours(): return lax.ppermute(value, TM, pairs)]
    all_to_all x4 -> x5, waiting for transfers between devices: 36.1 us -> 78.7 us  [exchange(): return lax.all_to_all(value, axis, split_axis=0, concat_axis=0, tiled=True)]
    all_to_all x2 -> x1, blocking collectives: 50.1 us -> 18.9 us  [exchange(): return lax.all_to_all(value, axis, split_axis=0, concat_axis=0, tiled=True)]
    dot_general x2 -> x0, matrix products: 10.8 us -> none  [filter_terms(): lax.dot_general(inputs, lagged, (((0,), (0,)), ((), ())), preferred_eleme...]
    pallas_call x2, Pallas kernels: 0.91 us -> 11.5 us  [filter_terms(): pl.pallas_call(lambda *refs: terms_kernel(videos, source_count, *refs), o...]
    dot_general x3, matrix products: 4.39 us -> 14 us  [on_device(): lax.dot_general(window, taps, (((1,), (1,)), ((), ())), preferred_element...]
    ppermute x5 -> x8, starting transfers between devices: 4.18 us -> 12.3 us  [ring_shift(): lax.ppermute(value, axis, [(i, (i + shift) % count) for i in range(count)])]
    reshape x1 -> x0, local copies, waits for them, and re-layouts: 6.69 us -> none  [filter_terms(): inputs = inputs.reshape(-1, inputs.shape[-1])]
  transfers between devices with their start and end apart: 15 -> 18, of which waited for: 9 -> 9; matrix products, arithmetic and copies ran while one was open for 18% -> 13% of each run, Pallas kernels for 1% -> 5%
where the time goes in v1:
time: 236 us; the launch traced here: 234 us
  waiting for transfers between devices  83.9 us (36%)
  starting transfers between devices  56.9 us (24%)
  matrix products  20.1 us (9%)
  blocking collectives  18.9 us (8%)
  between operations  15.8 us (7%)
  other arithmetic  13.2 us (6%)
  local copies, waits for them, and re-layouts  12.7 us (5%)
  Pallas kernels  12.7 us (5%)
    all_to_all x5, waiting for transfers between devices, exchange(): return lax.all_to_all(value, axis, split_axis=0, concat_axis=0, tiled=True)  78.7 us
    all_to_all x5, starting transfers between devices, exchange(): return lax.all_to_all(value, axis, split_axis=0, concat_axis=0, tiled=True)  31.6 us
    all_to_all x1, blocking collectives, exchange(): return lax.all_to_all(value, axis, split_axis=0, concat_axis=0, tiled=True)  18.9 us
    dot_general x3, matrix products, on_device(): lax.dot_general(window, taps, (((1,), (1,)), ((), ())), preferred_element...  14 us
    ppermute x4, starting transfers between devices, neighbours(): return lax.ppermute(value, TM, pairs)  13 us
    ppermute x8, starting transfers between devices, ring_shift(): lax.ppermute(value, axis, [(i, (i + shift) % count) for i in range(count)])  12.3 us
    pallas_call x2, Pallas kernels, filter_terms(): pl.pallas_call(lambda *refs: terms_kernel(videos, source_count, *refs), o...  11.5 us
    unnamed x25, local copies, waits for them, and re-layouts  9.2 us
  transfers between devices with their start and end apart: 18, of which 9 were waited for; matrix products, arithmetic and copies ran while one was open for 13% of the time, Pallas kernels for 5%

profile of v1, /device:TPU:2, one launch (start us, length us, event | category | flops | bytes accessed | tf_op | source)
XLA Modules:
  0.0 234.3 jit_solution(1369567152764517038)
XLA Ops:
  9.7 3.4 %convolution_convert_fusion = bf16[1024,1152]{1,0:T(8,128)(2,1)} fusion(bf16[256,128]{1,0:T(8,128)(2,1)S(1)} %select_convert_fusion, bf16[256,1024]{1,0:T(8,128)(2,1)} %bitcast.116, s32[256]{0:T(256)S(1)} %get-tuple-element.60), kind=kOutput, calls=%fused_computation.4 | convolution fusion | flops 606601216 | bytes 2950144 | tf_op jit(solution)/shard_map/dot_general | solution.py:103
  13.1 12.2 %all-to-all-start = ((bf16[64,16,1152]{2,1,0:T(8,128)(2,1)}), bf16[64,16,1152]{2,1,0:T(8,128)(2,1)S(1)}, u32[]{:S(2)}, u32[]{:S(2)}) async-start(bf16[64,16,1152]{2,1,0:T(8,128)(2,1)} %bitcast.12), calls=%async_computation | async-start | bytes 4718592 | tf_op jit(solution)/shard_map/all_to_all | solution.py:34
  25.6 1.5 fusion.26
  29.0 2.3 broadcast_add_fusion
  31.3 1.6 collective-permute-start.4
  32.9 2.9 %collective-permute-start.5 = (bf16[512,1024]{1,0:T(8,128)(2,1)}, bf16[512,1024]{1,0:T(8,128)(2,1)}, u32[]{:S(2)}, u32[]{:S(2)}) collective-permute-start(bf16[512,1024]{1,0:T(8,128)(2,1)} %bitcast.38.refs_2_), channel_id=1, source_target_pairs={{0,128},{64,192},{128,0},{192,64},{1,129},{65,193},{129,1},{193,65... | collective-permute-start | bytes 3145736 | tf_op jit(solution)/shard_map/ppermute | solution.py:30
  35.8 1.9 collective-permute-start.2
  37.7 5.8 %collective-permute-start.3 = (bf16[4,1024]{1,0:T(4,128)(2,1)S(1)}, bf16[4,1024]{1,0:T(4,128)(2,1)S(1)}, u32[]{:S(2)}, u32[]{:S(2)}) collective-permute-start(bf16[4,1024]{1,0:T(4,128)(2,1)S(1)} %fusion.58), channel_id=1, source_target_pairs={{1,0},{2,1},{3,2},{4,3},{5,4},{6,5},{7,6},{8,7},{9,8},{10,9},{11,1... | collective-permute-start | bytes 24584 | tf_op jit(solution)/shard_map/ppermute | solution.py:25
  43.6 2.1 fusion.14
  45.7 34.8 %all-to-all-done = bf16[64,16,1152]{2,1,0:T(8,128)(2,1)S(1)} async-done(((bf16[64,16,1152]{2,1,0:T(8,128)(2,1)}), bf16[64,16,1152]{2,1,0:T(8,128)(2,1)S(1)}, u32[]{:S(2)}, u32[]{:S(2)}) %all-to-all-start) | async-done | bytes 2359328 | tf_op jit(solution)/shard_map/all_to_all | solution.py:34
  83.8 3.3 %collective-permute-start.1 = (f32[3,4,1024]{2,1,0:T(4,128)S(1)}, f32[3,4,1024]{2,1,0:T(4,128)S(1)}, u32[]{:S(2)}, u32[]{:S(2)}) collective-permute-start(f32[3,4,1024]{2,1,0:T(4,128)S(1)} %pad_maximum_fusion.3), channel_id=1, source_target_pairs={{1,0},{2,1},{3,2},{4,3},{5,4},{6,5},{7,6},{8,7},{9,8},{10,9},{11,1... | collective-permute-start | bytes 147464 | tf_op jit(solution)/shard_map/ppermute | solution.py:25
  87.1 2.1 collective-permute-start
  89.2 3.1 %collective-permute-start.6 = (bf16[512,1024]{1,0:T(8,128)(2,1)}, bf16[512,1024]{1,0:T(8,128)(2,1)}, u32[]{:S(2)}, u32[]{:S(2)}) collective-permute-start(bf16[512,1024]{1,0:T(8,128)(2,1)} %bitcast.38.refs_2_), channel_id=1, source_target_pairs={{0,192},{64,0},{128,64},{192,128},{1,193},{65,1},{129,65},{193,129... | collective-permute-start | bytes 3145736 | tf_op jit(solution)/shard_map/ppermute | solution.py:30
  92.3 2.3 collective-permute-done.low_in_ref
  96.9 4.4 %all-to-all-start.1 = ((bf16[4,528,256]{2,1,0:T(8,128)(2,1)}), bf16[4,528,256]{2,1,0:T(8,128)(2,1)S(1)}, u32[]{:S(2)}, u32[]{:S(2)}) async-start(bf16[4,528,256]{2,1,0:T(8,128)(2,1)} %get-tuple-element.13), calls=%async_computation.1 | async-start | bytes 2162688 | tf_op jit(solution)/shard_map/all_to_all | solution.py:34
  101.3 4.6 %fusion.17 = f32[528,1024]{1,0:T(8,128)} fusion(bf16[528,1024]{1,0:T(8,128)(2,1)} %copy-done.5, bf16[3,1024,1024]{2,1,0:T(8,128)(2,1)} %param.11), kind=kOutput, calls=%fused_computation.25 | convolution fusion | flops 1107296256 | bytes 5341184 | tf_op jit(solution)/shard_map/dot_general | solution.py:293
  105.9 4.3 %fusion.19 = f32[528,1024]{1,0:T(8,128)} fusion(bf16[528,1024]{1,0:T(8,128)(2,1)S(1)} %get-tuple-element.10, bf16[3,1024,1024]{2,1,0:T(8,128)(2,1)} %param.11), kind=kOutput, calls=%fused_computation.27 | convolution fusion | flops 1107296256 | bytes 5341184 | tf_op jit(solution)/shard_map/dot_general | solution.py:293
  110.2 16.7 %all-to-all-done.1.refs_1_ = bf16[4,528,256]{2,1,0:T(8,128)(2,1)S(1)} async-done(((bf16[4,528,256]{2,1,0:T(8,128)(2,1)}), bf16[4,528,256]{2,1,0:T(8,128)(2,1)S(1)}, u32[]{:S(2)}, u32[]{:S(2)}) %all-to-all-start.1) | async-done | bytes 1081376 | tf_op jit(solution)/shard_map/all_to_all | solution.py:34
  128.1 5.0 %fusion.34 = bf16[528,1024]{1,0:T(8,128)(2,1)S(1)} fusion(f32[4,1024]{1,0:T(4,128)S(1)} %fusion.57, f32[4,1024]{1,0:T(4,128)S(1)} %fusion.51, f32[512,1024]{1,0:T(8,128)} %fusion.14, bf16[528,1024]{1,0:T(8,128)(2,1)S(1)} %get-tuple-element.12, bf16[3,1024,1024]{2,1,0:T(8,128)(2,1)} %param.11, f32[528,1024]{1,0:T(8,128)} %fusion.19, ...), kind=kOutput, calls=%fused_computation.40 | convolution fusion | flops 1111621632 | bytes 10717760 | tf_op jit(solution)/shard_map/dot_general | solution.py:293
  134.4 5.2 %all-to-all-start.2 = ((bf16[4,528,256]{2,1,0:T(8,128)(2,1)}), bf16[4,528,256]{2,1,0:T(8,128)(2,1)S(1)}, u32[]{:S(2)}, u32[]{:S(2)}) async-start(bf16[4,528,256]{2,1,0:T(8,128)(2,1)} %pad_maximum_fusion), calls=%async_computation.2 | async-start | bytes 2162688 | tf_op jit(solution)/shard_map/all_to_all | solution.py:34
  141.0 2.2 copy-done.4
  143.2 4.9 %shard_map.79 = (f32[32,16,768]{2,1,0:T(8,128)S(1)}, bf16[32,16,768]{2,1,0:T(8,128)(2,1)}) custom-call(s32[5]{0:T(128)S(1)} %stack.68.refs_0_, bf16[4,528,256]{2,1,0:T(8,128)(2,1)S(1)} %copy-done.3, bf16[4,512,1024]{2,1,0:T(8,128)(2,1)S(1)} %copy-done.4), custom_call_target="tpu_custom_call" | custom-call | flops 3221225472 | bytes 10485760 | tf_op jit(solution)/shard_map/pallas_call | solution.py:224
  148.2 7.4 %all-to-all-done.2.refs_1_ = bf16[4,528,256]{2,1,0:T(8,128)(2,1)S(1)} async-done(((bf16[4,528,256]{2,1,0:T(8,128)(2,1)}), bf16[4,528,256]{2,1,0:T(8,128)(2,1)S(1)}, u32[]{:S(2)}, u32[]{:S(2)}) %all-to-all-start.2) | async-done | bytes 1081376 | tf_op jit(solution)/shard_map/all_to_all | solution.py:34
  157.8 6.6 %shard_map.78 = (f32[32,16,768]{2,1,0:T(8,128)S(1)}, bf16[32,16,768]{2,1,0:T(8,128)(2,1)}) custom-call(s32[5]{0:T(128)S(1)} %stack.58.refs_0_, bf16[4,528,256]{2,1,0:T(8,128)(2,1)S(1)} %copy-done.1, bf16[512,1024]{1,0:T(8,128)(2,1)} %bitcast.38.refs_2_, bf16[512,1024]{1,0:T(8,128)(2,1)} %collective-permute-done.4.refs_3_, ...), custom_call_target="tpu_custom_call" | custom-call | flops 3221225472 | bytes 10485760 | tf_op jit(solution)/shard_map/pallas_call | solution.py:224
  164.4 2.2 add_convert_fusion
  166.6 4.9 %all-to-all-start.4 = ((bf16[4,128,768]{2,1,0:T(8,128)(2,1)}), bf16[4,128,768]{2,1,0:T(8,128)(2,1)S(1)}, u32[]{:S(2)}, u32[]{:S(2)}) async-start(bf16[4,128,768]{2,1,0:T(8,128)(2,1)} %bitcast.108), calls=%async_computation.4 | async-start | bytes 1572864 | tf_op jit(solution)/shard_map/all_to_all | solution.py:34
  171.5 2.2 add_convert_fusion.1
  173.8 9.3 %all-to-all-done.4 = bf16[4,128,768]{2,1,0:T(8,128)(2,1)S(1)} async-done(((bf16[4,128,768]{2,1,0:T(8,128)(2,1)}), bf16[4,128,768]{2,1,0:T(8,128)(2,1)S(1)}, u32[]{:S(2)}, u32[]{:S(2)}) %all-to-all-start.4) | async-done | bytes 786464 | tf_op jit(solution)/shard_map/all_to_all | solution.py:34
  183.0 4.9 %all-to-all-start.3 = ((bf16[4,128,768]{2,1,0:T(8,128)(2,1)}), bf16[4,128,768]{2,1,0:T(8,128)(2,1)S(1)}, u32[]{:S(2)}, u32[]{:S(2)}) async-start(bf16[4,128,768]{2,1,0:T(8,128)(2,1)} %bitcast.109), calls=%async_computation.3 | async-start | bytes 1572864 | tf_op jit(solution)/shard_map/all_to_all | solution.py:34
  188.1 10.6 %all-to-all-done.3 = bf16[4,128,768]{2,1,0:T(8,128)(2,1)S(1)} async-done(((bf16[4,128,768]{2,1,0:T(8,128)(2,1)}), bf16[4,128,768]{2,1,0:T(8,128)(2,1)S(1)}, u32[]{:S(2)}, u32[]{:S(2)}) %all-to-all-start.3) | async-done | bytes 786464 | tf_op jit(solution)/shard_map/all_to_all | solution.py:34
  198.8 18.9 %all_to_all.30 = bf16[8,2,16,768]{3,2,1,0:T(8,128)(2,1)S(1)} all-to-all(bf16[8,2,16,768]{3,2,1,0:T(8,128)(2,1)S(1)} %pad_maximum_fusion.1), channel_id=1, replica_groups=mesh['video'=4,'x'=4,'z'=8,'core'=2] {'z'}, dimensions={0} | all-to-all | bytes 786432 | tf_op jit(solution)/shard_map/all_to_all | solution.py:34
  220.7 1.8 collective-permute-start.9
  (98 shorter events, 23.3 us)
Async XLA Ops:
  13.1 12.2 %copy-start.6 = (bf16[4,128,1024]{2,1,0:T(8,128)(2,1)S(1)}, bf16[4,128,1024]{2,1,0:T(8,128)(2,1)}, u32[]{:S(2)}) copy-start(bf16[4,128,1024]{2,1,0:T(8,128)(2,1)} %param.10) | copy-start | bytes 3145732
  13.1 67.4 %all-to-all-start = ((bf16[64,16,1152]{2,1,0:T(8,128)(2,1)}), bf16[64,16,1152]{2,1,0:T(8,128)(2,1)S(1)}, u32[]{:S(2)}, u32[]{:S(2)}) async-start(bf16[64,16,1152]{2,1,0:T(8,128)(2,1)} %bitcast.12), calls=%async_computation | async-start | bytes 4718592 | tf_op jit(solution)/shard_map/all_to_all | solution.py:34
  25.3 114.5 %all-gather.2.cloned.1.call-start = ((), (), s32[]{:S(2)}) async-start(), calls=%async_computation.6 | async-start | bytes 5242880 | tf_op jit(solution)/shard_map/all_gather | solution.py:264
  31.3 116.9 %collective-permute-start.4 = (bf16[512,1024]{1,0:T(8,128)(2,1)}, bf16[512,1024]{1,0:T(8,128)(2,1)}, u32[]{:S(2)}, u32[]{:S(2)}) collective-permute-start(bf16[512,1024]{1,0:T(8,128)(2,1)} %bitcast.38.refs_2_), channel_id=1, source_target_pairs={{0,64},{64,128},{128,192},{192,0},{1,65},{65,129},{129,193},{193,1... | collective-permute-start | bytes 3145736 | tf_op jit(solution)/shard_map/ppermute | solution.py:30
  32.9 115.4 %collective-permute-start.5 = (bf16[512,1024]{1,0:T(8,128)(2,1)}, bf16[512,1024]{1,0:T(8,128)(2,1)}, u32[]{:S(2)}, u32[]{:S(2)}) collective-permute-start(bf16[512,1024]{1,0:T(8,128)(2,1)} %bitcast.38.refs_2_), channel_id=1, source_target_pairs={{0,128},{64,192},{128,0},{192,64},{1,129},{65,193},{129,1},{193,65... | collective-permute-start | bytes 3145736 | tf_op jit(solution)/shard_map/ppermute | solution.py:30
  35.8 51.3 %collective-permute-start.2 = (bf16[4,1024]{1,0:T(4,128)(2,1)S(1)}, bf16[4,1024]{1,0:T(4,128)(2,1)S(1)}, u32[]{:S(2)}, u32[]{:S(2)}) collective-permute-start(bf16[4,1024]{1,0:T(4,128)(2,1)S(1)} %fusion.59), channel_id=1, source_target_pairs={{0,1},{1,2},{2,3},{3,4},{4,5},{5,6},{6,7},{7,8},{8,9},{9,10},{10,1... | collective-permute-start | bytes 24584 | tf_op jit(solution)/shard_map/ppermute | solution.py:25
  37.7 63.5 %collective-permute-start.3 = (bf16[4,1024]{1,0:T(4,128)(2,1)S(1)}, bf16[4,1024]{1,0:T(4,128)(2,1)S(1)}, u32[]{:S(2)}, u32[]{:S(2)}) collective-permute-start(bf16[4,1024]{1,0:T(4,128)(2,1)S(1)} %fusion.58), channel_id=1, source_target_pairs={{1,0},{2,1},{3,2},{4,3},{5,4},{6,5},{7,6},{8,7},{9,8},{10,9},{11,1... | collective-permute-start | bytes 24584 | tf_op jit(solution)/shard_map/ppermute | solution.py:25
  83.8 5.4 %collective-permute-start.1 = (f32[3,4,1024]{2,1,0:T(4,128)S(1)}, f32[3,4,1024]{2,1,0:T(4,128)S(1)}, u32[]{:S(2)}, u32[]{:S(2)}) collective-permute-start(f32[3,4,1024]{2,1,0:T(4,128)S(1)} %pad_maximum_fusion.3), channel_id=1, source_target_pairs={{1,0},{2,1},{3,2},{4,3},{5,4},{6,5},{7,6},{8,7},{9,8},{10,9},{11,1... | collective-permute-start | bytes 147464 | tf_op jit(solution)/shard_map/ppermute | solution.py:25
  87.1 7.5 %collective-permute-start = (f32[3,4,1024]{2,1,0:T(4,128)S(1)}, f32[3,4,1024]{2,1,0:T(4,128)S(1)}, u32[]{:S(2)}, u32[]{:S(2)}) collective-permute-start(f32[3,4,1024]{2,1,0:T(4,128)S(1)} %pad_maximum_fusion.2), channel_id=1, source_target_pairs={{0,1},{1,2},{2,3},{3,4},{4,5},{5,6},{6,7},{7,8},{8,9},{9,10},{10,1... | collective-permute-start | bytes 147464 | tf_op jit(solution)/shard_map/ppermute | solution.py:25
  89.2 59.0 %collective-permute-start.6 = (bf16[512,1024]{1,0:T(8,128)(2,1)}, bf16[512,1024]{1,0:T(8,128)(2,1)}, u32[]{:S(2)}, u32[]{:S(2)}) collective-permute-start(bf16[512,1024]{1,0:T(8,128)(2,1)} %bitcast.38.refs_2_), channel_id=1, source_target_pairs={{0,192},{64,0},{128,64},{192,128},{1,193},{65,1},{129,65},{193,129... | collective-permute-start | bytes 3145736 | tf_op jit(solution)/shard_map/ppermute | solution.py:30
  95.9 1.0 copy-start.5
  96.9 30.0 %all-to-all-start.1 = ((bf16[4,528,256]{2,1,0:T(8,128)(2,1)}), bf16[4,528,256]{2,1,0:T(8,128)(2,1)S(1)}, u32[]{:S(2)}, u32[]{:S(2)}) async-start(bf16[4,528,256]{2,1,0:T(8,128)(2,1)} %get-tuple-element.13), calls=%async_computation.1 | async-start | bytes 2162688 | tf_op jit(solution)/shard_map/all_to_all | solution.py:34
  126.9 6.2 %copy-start.2 = (bf16[4,528,256]{2,1,0:T(8,128)(2,1)}, bf16[4,528,256]{2,1,0:T(8,128)(2,1)S(1)}, u32[]{:S(2)}) copy-start(bf16[4,528,256]{2,1,0:T(8,128)(2,1)S(1)} %all-to-all-done.1.refs_1_) | copy-start | bytes 3244036
  134.4 21.2 %all-to-all-start.2 = ((bf16[4,528,256]{2,1,0:T(8,128)(2,1)}), bf16[4,528,256]{2,1,0:T(8,128)(2,1)S(1)}, u32[]{:S(2)}, u32[]{:S(2)}) async-start(bf16[4,528,256]{2,1,0:T(8,128)(2,1)} %pad_maximum_fusion), calls=%async_computation.2 | async-start | bytes 2162688 | tf_op jit(solution)/shard_map/all_to_all | solution.py:34
  139.7 1.2 copy-start.3
  141.0 2.2 copy-start.4
  148.1 16.3 %collective-permute-start.8 = (bf16[32,16,768]{2,1,0:T(8,128)(2,1)}, bf16[32,16,768]{2,1,0:T(8,128)(2,1)}, u32[]{:S(2)}, u32[]{:S(2)}) collective-permute-start(bf16[32,16,768]{2,1,0:T(8,128)(2,1)} %get-tuple-element.17), channel_id=1, source_target_pairs={{0,1},{1,0},{2,3},{3,2},{4,5},{5,4},{6,7},{7,6},{8,9},{9,8},{10,11... | collective-permute-start | bytes 2359304 | tf_op jit(solution)/shard_map/ppermute | solution.py:30
  155.6 1.0 copy-start
  156.6 1.2 copy-start.1
  164.4 7.2 %collective-permute-start.7 = (bf16[32,16,768]{2,1,0:T(8,128)(2,1)}, bf16[32,16,768]{2,1,0:T(8,128)(2,1)}, u32[]{:S(2)}, u32[]{:S(2)}) collective-permute-start(bf16[32,16,768]{2,1,0:T(8,128)(2,1)} %get-tuple-element.15), channel_id=1, source_target_pairs={{0,1},{1,0},{2,3},{3,2},{4,5},{5,4},{6,7},{7,6},{8,9},{9,8},{10,11... | collective-permute-start | bytes 2359304 | tf_op jit(solution)/shard_map/ppermute | solution.py:30
  166.6 16.4 %all-to-all-start.4 = ((bf16[4,128,768]{2,1,0:T(8,128)(2,1)}), bf16[4,128,768]{2,1,0:T(8,128)(2,1)S(1)}, u32[]{:S(2)}, u32[]{:S(2)}) async-start(bf16[4,128,768]{2,1,0:T(8,128)(2,1)} %bitcast.108), calls=%async_computation.4 | async-start | bytes 1572864 | tf_op jit(solution)/shard_map/all_to_all | solution.py:34
  183.0 15.6 %all-to-all-start.3 = ((bf16[4,128,768]{2,1,0:T(8,128)(2,1)}), bf16[4,128,768]{2,1,0:T(8,128)(2,1)S(1)}, u32[]{:S(2)}, u32[]{:S(2)}) async-start(bf16[4,128,768]{2,1,0:T(8,128)(2,1)} %bitcast.109), calls=%async_computation.3 | async-start | bytes 1572864 | tf_op jit(solution)/shard_map/all_to_all | solution.py:34
  217.8 6.2 %collective-permute-start.10 = (f32[2,16,768]{2,1,0:T(8,128)S(1)}, f32[2,16,768]{2,1,0:T(8,128)S(1)}, u32[]{:S(2)}, u32[]{:S(2)}) collective-permute-start(f32[2,16,768]{2,1,0:T(8,128)S(1)} %convert_reduce_fusion), channel_id=1, source_target_pairs={{0,128},{64,192},{128,0},{192,64},{1,129},{65,193},{129,1},{193,65... | collective-permute-start | bytes 294920 | tf_op jit(solution)/shard_map/ppermute | solution.py:30
  219.2 5.8 %collective-permute-start.11 = (f32[2,16,768]{2,1,0:T(8,128)S(1)}, f32[2,16,768]{2,1,0:T(8,128)S(1)}, u32[]{:S(2)}, u32[]{:S(2)}) collective-permute-start(f32[2,16,768]{2,1,0:T(8,128)S(1)} %convert_reduce_fusion), channel_id=1, source_target_pairs={{0,64},{64,128},{128,192},{192,0},{1,65},{65,129},{129,193},{193,1... | collective-permute-start | bytes 294920 | tf_op jit(solution)/shard_map/ppermute | solution.py:30
  220.7 4.6 %collective-permute-start.9 = (f32[2,16,768]{2,1,0:T(8,128)S(1)}, f32[2,16,768]{2,1,0:T(8,128)S(1)}, u32[]{:S(2)}, u32[]{:S(2)}) collective-permute-start(f32[2,16,768]{2,1,0:T(8,128)S(1)} %convert_reduce_fusion), channel_id=1, source_target_pairs={{0,192},{64,0},{128,64},{192,128},{1,193},{65,1},{129,65},{193,129... | collective-permute-start | bytes 294920 | tf_op jit(solution)/shard_map/ppermute | solution.py:30
Sparse Core Ops, SparseCore 0:
  27.9 90.0 all-gather.1

commit v2 on v1

--- a/solution.py
+++ b/solution.py
@@ -28,6 +28,16 @@
 def ring_shift(value, axis, shift):
     count = lax.axis_size(axis)
     return lax.ppermute(value, axis, [(i, (i + shift) % count) for i in range(count)])
+
+
+def around_video(rows):
+    count = lax.axis_size("video")
+    if count != 4:
+        return [[rows]] + [[ring_shift(rows, "video", shift)] for shift in range(1, count)]
+    half = rows.shape[0] // 2
+    below, above = ring_shift(rows, "video", 1), ring_shift(rows, "video", 3)
+    far = [ring_shift(below[:half], "video", 1), ring_shift(above[half:], "video", 3)]
+    return [[rows], [below], far, [above]]
 
 
 def exchange(value, axis):
@@ -166,12 +176,46 @@
     return pl.pallas_call(
         finish_kernel,
         out_shape=(full, full, full, share),
-        compiler_params=pltpu.CompilerParams(vmem_limit_bytes=40 * 2**20),
+        compiler_params=pltpu.CompilerParams(vmem_limit_bytes=14 * 2**20),
         cost_estimate=pl.CostEstimate(flops=0, bytes_accessed=8 * 2**20, transcendentals=0),
     )(partial, from_low, from_high)
 
 
-def terms_kernel(videos, source_count, order_ref, grad_ref, *refs):
+def pre_grad_kernel(after_ref, main_ref, before_ref, taps_ref, pre_ref, edge_ref, out_ref):
+    total = jnp.zeros(out_ref.shape[1:], jnp.float32)
+    for index, ref in enumerate((after_ref, main_ref, before_ref)):
+        total = total + lax.dot_general(
+            ref[...], taps_ref[index], (((1,), (1,)), ((), ())), preferred_element_type=jnp.float32
+        )
+    slope = jnp.concatenate([silu_slope(pre_ref[...].astype(jnp.float32)), edge_ref[...]], axis=0)
+    out_ref[0] = (total * slope).astype(jnp.bfloat16)
+
+
+def pre_grad_share(windows, filter_second, pre_rows, edge_slope, quarters):
+    lag_count, channels, _ = filter_second.shape
+    rows, width = windows[0].shape[0], channels // quarters
+    whole = pl.BlockSpec((rows, channels), lambda q: (0, 0))
+    return pl.pallas_call(
+        pre_grad_kernel,
+        grid=(quarters,),
+        out_shape=jax.ShapeDtypeStruct((quarters, rows, width), jnp.bfloat16),
+        in_specs=[whole] * 3
+        + [
+            pl.BlockSpec((lag_count, width, channels), lambda q: (0, q, 0)),
+            pl.BlockSpec((pre_rows.shape[0], width), lambda q: (0, q)),
+            pl.BlockSpec((16, width), lambda q: (0, q)),
+        ],
+        out_specs=pl.BlockSpec((1, rows, width), lambda q: (q, 0, 0)),
+        compiler_params=pltpu.CompilerParams(vmem_limit_bytes=20 * 2**20),
+        cost_estimate=pl.CostEstimate(
+            flops=2 * rows * channels * channels * lag_count,
+            bytes_accessed=11 * 2**20,
+            transcendentals=rows * channels,
+        ),
+    )(*windows, filter_second, pre_rows, edge_slope)
+
+
+def terms_kernel(videos, source_count, pieces, order_ref, grad_ref, *refs):
     input_refs, (keep_ref, give_ref, lag_ref) = refs[:-3], refs[-3:]
     width = grad_ref.shape[2]
     main = grad_ref.shape[1] - 16
@@ -197,14 +241,10 @@
     step = min(256, channels)
     for start in range(0, channels, step):
         total = jnp.zeros((step, outs), jnp.float32)
-        for source in range(source_count):
-            if len(input_refs) == 1:
-                block = input_refs[0][source, :, start : start + step]
-            else:
-                block = input_refs[source][:, start : start + step]
+        for ref, (offset, count) in zip(input_refs, pieces):
             total = total + lax.dot_general(
-                block,
-                lag_ref[source * main : (source + 1) * main, :],
+                ref[:, start : start + step],
+                lag_ref[offset : offset + count, :],
                 (((0,), (0,)), ((), ())),
                 preferred_element_type=jnp.float32,
             )
@@ -218,11 +258,15 @@
 def filter_terms(inputs, gradient, order, videos, lag_count, each):
     source_count, block, width = gradient.shape
     channels = inputs[0].shape[-1]
+    pieces, offset = [], 0
+    for piece in inputs:
+        pieces.append((offset, piece.shape[0]))
+        offset += piece.shape[0]
     shape = (channels // (2 * each), each, lag_count * width)
     rows = source_count * (block - 16)
     vmem = pl.BlockSpec(memory_space=pltpu.VMEM)
     return pl.pallas_call(
-        lambda *refs: terms_kernel(videos, source_count, *refs),
+        lambda *refs: terms_kernel(videos, source_count, pieces, *refs),
         out_shape=(
             jax.ShapeDtypeStruct(shape, jnp.float32),
             jax.ShapeDtypeStruct(shape, jnp.bfloat16),
@@ -230,7 +274,7 @@
         in_specs=[pl.BlockSpec(memory_space=pltpu.SMEM)] + [vmem] * (1 + len(inputs)),
         out_specs=(vmem, vmem),
         scratch_shapes=[pltpu.VMEM((rows, lag_count * width), jnp.bfloat16)],
-        compiler_params=pltpu.CompilerParams(vmem_limit_bytes=40 * 2**20),
+        compiler_params=pltpu.CompilerParams(vmem_limit_bytes=20 * 2**20),
         cost_estimate=pl.CostEstimate(
             flops=2 * rows * channels * lag_count * width,
             bytes_accessed=10 * 2**20,
@@ -239,11 +283,14 @@
     )(order, gradient, *inputs)
 
 
-def reduce_core_x(keep, give):
+def share_by_core(keep, give):
+    got = ring_shift(give, "core", 1)
+    return (keep + got.astype(jnp.float32)).astype(jnp.bfloat16)
+
+
+def sum_over_x(share):
     x_total, z_total = lax.axis_size("x"), lax.axis_size("z")
-    groups, each, outs = keep.shape
-    got = ring_shift(give, "core", 1)
-    share = (keep + got.astype(jnp.float32)).astype(jnp.bfloat16)
+    groups, each, outs = share.shape
     share = exchange(share.reshape(x_total, z_total * each, outs), "x")
     return jnp.sum(share.astype(jnp.float32), axis=0).reshape(z_total, each, outs)
 
@@ -261,54 +308,55 @@
 
     pre_values = preact.astype(jnp.float32).reshape(main_rows, channels)
     activation = jax.nn.silu(pre_values).astype(jnp.bfloat16)
-    act_all = lax.all_gather(activation, "video", axis=0, tiled=False)
-    after_send = sent[0, 0, 0] * 0
-    feature_rows = features.reshape(main_rows, channels) + after_send
-    feature_all = [feature_rows] + [
-        ring_shift(feature_rows, "video", shift) for shift in range(1, quarters)
-    ]
-    pre_low = neighbours(preact[:, -1] + after_send, True)
-    pre_high = neighbours(preact[:, 0] + after_send, False)
-    at = lax.axis_index(TM)
-    edge_slope = jnp.concatenate(
-        [
-            jnp.where(at > 0, silu_slope(pre_low.astype(jnp.float32)), 0.0),
-            jnp.where(at < peers - 1, silu_slope(pre_high.astype(jnp.float32)), 0.0),
-            jnp.zeros((16 - 2 * video_count, channels), jnp.float32),
-        ],
-        axis=0,
-    )
+    feature_all = lax.all_gather(
+        features.reshape(main_rows, channels), "video", axis=0, tiled=False
+    )
+    act_all = around_video(activation + sent[0, 0, 0] * 0)
 
     partial = collect(got, channels, main_rows + 2 * video_count)
     ends = partial[:main_rows].reshape(video_count, snip_count, channels)
     low = partial[main_rows : main_rows + video_count]
     high = partial[main_rows + video_count :]
-    from_low = neighbours(jnp.stack([ends[:, -2], ends[:, -1], high]), True)
-    from_high = neighbours(jnp.stack([low, ends[:, 0], ends[:, 1]]), False)
+    pre_ends = pre_values.reshape(ends.shape)
+    from_low = neighbours(jnp.stack([ends[:, -2], ends[:, -1], high, pre_ends[:, -1]]), True)
+    from_high = neighbours(jnp.stack([low, ends[:, 0], ends[:, 1], pre_ends[:, 0]]), False)
     *windows, snippet_share = finish(partial, from_low, from_high, main_rows, quarters)
     snippet_share = exchange(snippet_share, "video")
 
-    act_grad = jnp.zeros((main_rows + 16, channels), jnp.float32)
-    for window, taps in zip(windows, filter_second):
-        act_grad = act_grad + lax.dot_general(
-            window, taps, (((1,), (1,)), ((), ())), preferred_element_type=jnp.float32
-        )
-    slope = jnp.concatenate([silu_slope(pre_values), edge_slope], axis=0)
-    pre_grad = (act_grad * slope).astype(jnp.bfloat16)
-    pre_grad = pre_grad + snippet_share[0, 0, 0] * 0
+    at = lax.axis_index(TM)
+    edge_slope = jnp.concatenate(
+        [
+            jnp.where(at > 0, silu_slope(from_low[3]), 0.0),
+            jnp.where(at < peers - 1, silu_slope(from_high[3]), 0.0),
+            jnp.zeros((16 - 2 * video_count, channels), jnp.float32),
+        ],
+        axis=0,
+    )
+    pre_rows = preact.reshape(main_rows, channels)
+    pre_share = pre_grad_share(windows, filter_second, pre_rows, edge_slope, quarters)
+    after_pre = (pre_share[0, 0, 0] * 0).astype(jnp.int32)
+    pre_share = exchange(pre_share + snippet_share[0, 0, 0] * 0, "video")
     width = channels // quarters
-    pre_share = jnp.stack([pre_grad[:, q * width : (q + 1) * width] for q in range(quarters)])
-    pre_share = exchange(pre_share, "video")
 
     in_order = [jnp.int32(source) for source in range(quarters)]
     around = [(place + quarters - source) % quarters for source in range(quarters)]
-    second = filter_terms(
-        [act_all], snippet_share, jnp.stack(in_order + [core]), video_count, lag_count, each
-    )
-    first = filter_terms(
-        feature_all, pre_share, jnp.stack(around + [core]), video_count, lag_count, each
-    )
-    second, first = reduce_core_x(*second), reduce_core_x(*first)
+    act_pieces = [piece for source in act_all for piece in source]
+    second = share_by_core(
+        *filter_terms(
+            act_pieces,
+            snippet_share,
+            jnp.stack(around + [core]) + after_pre,
+            video_count,
+            lag_count,
+            each,
+        )
+    )
+    turn = jnp.stack(in_order + [core]) + (second[0, 0, 0] * 0).astype(jnp.int32)
+    feature_all = feature_all.reshape(-1, channels)
+    first = share_by_core(
+        *filter_terms([feature_all], pre_share, turn, video_count, lag_count, each)
+    )
+    second, first = sum_over_x(second), sum_over_x(first)
     both = jnp.stack([first, second], axis=1).astype(jnp.bfloat16)
     mine = jnp.sum(exchange(both, "z").astype(jnp.float32), axis=0)
 

time: 236 us -> 233 us (0.987)
  local copies, waits for them, and re-layouts: 12.7 us -> 30.3 us
  matrix products: 20.1 us -> 7.7 us
  starting transfers between devices: 56.9 us -> 46.5 us
  other arithmetic: 13.2 us -> 8.78 us
  Pallas kernels: 12.7 us -> 16 us
  waiting for transfers between devices: 83.9 us -> 86.6 us
    dot_general x3 -> x0, matrix products: 14 us -> none  [on_device(): lax.dot_general(window, taps, (((1,), (1,)), ((), ())), preferred_element...]
    unnamed x25 -> x45, local copies, waits for them, and re-layouts: 9.2 us -> 21.2 us
    ppermute x4 -> x2, starting transfers between devices: 13 us -> 7.67 us  [neighbours(): return lax.ppermute(value, TM, pairs)]
    slice x4 -> x8, local copies, waits for them, and re-layouts: 1.78 us -> 6.56 us  [the longest x1 1.89 us: around_video(): below[:half]]
    pallas_call x2 -> x3, Pallas kernels: 11.5 us -> 15.4 us  [the longest x2 10.6 us: filter_terms(): pl.pallas_call(lambda *refs: terms_kernel(videos, source_count, pieces, *...]
    ppermute x8 -> x9, starting transfers between devices: 12.3 us -> 9.3 us  [ring_shift(): lax.ppermute(value, axis, [(i, (i + shift) % count) for i in range(count)])]
    ppermute x8 -> x9, waiting for transfers between devices: 2.86 us -> 5.84 us  [ring_shift(): lax.ppermute(value, axis, [(i, (i + shift) % count) for i in range(count)])]
    convert_element_type x4 -> x2, other arithmetic: 6.26 us -> 3.56 us  [share_by_core(): return (keep + got.astype(jnp.float32)).astype(jnp.bfloat16)]
  transfers between devices with their start and end apart: 18 -> 17, of which waited for: 9 -> 7; matrix products, arithmetic and copies ran while one was open for 13% -> 9% of each run, Pallas kernels for 5% -> 5%
where the time goes in v2:
time: 233 us; the launch traced here: 232 us
  waiting for transfers between devices  86.6 us (37%)
  starting transfers between devices  46.5 us (20%)
  local copies, waits for them, and re-layouts  30.3 us (13%)
  blocking collectives  18.7 us (8%)
  between operations  17.2 us (7%)
  Pallas kernels  16 us (7%)
  other arithmetic  8.78 us (4%)
  matrix products  7.7 us (3%)
    all_to_all x5, waiting for transfers between devices, exchange(): return lax.all_to_all(value, axis, split_axis=0, concat_axis=0, tiled=True)  80 us
    all_to_all x5, starting transfers between devices, exchange(): return lax.all_to_all(value, axis, split_axis=0, concat_axis=0, tiled=True)  29.5 us
    unnamed x45, local copies, waits for them, and re-layouts  21.2 us
    all_to_all x1, blocking collectives, exchange(): return lax.all_to_all(value, axis, split_axis=0, concat_axis=0, tiled=True)  18.7 us
    pallas_call x2, Pallas kernels, filter_terms(): pl.pallas_call(lambda *refs: terms_kernel(videos, source_count, pieces, *...  10.6 us
    ppermute x9, starting transfers between devices, ring_shift(): lax.ppermute(value, axis, [(i, (i + shift) % count) for i in range(count)])  9.3 us
    ppermute x2, starting transfers between devices, neighbours(): return lax.ppermute(value, TM, pairs)  7.67 us
    ppermute x9, waiting for transfers between devices, ring_shift(): lax.ppermute(value, axis, [(i, (i + shift) % count) for i in range(count)])  5.84 us
  transfers between devices with their start and end apart: 17, of which 7 were waited for; matrix products, arithmetic and copies ran while one was open for 9% of the time, Pallas kernels for 5%

profile of v2, /device:TPU:2, one launch (start us, length us, event | category | flops | bytes accessed | tf_op | source)
XLA Modules:
  0.0 231.8 jit_solution(14425528639009468004)
XLA Ops:
  9.7 3.3 %convolution_convert_fusion = bf16[1024,1152]{1,0:T(8,128)(2,1)} fusion(bf16[256,128]{1,0:T(8,128)(2,1)S(1)} %select_convert_fusion, bf16[256,1024]{1,0:T(8,128)(2,1)} %bitcast.95, s32[256]{0:T(256)S(1)} %get-tuple-element.60), kind=kOutput, calls=%fused_computation.4 | convolution fusion | flops 606601216 | bytes 2950144 | tf_op jit(solution)/shard_map/dot_general | solution.py:113
  13.1 12.2 %all-to-all-start = ((bf16[64,16,1152]{2,1,0:T(8,128)(2,1)}), bf16[64,16,1152]{2,1,0:T(8,128)(2,1)S(1)}, u32[]{:S(2)}, u32[]{:S(2)}) async-start(bf16[64,16,1152]{2,1,0:T(8,128)(2,1)} %bitcast.12), calls=%async_computation | async-start | bytes 4718592 | tf_op jit(solution)/shard_map/all_to_all | solution.py:44
  27.8 1.7 fusion.19.refs_2_
  29.5 1.6 collective-permute-start.2
  31.1 1.7 collective-permute-start.4
  32.8 47.7 %all-to-all-done = bf16[64,16,1152]{2,1,0:T(8,128)(2,1)S(1)} async-done(((bf16[64,16,1152]{2,1,0:T(8,128)(2,1)}), bf16[64,16,1152]{2,1,0:T(8,128)(2,1)S(1)}, u32[]{:S(2)}, u32[]{:S(2)}) %all-to-all-start) | async-done | bytes 2359328 | tf_op jit(solution)/shard_map/all_to_all | solution.py:44
  81.3 1.9 copy.60
  84.2 1.4 fusion.2
  85.6 3.0 %fusion.14.part_ref = f32[520,1024]{1,0:T(8,128)S(1)} fusion(f32[520,1024]{1,0:T(8,128)S(1)} %fusion.2, f32[1024]{0:T(1024)S(1)} %bitcast.110, bf16[1024,1152]{1,0:T(8,128)(2,1)} %bitcast.90, s32[1024]{0:T(1024)S(1)} %bitcast.108), kind=kOutput, calls=%fused_computation.21 | convolution fusion | flops 1094729728 | bytes 6365184 | tf_op jit(solution)/shard_map/dot_general | solution.py:131
  89.0 3.3 %collective-permute-start = (f32[4,4,1024]{2,1,0:T(4,128)S(1)}, f32[4,4,1024]{2,1,0:T(4,128)S(1)}, u32[]{:S(2)}, u32[]{:S(2)}) collective-permute-start(f32[4,4,1024]{2,1,0:T(4,128)S(1)} %pad_maximum_fusion.1), channel_id=1, source_target_pairs={{0,1},{1,2},{2,3},{3,4},{4,5},{5,6},{6,7},{7,8},{8,9},{9,10},{10,1... | collective-permute-start | bytes 196616 | tf_op jit(solution)/shard_map/ppermute | solution.py:25
  92.4 4.4 %collective-permute-start.1 = (f32[4,4,1024]{2,1,0:T(4,128)S(1)}, f32[4,4,1024]{2,1,0:T(4,128)S(1)}, u32[]{:S(2)}, u32[]{:S(2)}) collective-permute-start(f32[4,4,1024]{2,1,0:T(4,128)S(1)} %pad_maximum_fusion.2), channel_id=1, source_target_pairs={{1,0},{2,1},{3,2},{4,3},{5,4},{6,5},{7,6},{8,7},{9,8},{10,9},{11,1... | collective-permute-start | bytes 196616 | tf_op jit(solution)/shard_map/ppermute | solution.py:25
  96.9 1.9 slice.168
  98.8 1.6 collective-permute-start.3
  100.4 1.9 slice.169
  102.3 1.6 collective-permute-start.5
  108.6 3.7 %all-to-all-start.1 = ((bf16[4,528,256]{2,1,0:T(8,128)(2,1)}), bf16[4,528,256]{2,1,0:T(8,128)(2,1)S(1)}, u32[]{:S(2)}, u32[]{:S(2)}) async-start(bf16[4,528,256]{2,1,0:T(8,128)(2,1)} %copy-done.5), calls=%async_computation.1 | async-start | bytes 2162688 | tf_op jit(solution)/shard_map/all_to_all | solution.py:44
  112.4 2.8 %copy-done.6 = bf16[3,1024,1024]{2,1,0:T(8,128)(2,1)S(1)} copy-done((bf16[3,1024,1024]{2,1,0:T(8,128)(2,1)S(1)}, bf16[3,1024,1024]{2,1,0:T(8,128)(2,1)}, u32[]{:S(2)}) %copy-start.6) | copy-done | bytes 6291480
  118.9 4.8 %shard_map.78 = bf16[4,528,256]{2,1,0:T(8,128)(2,1)S(1)} custom-call(bf16[528,1024]{1,0:T(8,128)(2,1)S(1)} %copy-done.9, bf16[528,1024]{1,0:T(8,128)(2,1)S(1)} %copy-done.11, bf16[528,1024]{1,0:T(8,128)(2,1)S(1)} %copy-done.13, bf16[3,1024,1024]{2,1,0:T(8,128)(2,1)S(1)} %copy-done.6, bf16[512,1024]{1,0:T(8,128)(2,1)S(1)} %bitcast.85, ...), custom_call_target="tpu_custom_call" | custom-call | flops 3321888768 | bytes 11534336 | tf_op jit(solution)/shard_map/pallas_call | solution.py:198
  128.3 6.6 %shard_map.79 = (f32[32,16,768]{2,1,0:T(8,128)S(1)}, bf16[32,16,768]{2,1,0:T(8,128)(2,1)}) custom-call(s32[5]{0:T(128)S(1)} %broadcast_add_fusion.2.refs_0_, bf16[4,528,256]{2,1,0:T(8,128)(2,1)S(1)} %copy-done.4, bf16[512,1024]{1,0:T(8,128)(2,1)} %fusion.19.refs_2_, bf16[512,1024]{1,0:T(8,128)(2,1)} %collective-permute-done.2.refs_3_, ...), custom_call_target="tpu_custom_call" | custom-call | flops 3221225472 | bytes 10485760 | tf_op jit(solution)/shard_map/pallas_call | solution.py:268
  137.1 4.6 %all-to-all-start.2 = ((bf16[4,528,256]{2,1,0:T(8,128)(2,1)}), bf16[4,528,256]{2,1,0:T(8,128)(2,1)S(1)}, u32[]{:S(2)}, u32[]{:S(2)}) async-start(bf16[4,528,256]{2,1,0:T(8,128)(2,1)} %broadcast_add_fusion), calls=%async_computation.2 | async-start | bytes 2162688 | tf_op jit(solution)/shard_map/all_to_all | solution.py:44
  145.3 12.6 %all-to-all-done.2.refs_1_ = bf16[4,528,256]{2,1,0:T(8,128)(2,1)S(1)} async-done(((bf16[4,528,256]{2,1,0:T(8,128)(2,1)}), bf16[4,528,256]{2,1,0:T(8,128)(2,1)S(1)}, u32[]{:S(2)}, u32[]{:S(2)}) %all-to-all-start.2) | async-done | bytes 1081376 | tf_op jit(solution)/shard_map/all_to_all | solution.py:44
  157.8 2.2 copy-done.7
  160.0 4.0 %shard_map.80 = (f32[32,16,768]{2,1,0:T(8,128)S(1)}, bf16[32,16,768]{2,1,0:T(8,128)(2,1)S(1)}) custom-call(s32[5]{0:T(128)S(1)} %broadcast_add_fusion.1.refs_0_, bf16[4,528,256]{2,1,0:T(8,128)(2,1)S(1)} %all-to-all-done.2.refs_1_, bf16[2048,1024]{1,0:T(8,128)(2,1)S(1)} %bitcast.86), custom_call_target="tpu_custom_call" | custom-call | flops 3221225472 | bytes 10485760 | tf_op jit(solution)/shard_map/pallas_call | solution.py:268
  164.1 4.2 %all-to-all-start.4 = ((bf16[4,128,768]{2,1,0:T(8,128)(2,1)}), bf16[4,128,768]{2,1,0:T(8,128)(2,1)S(1)}, u32[]{:S(2)}, u32[]{:S(2)}) async-start(bf16[4,128,768]{2,1,0:T(8,128)(2,1)} %bitcast.87), calls=%async_computation.4 | async-start | bytes 1572864 | tf_op jit(solution)/shard_map/all_to_all | solution.py:44
  168.3 2.2 add_convert_fusion
  170.6 9.2 %all-to-all-done.4 = bf16[4,128,768]{2,1,0:T(8,128)(2,1)S(1)} async-done(((bf16[4,128,768]{2,1,0:T(8,128)(2,1)}), bf16[4,128,768]{2,1,0:T(8,128)(2,1)S(1)}, u32[]{:S(2)}, u32[]{:S(2)}) %all-to-all-start.4) | async-done | bytes 786464 | tf_op jit(solution)/shard_map/all_to_all | solution.py:44
  179.8 4.9 %all-to-all-start.3 = ((bf16[4,128,768]{2,1,0:T(8,128)(2,1)}), bf16[4,128,768]{2,1,0:T(8,128)(2,1)S(1)}, u32[]{:S(2)}, u32[]{:S(2)}) async-start(bf16[4,128,768]{2,1,0:T(8,128)(2,1)} %bitcast.38), calls=%async_computation.3 | async-start | bytes 1572864 | tf_op jit(solution)/shard_map/all_to_all | solution.py:44
  184.8 10.5 %all-to-all-done.3 = bf16[4,128,768]{2,1,0:T(8,128)(2,1)S(1)} async-done(((bf16[4,128,768]{2,1,0:T(8,128)(2,1)}), bf16[4,128,768]{2,1,0:T(8,128)(2,1)S(1)}, u32[]{:S(2)}, u32[]{:S(2)}) %all-to-all-start.3) | async-done | bytes 786464 | tf_op jit(solution)/shard_map/all_to_all | solution.py:44
  195.5 18.7 %all_to_all.30 = bf16[8,2,16,768]{3,2,1,0:T(8,128)(2,1)S(1)} all-to-all(bf16[8,2,16,768]{3,2,1,0:T(8,128)(2,1)S(1)} %pad_maximum_fusion), channel_id=1, replica_groups=mesh['video'=4,'x'=4,'z'=8,'core'=2] {'z'}, dimensions={0} | all-to-all | bytes 786432 | tf_op jit(solution)/shard_map/all_to_all | solution.py:44
  215.5 1.5 collective-permute-start.9
  217.0 2.0 collective-permute-done.8
  219.0 2.7 %collective-permute-done.9 = f32[2,16,768]{2,1,0:T(8,128)S(1)} collective-permute-done((f32[2,16,768]{2,1,0:T(8,128)S(1)}, f32[2,16,768]{2,1,0:T(8,128)S(1)}, u32[]{:S(2)}, u32[]{:S(2)}) %collective-permute-start.9) | collective-permute-done | bytes 98336 | tf_op jit(solution)/shard_map/ppermute | solution.py:30
  (115 shorter events, 28.4 us)
Async XLA Ops:
  13.1 14.7 %copy-start = (bf16[4,128,1024]{2,1,0:T(8,128)(2,1)S(1)}, bf16[4,128,1024]{2,1,0:T(8,128)(2,1)}, u32[]{:S(2)}) copy-start(bf16[4,128,1024]{2,1,0:T(8,128)(2,1)} %param.10) | copy-start | bytes 3145732
  13.1 67.4 %all-to-all-start = ((bf16[64,16,1152]{2,1,0:T(8,128)(2,1)}), bf16[64,16,1152]{2,1,0:T(8,128)(2,1)S(1)}, u32[]{:S(2)}, u32[]{:S(2)}) async-start(bf16[64,16,1152]{2,1,0:T(8,128)(2,1)} %bitcast.12), calls=%async_computation | async-start | bytes 4718592 | tf_op jit(solution)/shard_map/all_to_all | solution.py:44
  25.2 120.0 %all-gather.2.cloned.1.call-start = ((), (), s32[]{:S(2)}) async-start(), calls=%async_computation.6 | async-start | bytes 5242880 | tf_op jit(solution)/shard_map/all_gather | solution.py:311
  29.5 67.4 %collective-permute-start.2 = (bf16[512,1024]{1,0:T(8,128)(2,1)}, bf16[512,1024]{1,0:T(8,128)(2,1)}, u32[]{:S(2)}, u32[]{:S(2)}) collective-permute-start(bf16[512,1024]{1,0:T(8,128)(2,1)} %fusion.19.refs_2_), channel_id=1, source_target_pairs={{0,64},{64,128},{128,192},{192,0},{1,65},{65,129},{129,193},{193,1... | collective-permute-start | bytes 3145736 | tf_op jit(solution)/shard_map/ppermute | solution.py:30
  31.1 69.3 %collective-permute-start.4 = (bf16[512,1024]{1,0:T(8,128)(2,1)}, bf16[512,1024]{1,0:T(8,128)(2,1)}, u32[]{:S(2)}, u32[]{:S(2)}) collective-permute-start(bf16[512,1024]{1,0:T(8,128)(2,1)} %fusion.19.refs_2_), channel_id=1, source_target_pairs={{0,192},{64,0},{128,64},{192,128},{1,193},{65,1},{129,65},{193,129... | collective-permute-start | bytes 3145736 | tf_op jit(solution)/shard_map/ppermute | solution.py:30
  80.5 5.1 %copy-start.15 = (bf16[64,16,1152]{2,1,0:T(8,128)(2,1)}, bf16[64,16,1152]{2,1,0:T(8,128)(2,1)S(1)}, u32[]{:S(2)}) copy-start(bf16[64,16,1152]{2,1,0:T(8,128)(2,1)S(1)} %all-to-all-done) | copy-start | bytes 7077892
  89.0 15.0 %collective-permute-start = (f32[4,4,1024]{2,1,0:T(4,128)S(1)}, f32[4,4,1024]{2,1,0:T(4,128)S(1)}, u32[]{:S(2)}, u32[]{:S(2)}) collective-permute-start(f32[4,4,1024]{2,1,0:T(4,128)S(1)} %pad_maximum_fusion.1), channel_id=1, source_target_pairs={{0,1},{1,2},{2,3},{3,4},{4,5},{5,6},{6,7},{7,8},{8,9},{9,10},{10,1... | collective-permute-start | bytes 196616 | tf_op jit(solution)/shard_map/ppermute | solution.py:25
  92.4 11.6 %collective-permute-start.1 = (f32[4,4,1024]{2,1,0:T(4,128)S(1)}, f32[4,4,1024]{2,1,0:T(4,128)S(1)}, u32[]{:S(2)}, u32[]{:S(2)}) collective-permute-start(f32[4,4,1024]{2,1,0:T(4,128)S(1)} %pad_maximum_fusion.2), channel_id=1, source_target_pairs={{1,0},{2,1},{3,2},{4,3},{5,4},{6,5},{7,6},{8,7},{9,8},{10,9},{11,1... | collective-permute-start | bytes 196616 | tf_op jit(solution)/shard_map/ppermute | solution.py:25
  98.8 27.2 %collective-permute-start.3 = (bf16[256,1024]{1,0:T(8,128)(2,1)}, bf16[256,1024]{1,0:T(8,128)(2,1)}, u32[]{:S(2)}, u32[]{:S(2)}) collective-permute-start(bf16[256,1024]{1,0:T(8,128)(2,1)} %slice.168), channel_id=1, source_target_pairs={{0,64},{64,128},{128,192},{192,0},{1,65},{65,129},{129,193},{193,1... | collective-permute-start | bytes 1572872 | tf_op jit(solution)/shard_map/ppermute | solution.py:30
  102.3 23.7 %collective-permute-start.5 = (bf16[256,1024]{1,0:T(8,128)(2,1)}, bf16[256,1024]{1,0:T(8,128)(2,1)}, u32[]{:S(2)}, u32[]{:S(2)}) collective-permute-start(bf16[256,1024]{1,0:T(8,128)(2,1)} %slice.169), channel_id=1, source_target_pairs={{0,192},{64,0},{128,64},{192,128},{1,193},{65,1},{129,65},{193,129... | collective-permute-start | bytes 1572872 | tf_op jit(solution)/shard_map/ppermute | solution.py:30
  104.5 1.0 copy-start.5
  105.5 1.0 copy-start.8
  106.5 1.0 copy-start.10
  107.5 1.1 copy-start.12
  108.6 17.4 %all-to-all-start.1 = ((bf16[4,528,256]{2,1,0:T(8,128)(2,1)}), bf16[4,528,256]{2,1,0:T(8,128)(2,1)S(1)}, u32[]{:S(2)}, u32[]{:S(2)}) async-start(bf16[4,528,256]{2,1,0:T(8,128)(2,1)} %copy-done.5), calls=%async_computation.1 | async-start | bytes 2162688 | tf_op jit(solution)/shard_map/all_to_all | solution.py:44
  112.4 2.8 %copy-start.6 = (bf16[3,1024,1024]{2,1,0:T(8,128)(2,1)S(1)}, bf16[3,1024,1024]{2,1,0:T(8,128)(2,1)}, u32[]{:S(2)}) copy-start(bf16[3,1024,1024]{2,1,0:T(8,128)(2,1)} %taps_ref.1) | copy-start | bytes 18874372
  115.2 1.2 copy-start.9
  116.5 1.2 copy-start.11
  117.7 1.2 copy-start.13
  123.8 1.0 copy-start.1
  126.0 10.0 %copy-start.2 = (bf16[4,528,256]{2,1,0:T(8,128)(2,1)S(1)}, bf16[4,528,256]{2,1,0:T(8,128)(2,1)}, u32[]{:S(2)}) copy-start(bf16[4,528,256]{2,1,0:T(8,128)(2,1)} %copy-done.1) | copy-start | bytes 3244036
  126.0 1.0 copy-start.3
  127.0 1.2 copy-start.4
  134.9 7.0 %collective-permute-start.6 = (bf16[32,16,768]{2,1,0:T(8,128)(2,1)}, bf16[32,16,768]{2,1,0:T(8,128)(2,1)}, u32[]{:S(2)}, u32[]{:S(2)}) collective-permute-start(bf16[32,16,768]{2,1,0:T(8,128)(2,1)} %get-tuple-element.15), channel_id=1, source_target_pairs={{0,1},{1,0},{2,3},{3,2},{4,5},{5,4},{6,7},{7,6},{8,9},{9,8},{10,11... | collective-permute-start | bytes 2359304 | tf_op jit(solution)/shard_map/ppermute | solution.py:30
  137.1 20.7 %all-to-all-start.2 = ((bf16[4,528,256]{2,1,0:T(8,128)(2,1)}), bf16[4,528,256]{2,1,0:T(8,128)(2,1)S(1)}, u32[]{:S(2)}, u32[]{:S(2)}) async-start(bf16[4,528,256]{2,1,0:T(8,128)(2,1)} %broadcast_add_fusion), calls=%async_computation.2 | async-start | bytes 2162688 | tf_op jit(solution)/shard_map/all_to_all | solution.py:44
  157.8 2.2 copy-start.7
  164.0 4.3 %collective-permute-start.7 = (bf16[32,16,768]{2,1,0:T(8,128)(2,1)S(1)}, bf16[32,16,768]{2,1,0:T(8,128)(2,1)}, u32[]{:S(2)}, u32[]{:S(2)}) collective-permute-start(bf16[32,16,768]{2,1,0:T(8,128)(2,1)S(1)} %get-tuple-element.17), channel_id=1, source_target_pairs={{0,1},{1,0},{2,3},{3,2},{4,5},{5,4},{6,7},{7,6},{8,9},{9,8},{10,11... | collective-permute-start | bytes 2359304 | tf_op jit(solution)/shard_map/ppermute | solution.py:30
  164.1 15.7 %all-to-all-start.4 = ((bf16[4,128,768]{2,1,0:T(8,128)(2,1)}), bf16[4,128,768]{2,1,0:T(8,128)(2,1)S(1)}, u32[]{:S(2)}, u32[]{:S(2)}) async-start(bf16[4,128,768]{2,1,0:T(8,128)(2,1)} %bitcast.87), calls=%async_computation.4 | async-start | bytes 1572864 | tf_op jit(solution)/shard_map/all_to_all | solution.py:44
  179.8 15.6 %all-to-all-start.3 = ((bf16[4,128,768]{2,1,0:T(8,128)(2,1)}), bf16[4,128,768]{2,1,0:T(8,128)(2,1)S(1)}, u32[]{:S(2)}, u32[]{:S(2)}) async-start(bf16[4,128,768]{2,1,0:T(8,128)(2,1)} %bitcast.38), calls=%async_computation.3 | async-start | bytes 1572864 | tf_op jit(solution)/shard_map/all_to_all | solution.py:44
  214.3 4.7 %collective-permute-start.8 = (f32[2,16,768]{2,1,0:T(8,128)S(1)}, f32[2,16,768]{2,1,0:T(8,128)S(1)}, u32[]{:S(2)}, u32[]{:S(2)}) collective-permute-start(f32[2,16,768]{2,1,0:T(8,128)S(1)} %convert_reduce_fusion), channel_id=1, source_target_pairs={{0,192},{64,0},{128,64},{192,128},{1,193},{65,1},{129,65},{193,129... | collective-permute-start | bytes 294920 | tf_op jit(solution)/shard_map/ppermute | solution.py:30
  215.5 6.1 %collective-permute-start.9 = (f32[2,16,768]{2,1,0:T(8,128)S(1)}, f32[2,16,768]{2,1,0:T(8,128)S(1)}, u32[]{:S(2)}, u32[]{:S(2)}) collective-permute-start(f32[2,16,768]{2,1,0:T(8,128)S(1)} %convert_reduce_fusion), channel_id=1, source_target_pairs={{0,128},{64,192},{128,0},{192,64},{1,129},{65,193},{129,1},{193,65... | collective-permute-start | bytes 294920 | tf_op jit(solution)/shard_map/ppermute | solution.py:30
  217.0 5.8 %collective-permute-start.10 = (f32[2,16,768]{2,1,0:T(8,128)S(1)}, f32[2,16,768]{2,1,0:T(8,128)S(1)}, u32[]{:S(2)}, u32[]{:S(2)}) collective-permute-start(f32[2,16,768]{2,1,0:T(8,128)S(1)} %convert_reduce_fusion), channel_id=1, source_target_pairs={{0,64},{64,128},{128,192},{192,0},{1,65},{65,129},{129,193},{193,1... | collective-permute-start | bytes 294920 | tf_op jit(solution)/shard_map/ppermute | solution.py:30
  (1 other events, 0.9 us)
Sparse Core Ops, SparseCore 0:
  27.9 62.3 all-gather.1

commit v3 on v1

--- a/solution.py
+++ b/solution.py
@@ -122,57 +122,109 @@
     return total
 
 
-def finish_kernel(part_ref, low_in_ref, high_in_ref, after_ref, main_ref, before_ref, share_ref):
-    videos, quarters = low_in_ref.shape[1], share_ref.shape[0]
+def grads_kernel(
+    valid_ref,
+    part_ref,
+    low_in_ref,
+    high_in_ref,
+    taps_ref,
+    pre_ref,
+    pre_low_ref,
+    pre_high_ref,
+    share_ref,
+    pre_share_ref,
+    windows_ref,
+):
+    videos = low_in_ref.shape[1]
     width = share_ref.shape[2]
     edges = part_ref.shape[0] - 2 * videos
     rows = edges // videos
-    row = lax.broadcasted_iota(jnp.int32, (rows, part_ref.shape[1]), 0)
-    low_edges, high_edges = ([], [], []), ([], [], [])
-    for video in range(videos):
-        span = slice(video * rows, (video + 1) * rows)
-        main = part_ref[span, :]
-        main = main + jnp.where(row == 0, low_in_ref[2, video : video + 1, :], 0.0)
-        main = main + jnp.where(row == rows - 1, high_in_ref[0, video : video + 1, :], 0.0)
-        low = part_ref[edges + video : edges + video + 1, :] + low_in_ref[1, video : video + 1, :]
-        high_at = edges + videos + video
-        high = part_ref[high_at : high_at + 1, :] + high_in_ref[1, video : video + 1, :]
-        before_ref[span, :] = jnp.where(row == 0, low, pltpu.roll(main, 1, 0)).astype(jnp.bfloat16)
-        after_ref[span, :] = jnp.where(row == rows - 1, high, pltpu.roll(main, rows - 1, 0)).astype(
-            jnp.bfloat16
+    channels = part_ref.shape[1]
+    quarter = pl.program_id(0)
+
+    @pl.when(quarter == 0)
+    def _():
+        row = lax.broadcasted_iota(jnp.int32, (rows, channels), 0)
+        low_edges, high_edges = ([], [], []), ([], [], [])
+        for video in range(videos):
+            span = slice(video * rows, (video + 1) * rows)
+            one = slice(video, video + 1)
+            main = part_ref[span, :]
+            main = main + jnp.where(row == 0, low_in_ref[2, one, :], 0.0)
+            main = main + jnp.where(row == rows - 1, high_in_ref[0, one, :], 0.0)
+            low = part_ref[edges + video : edges + video + 1, :] + low_in_ref[1, one, :]
+            high_at = edges + videos + video
+            high = part_ref[high_at : high_at + 1, :] + high_in_ref[1, one, :]
+            after = jnp.where(row == rows - 1, high, pltpu.roll(main, rows - 1, 0))
+            before = jnp.where(row == 0, low, pltpu.roll(main, 1, 0))
+            for index, part in enumerate((after, main, before)):
+                windows_ref[index, span, :] = part.astype(jnp.bfloat16)
+            for index, part in enumerate((main[:1], low, low_in_ref[0, one, :])):
+                low_edges[index].append(part)
+            for index, part in enumerate((high_in_ref[2, one, :], high, main[rows - 1 :])):
+                high_edges[index].append(part)
+        spare = [jnp.zeros((windows_ref.shape[1] - edges - 2 * videos, channels), jnp.float32)]
+        for index in range(3):
+            edge = jnp.concatenate(low_edges[index] + high_edges[index] + spare, axis=0)
+            windows_ref[index, edges:, :] = edge.astype(jnp.bfloat16)
+
+    total = jnp.zeros(share_ref.shape[1:], jnp.float32)
+    for index in range(3):
+        total = total + lax.dot_general(
+            windows_ref[index],
+            taps_ref[index],
+            (((1,), (1,)), ((), ())),
+            preferred_element_type=jnp.float32,
         )
-        for index, part in enumerate((main[:1], low, low_in_ref[0, video : video + 1, :])):
-            low_edges[index].append(part)
-        for index, part in enumerate((high_in_ref[2, video : video + 1, :], high, main[rows - 1 :])):
-            high_edges[index].append(part)
-        main = main.astype(jnp.bfloat16)
-        main_ref[span, :] = main
-        for quarter in range(quarters):
-            share_ref[quarter, span, :] = main[:, quarter * width : (quarter + 1) * width]
-    spare = [jnp.zeros((main_ref.shape[0] - edges - 2 * videos, part_ref.shape[1]), jnp.float32)]
-    for index, ref in enumerate((after_ref, main_ref, before_ref)):
-        edge = jnp.concatenate(low_edges[index] + high_edges[index] + spare, axis=0)
-        edge = edge.astype(jnp.bfloat16)
-        ref[edges:, :] = edge
-        if ref is main_ref:
-            for quarter in range(quarters):
-                share_ref[quarter, edges:, :] = edge[:, quarter * width : (quarter + 1) * width]
-
-
-def finish(partial, from_low, from_high, main_rows, quarters):
-    channels = partial.shape[1]
-    full = jax.ShapeDtypeStruct((main_rows + 16, channels), jnp.bfloat16)
-    share = jax.ShapeDtypeStruct((quarters, main_rows + 16, channels // quarters), jnp.bfloat16)
+    spare = jnp.zeros((windows_ref.shape[1] - edges - 2 * videos, width), jnp.float32)
+    slope = jnp.concatenate(
+        [
+            silu_slope(pre_ref[...].astype(jnp.float32)),
+            jnp.where(valid_ref[0] > 0, silu_slope(pre_low_ref[3]), 0.0),
+            jnp.where(valid_ref[1] > 0, silu_slope(pre_high_ref[3]), 0.0),
+            spare,
+        ],
+        axis=0,
+    )
+    pre_share_ref[0] = (total * slope).astype(jnp.bfloat16)
+    lanes = pl.ds(pl.multiple_of(quarter * width, width), width)
+    share_ref[0] = windows_ref[1, :, lanes]
+
+
+def gradients(partial, from_low, from_high, filter_second, pre_rows, valid, quarters):
+    lag_count, channels, _ = filter_second.shape
+    rows, width = pre_rows.shape[0] + 16, channels // quarters
+    edge_shape = from_low.shape
+    share = jax.ShapeDtypeStruct((quarters, rows, width), jnp.bfloat16)
+    share_spec = pl.BlockSpec((1, rows, width), lambda q: (q, 0, 0))
+    edge_spec = pl.BlockSpec(edge_shape, lambda q: (0, 0, 0))
+    edge_part = pl.BlockSpec(edge_shape[:2] + (width,), lambda q: (0, 0, q))
     return pl.pallas_call(
-        finish_kernel,
-        out_shape=(full, full, full, share),
-        compiler_params=pltpu.CompilerParams(vmem_limit_bytes=40 * 2**20),
-        cost_estimate=pl.CostEstimate(flops=0, bytes_accessed=8 * 2**20, transcendentals=0),
-    )(partial, from_low, from_high)
-
-
-def terms_kernel(videos, source_count, order_ref, grad_ref, *refs):
-    input_refs, (keep_ref, give_ref, lag_ref) = refs[:-3], refs[-3:]
+        grads_kernel,
+        grid=(quarters,),
+        out_shape=(share, share),
+        in_specs=[
+            pl.BlockSpec(memory_space=pltpu.SMEM),
+            pl.BlockSpec(partial.shape, lambda q: (0, 0)),
+            edge_spec,
+            edge_spec,
+            pl.BlockSpec((lag_count, width, channels), lambda q: (0, q, 0)),
+            pl.BlockSpec((pre_rows.shape[0], width), lambda q: (0, q)),
+            edge_part,
+            edge_part,
+        ],
+        out_specs=(share_spec, share_spec),
+        scratch_shapes=[pltpu.VMEM((lag_count, rows, channels), jnp.bfloat16)],
+        compiler_params=pltpu.CompilerParams(vmem_limit_bytes=24 * 2**20),
+        cost_estimate=pl.CostEstimate(
+            flops=2 * rows * channels * channels * lag_count,
+            bytes_accessed=12 * 2**20,
+            transcendentals=rows * channels,
+        ),
+    )(valid, partial, from_low, from_high, filter_second, pre_rows, from_low, from_high)
+
+
+def terms_kernel(videos, source_count, order_ref, grad_ref, input_ref, keep_ref, give_ref, lag_ref):
     width = grad_ref.shape[2]
     main = grad_ref.shape[1] - 16
     rows = main // videos
@@ -196,18 +248,12 @@
     channels = groups * 2 * each
     step = min(256, channels)
     for start in range(0, channels, step):
-        total = jnp.zeros((step, outs), jnp.float32)
-        for source in range(source_count):
-            if len(input_refs) == 1:
-                block = input_refs[0][source, :, start : start + step]
-            else:
-                block = input_refs[source][:, start : start + step]
-            total = total + lax.dot_general(
-                block,
-                lag_ref[source * main : (source + 1) * main, :],
-                (((0,), (0,)), ((), ())),
-                preferred_element_type=jnp.float32,
-            )
+        total = lax.dot_general(
+            input_ref[:, start : start + step],
+            lag_ref[...],
+            (((0,), (0,)), ((), ())),
+            preferred_element_type=jnp.float32,
+        )
         total = total.reshape(step // (2 * each), 2, each, outs)
         first, second = total[:, 0], total[:, 1]
         span = slice(start // (2 * each), (start + step) // (2 * each))
@@ -217,7 +263,7 @@
 
 def filter_terms(inputs, gradient, order, videos, lag_count, each):
     source_count, block, width = gradient.shape
-    channels = inputs[0].shape[-1]
+    channels = inputs.shape[-1]
     shape = (channels // (2 * each), each, lag_count * width)
     rows = source_count * (block - 16)
     vmem = pl.BlockSpec(memory_space=pltpu.VMEM)
@@ -227,23 +273,26 @@
             jax.ShapeDtypeStruct(shape, jnp.float32),
             jax.ShapeDtypeStruct(shape, jnp.bfloat16),
         ),
-        in_specs=[pl.BlockSpec(memory_space=pltpu.SMEM)] + [vmem] * (1 + len(inputs)),
+        in_specs=[pl.BlockSpec(memory_space=pltpu.SMEM)] + [vmem] * 2,
         out_specs=(vmem, vmem),
         scratch_shapes=[pltpu.VMEM((rows, lag_count * width), jnp.bfloat16)],
-        compiler_params=pltpu.CompilerParams(vmem_limit_bytes=40 * 2**20),
+        compiler_params=pltpu.CompilerParams(vmem_limit_bytes=20 * 2**20),
         cost_estimate=pl.CostEstimate(
             flops=2 * rows * channels * lag_count * width,
             bytes_accessed=10 * 2**20,
             transcendentals=0,
         ),
-    )(order, gradient, *inputs)
-
-
-def reduce_core_x(keep, give):
+    )(order, gradient, inputs)
+
+
+def share_by_core(keep, give):
+    got = ring_shift(give, "core", 1)
+    return (keep + got.astype(jnp.float32)).astype(jnp.bfloat16)
+
+
+def sum_over_x(share):
     x_total, z_total = lax.axis_size("x"), lax.axis_size("z")
-    groups, each, outs = keep.shape
-    got = ring_shift(give, "core", 1)
-    share = (keep + got.astype(jnp.float32)).astype(jnp.bfloat16)
+    groups, each, outs = share.shape
     share = exchange(share.reshape(x_total, z_total * each, outs), "x")
     return jnp.sum(share.astype(jnp.float32), axis=0).reshape(z_total, each, outs)
 
@@ -261,57 +310,41 @@
 
     pre_values = preact.astype(jnp.float32).reshape(main_rows, channels)
     activation = jax.nn.silu(pre_values).astype(jnp.bfloat16)
-    act_all = lax.all_gather(activation, "video", axis=0, tiled=False)
-    after_send = sent[0, 0, 0] * 0
-    feature_rows = features.reshape(main_rows, channels) + after_send
-    feature_all = [feature_rows] + [
-        ring_shift(feature_rows, "video", shift) for shift in range(1, quarters)
-    ]
-    pre_low = neighbours(preact[:, -1] + after_send, True)
-    pre_high = neighbours(preact[:, 0] + after_send, False)
-    at = lax.axis_index(TM)
-    edge_slope = jnp.concatenate(
-        [
-            jnp.where(at > 0, silu_slope(pre_low.astype(jnp.float32)), 0.0),
-            jnp.where(at < peers - 1, silu_slope(pre_high.astype(jnp.float32)), 0.0),
-            jnp.zeros((16 - 2 * video_count, channels), jnp.float32),
-        ],
-        axis=0,
+    act_all = lax.all_gather(activation, "video", axis=0, tiled=True)
+    feature_all = lax.all_gather(
+        features.reshape(main_rows, channels), "video", axis=0, tiled=True
     )
 
     partial = collect(got, channels, main_rows + 2 * video_count)
     ends = partial[:main_rows].reshape(video_count, snip_count, channels)
     low = partial[main_rows : main_rows + video_count]
     high = partial[main_rows + video_count :]
-    from_low = neighbours(jnp.stack([ends[:, -2], ends[:, -1], high]), True)
-    from_high = neighbours(jnp.stack([low, ends[:, 0], ends[:, 1]]), False)
-    *windows, snippet_share = finish(partial, from_low, from_high, main_rows, quarters)
+    pre_ends = pre_values.reshape(ends.shape)
+    from_low = neighbours(jnp.stack([ends[:, -2], ends[:, -1], high, pre_ends[:, -1]]), True)
+    from_high = neighbours(jnp.stack([low, ends[:, 0], ends[:, 1], pre_ends[:, 0]]), False)
+    at = lax.axis_index(TM)
+    valid = jnp.stack([at > 0, at < peers - 1]).astype(jnp.int32)
+    pre_rows = preact.reshape(main_rows, channels)
+    snippet_share, pre_share = gradients(
+        partial, from_low, from_high, filter_second, pre_rows, valid, quarters
+    )
     snippet_share = exchange(snippet_share, "video")
-
-    act_grad = jnp.zeros((main_rows + 16, channels), jnp.float32)
-    for window, taps in zip(windows, filter_second):
-        act_grad = act_grad + lax.dot_general(
-            window, taps, (((1,), (1,)), ((), ())), preferred_element_type=jnp.float32
-        )
-    slope = jnp.concatenate([silu_slope(pre_values), edge_slope], axis=0)
-    pre_grad = (act_grad * slope).astype(jnp.bfloat16)
-    pre_grad = pre_grad + snippet_share[0, 0, 0] * 0
-    width = channels // quarters
-    pre_share = jnp.stack([pre_grad[:, q * width : (q + 1) * width] for q in range(quarters)])
+    pre_share = pre_share + snippet_share[0, 0, 0] * 0
+    after_pre = (pre_share[0, 0, 0] * 0).astype(jnp.int32)
     pre_share = exchange(pre_share, "video")
 
-    in_order = [jnp.int32(source) for source in range(quarters)]
-    around = [(place + quarters - source) % quarters for source in range(quarters)]
-    second = filter_terms(
-        [act_all], snippet_share, jnp.stack(in_order + [core]), video_count, lag_count, each
-    )
-    first = filter_terms(
-        feature_all, pre_share, jnp.stack(around + [core]), video_count, lag_count, each
-    )
-    second, first = reduce_core_x(*second), reduce_core_x(*first)
+    order = jnp.stack([jnp.int32(source) for source in range(quarters)] + [core])
+    second = share_by_core(
+        *filter_terms(act_all, snippet_share, order + after_pre, video_count, lag_count, each)
+    )
+    first = share_by_core(
+        *filter_terms(feature_all, pre_share, order, video_count, lag_count, each)
+    )
+    second, first = sum_over_x(second), sum_over_x(first)
     both = jnp.stack([first, second], axis=1).astype(jnp.bfloat16)
     mine = jnp.sum(exchange(both, "z").astype(jnp.float32), axis=0)
 
+    width = channels // quarters
     held = [mine] + [ring_shift(mine, "video", shift) for shift in range(1, quarters)]
     blocks = []
     for quarter in range(quarters):

time: 236 us -> 233 us (0.987)
  waiting for transfers between devices: 83.9 us -> 111 us
  starting transfers between devices: 56.9 us -> 41.8 us
  matrix products: 20.1 us -> 5.16 us
  Pallas kernels: 12.7 us -> 16.6 us
  local copies, waits for them, and re-layouts: 12.7 us -> 9.86 us
    all_to_all x5, waiting for transfers between devices: 78.7 us -> 103 us  [exchange(): return lax.all_to_all(value, axis, split_axis=0, concat_axis=0, tiled=True)]
    dot_general x3 -> x0, matrix products: 14 us -> none  [on_device(): lax.dot_general(window, taps, (((1,), (1,)), ((), ())), preferred_element...]
    ppermute x8 -> x5, starting transfers between devices: 12.3 us -> 2.72 us  [ring_shift(): lax.ppermute(value, axis, [(i, (i + shift) % count) for i in range(count)])]
    ppermute x4 -> x2, starting transfers between devices: 13 us -> 7.67 us  [neighbours(): return lax.ppermute(value, TM, pairs)]
    pallas_call x1, Pallas kernels: 1.24 us -> 5.85 us  [gradients(): pl.pallas_call(grads_kernel, grid=(quarters,), out_shape=(share, share),...]
    ppermute x8 -> x5, waiting for transfers between devices: 2.86 us -> 5.83 us  [ring_shift(): lax.ppermute(value, axis, [(i, (i + shift) % count) for i in range(count)])]
    unnamed x25 -> x30, local copies, waits for them, and re-layouts: 9.2 us -> 7.19 us
  transfers between devices with their start and end apart: 18 -> 14, of which waited for: 9 -> 9; matrix products, arithmetic and copies ran while one was open for 13% -> 7% of each run, Pallas kernels for 5% -> 7%
where the time goes in v3:
time: 233 us; the launch traced here: 232 us
  waiting for transfers between devices  111 us (48%)
  starting transfers between devices  41.8 us (18%)
  blocking collectives  19.6 us (8%)
  Pallas kernels  16.6 us (7%)
  between operations  15.8 us (7%)
  other arithmetic  11.8 us (5%)
  local copies, waits for them, and re-layouts  9.86 us (4%)
  matrix products  5.16 us (2%)
    all_to_all x5, waiting for transfers between devices, exchange(): return lax.all_to_all(value, axis, split_axis=0, concat_axis=0, tiled=True)  103 us
    all_to_all x5, starting transfers between devices, exchange(): return lax.all_to_all(value, axis, split_axis=0, concat_axis=0, tiled=True)  31.3 us
    all_to_all x1, blocking collectives, exchange(): return lax.all_to_all(value, axis, split_axis=0, concat_axis=0, tiled=True)  19.6 us
    pallas_call x2, Pallas kernels, filter_terms(): pl.pallas_call(lambda *refs: terms_kernel(videos, source_count, *refs), o...  10.7 us
    ppermute x2, starting transfers between devices, neighbours(): return lax.ppermute(value, TM, pairs)  7.67 us
    unnamed x30, local copies, waits for them, and re-layouts  7.19 us
    pallas_call x1, Pallas kernels, gradients(): pl.pallas_call(grads_kernel, grid=(quarters,), out_shape=(share, share),...  5.85 us
    ppermute x5, waiting for transfers between devices, ring_shift(): lax.ppermute(value, axis, [(i, (i + shift) % count) for i in range(count)])  5.83 us
  transfers between devices with their start and end apart: 14, of which 9 were waited for; matrix products, arithmetic and copies ran while one was open for 7% of the time, Pallas kernels for 7%

profile of v3, /device:TPU:2, one launch (start us, length us, event | category | flops | bytes accessed | tf_op | source)
XLA Modules:
  0.0 231.8 jit_solution(9104979686272297920)
XLA Ops:
  7.2 2.9 %fusion.11 = bf16[512,1024]{1,0:T(8,128)(2,1)} fusion(bf16[4,128,1024]{2,1,0:T(8,128)(2,1)} %param.10), kind=kLoop, calls=%fused_computation.16 | loop fusion | flops 3145728 | bytes 2097152 | tf_op jit(solution)/shard_map/convert_element_type | solution.py:312
  11.3 2.4 %convolution_convert_fusion = bf16[1024,1152]{1,0:T(8,128)(2,1)} fusion(bf16[256,128]{1,0:T(8,128)(2,1)S(1)} %select_convert_fusion, bf16[256,1024]{1,0:T(8,128)(2,1)S(1)} %bitcast.77, s32[256]{0:T(256)S(1)} %get-tuple-element.58), kind=kOutput, calls=%fused_computation.4 | convolution fusion | flops 606601216 | bytes 2950144 | tf_op jit(solution)/shard_map/dot_general | solution.py:103
  13.7 12.2 %all-to-all-start = ((bf16[64,16,1152]{2,1,0:T(8,128)(2,1)}), bf16[64,16,1152]{2,1,0:T(8,128)(2,1)S(1)}, u32[]{:S(2)}, u32[]{:S(2)}) async-start(bf16[64,16,1152]{2,1,0:T(8,128)(2,1)} %bitcast.10), calls=%async_computation | async-start | bytes 4718592 | tf_op jit(solution)/shard_map/all_to_all | solution.py:34
  26.7 54.4 %all-to-all-done = bf16[64,16,1152]{2,1,0:T(8,128)(2,1)S(1)} async-done(((bf16[64,16,1152]{2,1,0:T(8,128)(2,1)}), bf16[64,16,1152]{2,1,0:T(8,128)(2,1)S(1)}, u32[]{:S(2)}, u32[]{:S(2)}) %all-to-all-start) | async-done | bytes 2359328 | tf_op jit(solution)/shard_map/all_to_all | solution.py:34
  81.9 1.2 fusion.22
  83.1 1.4 fusion.2
  84.5 1.4 fusion.14.part_ref
  86.3 3.3 %collective-permute-start = (f32[4,4,1024]{2,1,0:T(4,128)S(1)}, f32[4,4,1024]{2,1,0:T(4,128)S(1)}, u32[]{:S(2)}, u32[]{:S(2)}) collective-permute-start(f32[4,4,1024]{2,1,0:T(4,128)S(1)} %pad_maximum_fusion.1), channel_id=1, source_target_pairs={{0,1},{1,2},{2,3},{3,4},{4,5},{5,6},{6,7},{7,8},{8,9},{9,10},{10,1... | collective-permute-start | bytes 196616 | tf_op jit(solution)/shard_map/ppermute | solution.py:25
  89.7 4.4 %collective-permute-start.1 = (f32[4,4,1024]{2,1,0:T(4,128)S(1)}, f32[4,4,1024]{2,1,0:T(4,128)S(1)}, u32[]{:S(2)}, u32[]{:S(2)}) collective-permute-start(f32[4,4,1024]{2,1,0:T(4,128)S(1)} %pad_maximum_fusion.2), channel_id=1, source_target_pairs={{1,0},{2,1},{3,2},{4,3},{5,4},{6,5},{7,6},{8,7},{9,8},{10,9},{11,1... | collective-permute-start | bytes 196616 | tf_op jit(solution)/shard_map/ppermute | solution.py:25
  94.1 1.8 collective-permute-done.1.high_in_ref.pre_high_ref
  96.0 5.9 %shard_map.77 = (bf16[4,528,256]{2,1,0:T(8,128)(2,1)S(1)}, bf16[4,528,256]{2,1,0:T(8,128)(2,1)S(1)}) custom-call(s32[2]{0:T(128)S(1)} %add_convert_fusion.2.valid_ref, f32[520,1024]{1,0:T(8,128)S(1)} %fusion.14.part_ref, f32[4,4,1024]{2,1,0:T(4,128)S(1)} %collective-permute-done.low_in_ref.pre_low_ref, ...), custom_call_target="tpu_custom_call" | custom-call | flops 3321888768 | bytes 12582912 | tf_op jit(solution)/shard_map/pallas_call | solution.py:202
  102.9 4.5 %all-to-all-start.1 = ((bf16[4,528,256]{2,1,0:T(8,128)(2,1)}), bf16[4,528,256]{2,1,0:T(8,128)(2,1)S(1)}, u32[]{:S(2)}, u32[]{:S(2)}) async-start(bf16[4,528,256]{2,1,0:T(8,128)(2,1)} %copy-done.1), calls=%async_computation.1 | async-start | bytes 2162688 | tf_op jit(solution)/shard_map/all_to_all | solution.py:34
  107.5 21.1 %all-to-all-done.1.refs_1_ = bf16[4,528,256]{2,1,0:T(8,128)(2,1)S(1)} async-done(((bf16[4,528,256]{2,1,0:T(8,128)(2,1)}), bf16[4,528,256]{2,1,0:T(8,128)(2,1)S(1)}, u32[]{:S(2)}, u32[]{:S(2)}) %all-to-all-start.1) | async-done | bytes 1081376 | tf_op jit(solution)/shard_map/all_to_all | solution.py:34
  130.8 1.2 slice.141
  132.0 4.4 %all-to-all-start.2 = ((bf16[4,528,256]{2,1,0:T(8,128)(2,1)}), bf16[4,528,256]{2,1,0:T(8,128)(2,1)}, u32[]{:S(2)}, u32[]{:S(2)}) async-start(bf16[4,528,256]{2,1,0:T(8,128)(2,1)} %broadcast_add_fusion), calls=%async_computation.2 | async-start | bytes 2162688 | tf_op jit(solution)/shard_map/all_to_all | solution.py:34
  137.2 2.2 copy-done.2
  139.3 5.0 %shard_map.79 = (f32[32,16,768]{2,1,0:T(8,128)S(1)}, bf16[32,16,768]{2,1,0:T(8,128)(2,1)}) custom-call(s32[5]{0:T(128)S(1)} %broadcast_add_fusion.1.refs_0_, bf16[4,528,256]{2,1,0:T(8,128)(2,1)S(1)} %all-to-all-done.1.refs_1_, bf16[2048,1024]{1,0:T(8,128)(2,1)S(1)} %copy-done.2), custom_call_target="tpu_custom_call" | custom-call | flops 3221225472 | bytes 10485760 | tf_op jit(solution)/shard_map/pallas_call | solution.py:270
  144.3 7.5 %all-to-all-done.2.refs_1_ = bf16[4,528,256]{2,1,0:T(8,128)(2,1)} async-done(((bf16[4,528,256]{2,1,0:T(8,128)(2,1)}), bf16[4,528,256]{2,1,0:T(8,128)(2,1)}, u32[]{:S(2)}, u32[]{:S(2)}) %all-to-all-start.2) | async-done | bytes 1081376 | tf_op jit(solution)/shard_map/all_to_all | solution.py:34
  151.8 2.2 copy-done.3
  154.0 5.7 %shard_map.78 = (f32[32,16,768]{2,1,0:T(8,128)S(1)}, bf16[32,16,768]{2,1,0:T(8,128)(2,1)}) custom-call(s32[5]{0:T(128)S(1)} %stack.32.refs_0_, bf16[4,528,256]{2,1,0:T(8,128)(2,1)} %all-to-all-done.2.refs_1_, bf16[2048,1024]{1,0:T(8,128)(2,1)S(1)} %copy-done.3), custom_call_target="tpu_custom_call" | custom-call | flops 3221225472 | bytes 10485760 | tf_op jit(solution)/shard_map/pallas_call | solution.py:270
  159.7 2.3 add_convert_fusion
  162.0 5.3 %all-to-all-start.4 = ((bf16[4,128,768]{2,1,0:T(8,128)(2,1)}), bf16[4,128,768]{2,1,0:T(8,128)(2,1)S(1)}, u32[]{:S(2)}, u32[]{:S(2)}) async-start(bf16[4,128,768]{2,1,0:T(8,128)(2,1)} %bitcast.68), calls=%async_computation.4 | async-start | bytes 1572864 | tf_op jit(solution)/shard_map/all_to_all | solution.py:34
  167.3 2.3 add_convert_fusion.1
  169.5 9.2 %all-to-all-done.4 = bf16[4,128,768]{2,1,0:T(8,128)(2,1)S(1)} async-done(((bf16[4,128,768]{2,1,0:T(8,128)(2,1)}), bf16[4,128,768]{2,1,0:T(8,128)(2,1)S(1)}, u32[]{:S(2)}, u32[]{:S(2)}) %all-to-all-start.4) | async-done | bytes 786464 | tf_op jit(solution)/shard_map/all_to_all | solution.py:34
  178.8 4.9 %all-to-all-start.3 = ((bf16[4,128,768]{2,1,0:T(8,128)(2,1)}), bf16[4,128,768]{2,1,0:T(8,128)(2,1)S(1)}, u32[]{:S(2)}, u32[]{:S(2)}) async-start(bf16[4,128,768]{2,1,0:T(8,128)(2,1)} %bitcast.69), calls=%async_computation.3 | async-start | bytes 1572864 | tf_op jit(solution)/shard_map/all_to_all | solution.py:34
  183.8 10.6 %all-to-all-done.3 = bf16[4,128,768]{2,1,0:T(8,128)(2,1)S(1)} async-done(((bf16[4,128,768]{2,1,0:T(8,128)(2,1)}), bf16[4,128,768]{2,1,0:T(8,128)(2,1)S(1)}, u32[]{:S(2)}, u32[]{:S(2)}) %all-to-all-start.3) | async-done | bytes 786464 | tf_op jit(solution)/shard_map/all_to_all | solution.py:34
  194.6 19.6 %all_to_all.30 = bf16[8,2,16,768]{3,2,1,0:T(8,128)(2,1)S(1)} all-to-all(bf16[8,2,16,768]{3,2,1,0:T(8,128)(2,1)S(1)} %pad_maximum_fusion), channel_id=1, replica_groups=mesh['video'=4,'x'=4,'z'=8,'core'=2] {'z'}, dimensions={0} | all-to-all | bytes 786432 | tf_op jit(solution)/shard_map/all_to_all | solution.py:34
  214.3 1.3 collective-permute-start.4
  215.5 1.5 collective-permute-start.5
  217.0 2.0 collective-permute-done.4
  219.0 2.7 %collective-permute-done.5 = f32[2,16,768]{2,1,0:T(8,128)S(1)} collective-permute-done((f32[2,16,768]{2,1,0:T(8,128)S(1)}, f32[2,16,768]{2,1,0:T(8,128)S(1)}, u32[]{:S(2)}, u32[]{:S(2)}) %collective-permute-start.5) | collective-permute-done | bytes 98336 | tf_op jit(solution)/shard_map/ppermute | solution.py:30
  221.6 1.2 collective-permute-done.6
  (84 shorter events, 8.4 us)
Async XLA Ops:
  7.2 3.0 %copy-start.6 = (s32[4,4,16,2]{2,3,1,0:T(2,128)S(1)}, s32[4,4,16,2]{2,3,1,0:T(2,128)}, u32[]{:S(2)}) copy-start(s32[4,4,16,2]{2,3,1,0:T(2,128)} %param.8) | copy-start | bytes 6148
  7.2 3.1 %copy-start.5 = (f32[4,4,16,2]{2,3,1,0:T(2,128)S(1)}, f32[4,4,16,2]{2,3,1,0:T(2,128)}, u32[]{:S(2)}) copy-start(f32[4,4,16,2]{2,3,1,0:T(2,128)} %param.7) | copy-start | bytes 6148
  7.2 4.1 %copy-start.4 = (bf16[4,4,16,1024]{3,2,1,0:T(8,128)(2,1)S(1)}, bf16[4,4,16,1024]{3,2,1,0:T(8,128)(2,1)}, u32[]{:S(2)}) copy-start(bf16[4,4,16,1024]{3,2,1,0:T(8,128)(2,1)} %param.6) | copy-start | bytes 1572868
  7.2 129.9 %all-gather.5.cloned.1.call-start = ((), (), s32[]{:S(2)}) async-start(), calls=%async_computation.7 | async-start | bytes 5242880 | tf_op jit(solution)/shard_map/all_gather | solution.py:313
  13.7 12.9 %copy-start = (bf16[4,128,1024]{2,1,0:T(8,128)(2,1)S(1)}, bf16[4,128,1024]{2,1,0:T(8,128)(2,1)}, u32[]{:S(2)}) copy-start(bf16[4,128,1024]{2,1,0:T(8,128)(2,1)} %param.10) | copy-start | bytes 3145732
  13.7 67.4 %all-to-all-start = ((bf16[64,16,1152]{2,1,0:T(8,128)(2,1)}), bf16[64,16,1152]{2,1,0:T(8,128)(2,1)S(1)}, u32[]{:S(2)}, u32[]{:S(2)}) async-start(bf16[64,16,1152]{2,1,0:T(8,128)(2,1)} %bitcast.10), calls=%async_computation | async-start | bytes 4718592 | tf_op jit(solution)/shard_map/all_to_all | solution.py:34
  25.8 118.5 %all-gather.3.cloned.1.call-start = ((), (), s32[]{:S(2)}) async-start(), calls=%async_computation.6 | async-start | bytes 5242880 | tf_op jit(solution)/shard_map/all_gather | solution.py:314
  83.1 12.8 %slice-start = ((s8[6291456]{0:T(1024)(128)(4,1)}), s8[4194304]{0:T(1024)(128)(4,1)S(1)}, s32[]{:S(2)}) async-start(s8[6291456]{0:T(1024)(128)(4,1)} %bitcast.66), calls=%async_computation.8 | async-start | bytes 8388608
  84.5 11.4 %slice-start.1 = ((s8[6291456]{0:T(1024)(128)(4,1)}), s8[2097152]{0:T(1024)(128)(4,1)S(1)}, s32[]{:S(2)}) async-start(s8[6291456]{0:T(1024)(128)(4,1)} %bitcast.66), calls=%async_computation.9 | async-start | bytes 4194304
  86.3 7.8 %collective-permute-start = (f32[4,4,1024]{2,1,0:T(4,128)S(1)}, f32[4,4,1024]{2,1,0:T(4,128)S(1)}, u32[]{:S(2)}, u32[]{:S(2)}) collective-permute-start(f32[4,4,1024]{2,1,0:T(4,128)S(1)} %pad_maximum_fusion.1), channel_id=1, source_target_pairs={{0,1},{1,2},{2,3},{3,4},{4,5},{5,6},{6,7},{7,8},{8,9},{9,10},{10,1... | collective-permute-start | bytes 196616 | tf_op jit(solution)/shard_map/ppermute | solution.py:25
  89.7 6.3 %collective-permute-start.1 = (f32[4,4,1024]{2,1,0:T(4,128)S(1)}, f32[4,4,1024]{2,1,0:T(4,128)S(1)}, u32[]{:S(2)}, u32[]{:S(2)}) collective-permute-start(f32[4,4,1024]{2,1,0:T(4,128)S(1)} %pad_maximum_fusion.2), channel_id=1, source_target_pairs={{1,0},{2,1},{3,2},{4,3},{5,4},{6,5},{7,6},{8,7},{9,8},{10,9},{11,1... | collective-permute-start | bytes 196616 | tf_op jit(solution)/shard_map/ppermute | solution.py:25
  101.8 1.1 copy-start.1
  102.9 25.7 %all-to-all-start.1 = ((bf16[4,528,256]{2,1,0:T(8,128)(2,1)}), bf16[4,528,256]{2,1,0:T(8,128)(2,1)S(1)}, u32[]{:S(2)}, u32[]{:S(2)}) async-start(bf16[4,528,256]{2,1,0:T(8,128)(2,1)} %copy-done.1), calls=%async_computation.1 | async-start | bytes 2162688 | tf_op jit(solution)/shard_map/all_to_all | solution.py:34
  132.0 19.8 %all-to-all-start.2 = ((bf16[4,528,256]{2,1,0:T(8,128)(2,1)}), bf16[4,528,256]{2,1,0:T(8,128)(2,1)}, u32[]{:S(2)}, u32[]{:S(2)}) async-start(bf16[4,528,256]{2,1,0:T(8,128)(2,1)} %broadcast_add_fusion), calls=%async_computation.2 | async-start | bytes 2162688 | tf_op jit(solution)/shard_map/all_to_all | solution.py:34
  137.1 2.2 copy-start.2
  144.3 15.4 %collective-permute-start.3 = (bf16[32,16,768]{2,1,0:T(8,128)(2,1)}, bf16[32,16,768]{2,1,0:T(8,128)(2,1)}, u32[]{:S(2)}, u32[]{:S(2)}) collective-permute-start(bf16[32,16,768]{2,1,0:T(8,128)(2,1)} %get-tuple-element.13), channel_id=1, source_target_pairs={{0,1},{1,0},{2,3},{3,2},{4,5},{5,4},{6,7},{7,6},{8,9},{9,8},{10,11... | collective-permute-start | bytes 2359304 | tf_op jit(solution)/shard_map/ppermute | solution.py:30
  151.8 2.2 copy-start.3
  159.7 7.6 %collective-permute-start.2 = (bf16[32,16,768]{2,1,0:T(8,128)(2,1)}, bf16[32,16,768]{2,1,0:T(8,128)(2,1)}, u32[]{:S(2)}, u32[]{:S(2)}) collective-permute-start(bf16[32,16,768]{2,1,0:T(8,128)(2,1)} %get-tuple-element.11), channel_id=1, source_target_pairs={{0,1},{1,0},{2,3},{3,2},{4,5},{5,4},{6,7},{7,6},{8,9},{9,8},{10,11... | collective-permute-start | bytes 2359304 | tf_op jit(solution)/shard_map/ppermute | solution.py:30
  162.0 16.8 %all-to-all-start.4 = ((bf16[4,128,768]{2,1,0:T(8,128)(2,1)}), bf16[4,128,768]{2,1,0:T(8,128)(2,1)S(1)}, u32[]{:S(2)}, u32[]{:S(2)}) async-start(bf16[4,128,768]{2,1,0:T(8,128)(2,1)} %bitcast.68), calls=%async_computation.4 | async-start | bytes 1572864 | tf_op jit(solution)/shard_map/all_to_all | solution.py:34
  178.8 15.6 %all-to-all-start.3 = ((bf16[4,128,768]{2,1,0:T(8,128)(2,1)}), bf16[4,128,768]{2,1,0:T(8,128)(2,1)S(1)}, u32[]{:S(2)}, u32[]{:S(2)}) async-start(bf16[4,128,768]{2,1,0:T(8,128)(2,1)} %bitcast.69), calls=%async_computation.3 | async-start | bytes 1572864 | tf_op jit(solution)/shard_map/all_to_all | solution.py:34
  214.3 4.7 %collective-permute-start.4 = (f32[2,16,768]{2,1,0:T(8,128)S(1)}, f32[2,16,768]{2,1,0:T(8,128)S(1)}, u32[]{:S(2)}, u32[]{:S(2)}) collective-permute-start(f32[2,16,768]{2,1,0:T(8,128)S(1)} %convert_reduce_fusion), channel_id=1, source_target_pairs={{0,192},{64,0},{128,64},{192,128},{1,193},{65,1},{129,65},{193,129... | collective-permute-start | bytes 294920 | tf_op jit(solution)/shard_map/ppermute | solution.py:30
  215.5 6.1 %collective-permute-start.5 = (f32[2,16,768]{2,1,0:T(8,128)S(1)}, f32[2,16,768]{2,1,0:T(8,128)S(1)}, u32[]{:S(2)}, u32[]{:S(2)}) collective-permute-start(f32[2,16,768]{2,1,0:T(8,128)S(1)} %convert_reduce_fusion), channel_id=1, source_target_pairs={{0,128},{64,192},{128,0},{192,64},{1,129},{65,193},{129,1},{193,65... | collective-permute-start | bytes 294920 | tf_op jit(solution)/shard_map/ppermute | solution.py:30
  217.0 5.8 %collective-permute-start.6 = (f32[2,16,768]{2,1,0:T(8,128)S(1)}, f32[2,16,768]{2,1,0:T(8,128)S(1)}, u32[]{:S(2)}, u32[]{:S(2)}) collective-permute-start(f32[2,16,768]{2,1,0:T(8,128)S(1)} %convert_reduce_fusion), channel_id=1, source_target_pairs={{0,64},{64,128},{128,192},{192,0},{1,65},{65,129},{129,193},{193,1... | collective-permute-start | bytes 294920 | tf_op jit(solution)/shard_map/ppermute | solution.py:30
Sparse Core Ops, SparseCore 0:
  10.3 53.7 all-gather.4
  65.9 56.6 all-gather.2

commit v4 on v3

--- a/solution.py
+++ b/solution.py
@@ -132,11 +132,10 @@
     pre_low_ref,
     pre_high_ref,
     share_ref,
-    pre_share_ref,
     windows_ref,
 ):
     videos = low_in_ref.shape[1]
-    width = share_ref.shape[2]
+    width = share_ref.shape[3]
     edges = part_ref.shape[0] - 2 * videos
     rows = edges // videos
     channels = part_ref.shape[1]
@@ -168,7 +167,7 @@
             edge = jnp.concatenate(low_edges[index] + high_edges[index] + spare, axis=0)
             windows_ref[index, edges:, :] = edge.astype(jnp.bfloat16)
 
-    total = jnp.zeros(share_ref.shape[1:], jnp.float32)
+    total = jnp.zeros(share_ref.shape[2:], jnp.float32)
     for index in range(3):
         total = total + lax.dot_general(
             windows_ref[index],
@@ -186,23 +185,23 @@
         ],
         axis=0,
     )
-    pre_share_ref[0] = (total * slope).astype(jnp.bfloat16)
+    share_ref[0, 1] = (total * slope).astype(jnp.bfloat16)
     lanes = pl.ds(pl.multiple_of(quarter * width, width), width)
-    share_ref[0] = windows_ref[1, :, lanes]
+    share_ref[0, 0] = windows_ref[1, :, lanes]
 
 
 def gradients(partial, from_low, from_high, filter_second, pre_rows, valid, quarters):
     lag_count, channels, _ = filter_second.shape
     rows, width = pre_rows.shape[0] + 16, channels // quarters
     edge_shape = from_low.shape
-    share = jax.ShapeDtypeStruct((quarters, rows, width), jnp.bfloat16)
-    share_spec = pl.BlockSpec((1, rows, width), lambda q: (q, 0, 0))
+    share = jax.ShapeDtypeStruct((quarters, 2, rows, width), jnp.bfloat16)
+    share_spec = pl.BlockSpec((1, 2, rows, width), lambda q: (q, 0, 0, 0))
     edge_spec = pl.BlockSpec(edge_shape, lambda q: (0, 0, 0))
     edge_part = pl.BlockSpec(edge_shape[:2] + (width,), lambda q: (0, 0, q))
     return pl.pallas_call(
         grads_kernel,
         grid=(quarters,),
-        out_shape=(share, share),
+        out_shape=share,
         in_specs=[
             pl.BlockSpec(memory_space=pltpu.SMEM),
             pl.BlockSpec(partial.shape, lambda q: (0, 0)),
@@ -213,7 +212,7 @@
             edge_part,
             edge_part,
         ],
-        out_specs=(share_spec, share_spec),
+        out_specs=share_spec,
         scratch_shapes=[pltpu.VMEM((lag_count, rows, channels), jnp.bfloat16)],
         compiler_params=pltpu.CompilerParams(vmem_limit_bytes=24 * 2**20),
         cost_estimate=pl.CostEstimate(
@@ -224,19 +223,19 @@
     )(valid, partial, from_low, from_high, filter_second, pre_rows, from_low, from_high)
 
 
-def terms_kernel(videos, source_count, order_ref, grad_ref, input_ref, keep_ref, give_ref, lag_ref):
-    width = grad_ref.shape[2]
-    main = grad_ref.shape[1] - 16
+def terms_kernel(videos, layer, order_ref, grad_ref, *refs):
+    input_refs, (keep_ref, give_ref, lag_ref) = refs[:-3], refs[-3:]
+    sources, width = grad_ref.shape[0], grad_ref.shape[3]
+    main = grad_ref.shape[2] - 16
     rows = main // videos
     groups, each, outs = keep_ref.shape
-    core = order_ref[source_count]
+    core = order_ref[0]
     row = lax.broadcasted_iota(jnp.int32, (rows, width), 0)
-    for source in range(source_count):
-        at = order_ref[source]
-        edges = grad_ref[at, main:, :].astype(jnp.float32)
+    for source in range(sources):
+        edges = grad_ref[source, layer, main:, :].astype(jnp.float32)
         for video in range(videos):
             span = slice(video * rows, (video + 1) * rows)
-            grad = grad_ref[at, span, :].astype(jnp.float32)
+            grad = grad_ref[source, layer, span, :].astype(jnp.float32)
             low, high = edges[video : video + 1], edges[videos + video : videos + video + 1]
             after = jnp.where(row == rows - 1, high, pltpu.roll(grad, rows - 1, 0))
             before = jnp.where(row == 0, low, pltpu.roll(grad, 1, 0))
@@ -245,15 +244,27 @@
                     source * main + video * rows : source * main + (video + 1) * rows,
                     index * width : (index + 1) * width,
                 ] = part.astype(jnp.bfloat16)
+    pieces = []
+    gathered = input_refs[0].shape[0] // sources
+    if gathered == main:
+        pieces.append((input_refs[0], 0, sources * main, 0))
+    else:
+        for source in range(sources):
+            pieces.append((input_refs[0], source * gathered, gathered, source * main))
+        for index, ref in enumerate(input_refs[1:]):
+            at = pl.multiple_of(order_ref[1 + index] * main + gathered, gathered)
+            pieces.append((ref, 0, main - gathered, at))
     channels = groups * 2 * each
     step = min(256, channels)
     for start in range(0, channels, step):
-        total = lax.dot_general(
-            input_ref[:, start : start + step],
-            lag_ref[...],
-            (((0,), (0,)), ((), ())),
-            preferred_element_type=jnp.float32,
-        )
+        total = jnp.zeros((step, outs), jnp.float32)
+        for ref, first, count, at in pieces:
+            total = total + lax.dot_general(
+                ref[first : first + count, start : start + step],
+                lag_ref[pl.ds(at, count), :],
+                (((0,), (0,)), ((), ())),
+                preferred_element_type=jnp.float32,
+            )
         total = total.reshape(step // (2 * each), 2, each, outs)
         first, second = total[:, 0], total[:, 1]
         span = slice(start // (2 * each), (start + step) // (2 * each))
@@ -261,40 +272,33 @@
         give_ref[span] = jnp.where(core == 0, second, first).astype(jnp.bfloat16)
 
 
-def filter_terms(inputs, gradient, order, videos, lag_count, each):
-    source_count, block, width = gradient.shape
-    channels = inputs.shape[-1]
+def filter_terms(inputs, gradients, layer, order, videos, lag_count, each):
+    sources, _, block, width = gradients.shape
+    channels = inputs[0].shape[-1]
     shape = (channels // (2 * each), each, lag_count * width)
-    rows = source_count * (block - 16)
+    rows = sources * (block - 16)
     vmem = pl.BlockSpec(memory_space=pltpu.VMEM)
     return pl.pallas_call(
-        lambda *refs: terms_kernel(videos, source_count, *refs),
+        lambda *refs: terms_kernel(videos, layer, *refs),
         out_shape=(
             jax.ShapeDtypeStruct(shape, jnp.float32),
             jax.ShapeDtypeStruct(shape, jnp.bfloat16),
         ),
-        in_specs=[pl.BlockSpec(memory_space=pltpu.SMEM)] + [vmem] * 2,
+        in_specs=[pl.BlockSpec(memory_space=pltpu.SMEM)] + [vmem] * (1 + len(inputs)),
         out_specs=(vmem, vmem),
         scratch_shapes=[pltpu.VMEM((rows, lag_count * width), jnp.bfloat16)],
-        compiler_params=pltpu.CompilerParams(vmem_limit_bytes=20 * 2**20),
+        compiler_params=pltpu.CompilerParams(vmem_limit_bytes=24 * 2**20),
         cost_estimate=pl.CostEstimate(
             flops=2 * rows * channels * lag_count * width,
             bytes_accessed=10 * 2**20,
             transcendentals=0,
         ),
-    )(order, gradient, inputs)
+    )(order, gradients, *inputs)
 
 
 def share_by_core(keep, give):
     got = ring_shift(give, "core", 1)
     return (keep + got.astype(jnp.float32)).astype(jnp.bfloat16)
-
-
-def sum_over_x(share):
-    x_total, z_total = lax.axis_size("x"), lax.axis_size("z")
-    groups, each, outs = share.shape
-    share = exchange(share.reshape(x_total, z_total * each, outs), "x")
-    return jnp.sum(share.astype(jnp.float32), axis=0).reshape(z_total, each, outs)
 
 
 def on_device(bin_grad, tap_weight, tap_index, features, preact, filter_second):
@@ -311,40 +315,41 @@
     pre_values = preact.astype(jnp.float32).reshape(main_rows, channels)
     activation = jax.nn.silu(pre_values).astype(jnp.bfloat16)
     act_all = lax.all_gather(activation, "video", axis=0, tiled=True)
-    feature_all = lax.all_gather(
-        features.reshape(main_rows, channels), "video", axis=0, tiled=True
-    )
+    halves = features.reshape(2, main_rows // 2, channels)
+    feature_all = [lax.all_gather(halves[0], "video", axis=0, tiled=True), halves[1]]
+    for shift in range(1, quarters):
+        feature_all.append(ring_shift(halves[1], "video", shift))
 
     partial = collect(got, channels, main_rows + 2 * video_count)
     ends = partial[:main_rows].reshape(video_count, snip_count, channels)
     low = partial[main_rows : main_rows + video_count]
     high = partial[main_rows + video_count :]
-    pre_ends = pre_values.reshape(ends.shape)
-    from_low = neighbours(jnp.stack([ends[:, -2], ends[:, -1], high, pre_ends[:, -1]]), True)
+    arrived = sum(piece[0, 0] * 0 for piece in feature_all[2:]).astype(jnp.float32)
+    pre_ends = pre_values.reshape(ends.shape)[:, :: snip_count - 1] + arrived
+    from_low = neighbours(jnp.stack([ends[:, -2], ends[:, -1], high, pre_ends[:, 1]]), True)
     from_high = neighbours(jnp.stack([low, ends[:, 0], ends[:, 1], pre_ends[:, 0]]), False)
     at = lax.axis_index(TM)
     valid = jnp.stack([at > 0, at < peers - 1]).astype(jnp.int32)
     pre_rows = preact.reshape(main_rows, channels)
-    snippet_share, pre_share = gradients(
-        partial, from_low, from_high, filter_second, pre_rows, valid, quarters
-    )
-    snippet_share = exchange(snippet_share, "video")
-    pre_share = pre_share + snippet_share[0, 0, 0] * 0
-    after_pre = (pre_share[0, 0, 0] * 0).astype(jnp.int32)
-    pre_share = exchange(pre_share, "video")
-
-    order = jnp.stack([jnp.int32(source) for source in range(quarters)] + [core])
+    shares = gradients(partial, from_low, from_high, filter_second, pre_rows, valid, quarters)
+    block, width = shares.shape[2:]
+    shares = exchange(shares.reshape(quarters, 2 * block, width), "video")
+    shares = shares.reshape(quarters, 2, block, width)
+
+    order = jnp.stack([core] + [(place + quarters - source) % quarters for source in range(quarters)])
     second = share_by_core(
-        *filter_terms(act_all, snippet_share, order + after_pre, video_count, lag_count, each)
+        *filter_terms([act_all], shares, 0, order, video_count, lag_count, each)
     )
     first = share_by_core(
-        *filter_terms(feature_all, pre_share, order, video_count, lag_count, each)
-    )
-    second, first = sum_over_x(second), sum_over_x(first)
-    both = jnp.stack([first, second], axis=1).astype(jnp.bfloat16)
+        *filter_terms(feature_all, shares, 1, order, video_count, lag_count, each)
+    )
+    x_total, z_total = lax.axis_size("x"), lax.axis_size("z")
+    both = jnp.stack([part.reshape(x_total, -1, lag_count * width) for part in (first, second)], 1)
+    both = exchange(both.reshape(x_total, -1, lag_count * width), "x")
+    both = jnp.sum(both.astype(jnp.float32), axis=0).astype(jnp.bfloat16)
+    both = both.reshape(2, z_total, each, lag_count * width).transpose(1, 0, 2, 3)
     mine = jnp.sum(exchange(both, "z").astype(jnp.float32), axis=0)
 
-    width = channels // quarters
     held = [mine] + [ring_shift(mine, "video", shift) for shift in range(1, quarters)]
     blocks = []
     for quarter in range(quarters):

time: 233 us -> 228 us (0.979)
  blocking collectives: 19.6 us -> 45.3 us
  waiting for transfers between devices: 111 us -> 87.3 us
  starting transfers between devices: 41.8 us -> 32 us
  local copies, waits for them, and re-layouts: 9.86 us -> 16.1 us
  other arithmetic: 11.8 us -> 7.78 us
  matrix products: 5.16 us -> 8.68 us
  Pallas kernels: 16.6 us -> 14.1 us
    all_to_all x5 -> x2, waiting for transfers between devices: 103 us -> 40.2 us  [exchange(): return lax.all_to_all(value, axis, split_axis=0, concat_axis=0, tiled=True)]
    ppermute x5 -> x8, waiting for transfers between devices: 5.83 us -> 41.5 us  [ring_shift(): lax.ppermute(value, axis, [(i, (i + shift) % count) for i in range(count)])]
    all_to_all x1 -> x2, blocking collectives: 19.6 us -> 45.3 us  [exchange(): return lax.all_to_all(value, axis, split_axis=0, concat_axis=0, tiled=True)]
    all_to_all x5 -> x2, starting transfers between devices: 31.3 us -> 16.7 us  [exchange(): return lax.all_to_all(value, axis, split_axis=0, concat_axis=0, tiled=True)]
    ppermute x5 -> x8, starting transfers between devices: 2.72 us -> 9.87 us  [ring_shift(): lax.ppermute(value, axis, [(i, (i + shift) % count) for i in range(count)])]
    unnamed x30 -> x44, local copies, waits for them, and re-layouts: 7.19 us -> 11.2 us
    ppermute x2, waiting for transfers between devices: 1.81 us -> 5.57 us  [neighbours(): return lax.ppermute(value, TM, pairs)]
    dot_general x2, matrix products: 2.8 us -> 6.37 us  [collect(): total = total + jnp.dot(table, tap_rows, preferred_element_type=jnp.float32)]
  transfers between devices with their start and end apart: 14 -> 14, of which waited for: 9 -> 9; matrix products, arithmetic and copies ran while one was open for 7% -> 8% of each run, Pallas kernels for 7% -> 6%
where the time goes in v4:
time: 228 us
  waiting for transfers between devices  87.3 us (38%)
  blocking collectives  45.3 us (20%)
  starting transfers between devices  32 us (14%)
  between operations  16.5 us (7%)
  local copies, waits for them, and re-layouts  16.1 us (7%)
  Pallas kernels  14.1 us (6%)
  matrix products  8.68 us (4%)
  other arithmetic  7.78 us (3%)
    all_to_all x2, blocking collectives, exchange(): return lax.all_to_all(value, axis, split_axis=0, concat_axis=0, tiled=True)  45.3 us
    ppermute x8, waiting for transfers between devices, ring_shift(): lax.ppermute(value, axis, [(i, (i + shift) % count) for i in range(count)])  41.5 us
    all_to_all x2, waiting for transfers between devices, exchange(): return lax.all_to_all(value, axis, split_axis=0, concat_axis=0, tiled=True)  40.2 us
    all_to_all x2, starting transfers between devices, exchange(): return lax.all_to_all(value, axis, split_axis=0, concat_axis=0, tiled=True)  16.7 us
    unnamed x44, local copies, waits for them, and re-layouts  11.2 us
    ppermute x8, starting transfers between devices, ring_shift(): lax.ppermute(value, axis, [(i, (i + shift) % count) for i in range(count)])  9.87 us
    pallas_call x2, Pallas kernels, filter_terms(): pl.pallas_call(lambda *refs: terms_kernel(videos, layer, *refs), out_shap...  8.25 us
    dot_general x2, matrix products, collect(): total = total + jnp.dot(table, tap_rows, preferred_element_type=jnp.float32)  6.37 us
  transfers between devices with their start and end apart: 14, of which 9 were waited for; matrix products, arithmetic and copies ran while one was open for 8% of the time, Pallas kernels for 6%

profile of v4, /device:TPU:2, one launch (start us, length us, event | category | flops | bytes accessed | tf_op | source)
XLA Modules:
  0.0 227.7 jit_solution(6466260008975302214)
XLA Ops:
  7.2 2.2 fusion.46
  10.6 2.3 %convolution_convert_fusion = bf16[1024,1152]{1,0:T(8,128)(2,1)} fusion(bf16[256,128]{1,0:T(8,128)(2,1)S(1)} %select_convert_fusion, bf16[256,1024]{1,0:T(8,128)(2,1)S(1)} %bitcast.92, s32[256]{0:T(256)S(1)} %get-tuple-element.56), kind=kOutput, calls=%fused_computation.4 | convolution fusion | flops 606601216 | bytes 2950144 | tf_op jit(solution)/shard_map/dot_general | solution.py:103
  12.9 12.3 %all-to-all-start = ((bf16[64,16,1152]{2,1,0:T(8,128)(2,1)}), bf16[64,16,1152]{2,1,0:T(8,128)(2,1)}, u32[]{:S(2)}, u32[]{:S(2)}) async-start(bf16[64,16,1152]{2,1,0:T(8,128)(2,1)} %bitcast.85), calls=%async_computation | async-start | bytes 4718592 | tf_op jit(solution)/shard_map/all_to_all | solution.py:34
  25.3 1.6 fusion.11
  26.9 1.7 collective-permute-start
  28.6 2.9 %collective-permute-start.1 = (bf16[256,1024]{1,0:T(8,128)(2,1)S(1)}, bf16[256,1024]{1,0:T(8,128)(2,1)S(1)}, u32[]{:S(2)}, u32[]{:S(2)}) collective-permute-start(bf16[256,1024]{1,0:T(8,128)(2,1)S(1)} %bitcast.80), channel_id=1, source_target_pairs={{0,128},{64,192},{128,0},{192,64},{1,129},{65,193},{129,1},{193,65... | collective-permute-start | bytes 1572872 | tf_op jit(solution)/shard_map/ppermute | solution.py:30
  31.5 1.3 collective-permute-start.2
  32.9 21.0 %collective-permute-done.refs_4_ = bf16[256,1024]{1,0:T(8,128)(2,1)S(1)} collective-permute-done((bf16[256,1024]{1,0:T(8,128)(2,1)S(1)}, bf16[256,1024]{1,0:T(8,128)(2,1)S(1)}, u32[]{:S(2)}, u32[]{:S(2)}) %collective-permute-start) | collective-permute-done | bytes 524320 | tf_op jit(solution)/shard_map/ppermute | solution.py:30
  54.5 14.1 %collective-permute-done.1.refs_5_ = bf16[256,1024]{1,0:T(8,128)(2,1)S(1)} collective-permute-done((bf16[256,1024]{1,0:T(8,128)(2,1)S(1)}, bf16[256,1024]{1,0:T(8,128)(2,1)S(1)}, u32[]{:S(2)}, u32[]{:S(2)}) %collective-permute-start.1) | collective-permute-done | bytes 524320 | tf_op jit(solution)/shard_map/ppermute | solution.py:30
  71.7 8.7 %all-to-all-done = bf16[64,16,1152]{2,1,0:T(8,128)(2,1)} async-done(((bf16[64,16,1152]{2,1,0:T(8,128)(2,1)}), bf16[64,16,1152]{2,1,0:T(8,128)(2,1)}, u32[]{:S(2)}, u32[]{:S(2)}) %all-to-all-start) | async-done | bytes 2359328 | tf_op jit(solution)/shard_map/all_to_all | solution.py:34
  82.2 1.2 fusion.22
  83.5 3.2 %fusion.2 = f32[520,1024]{1,0:T(8,128)S(1)} fusion(f32[1024]{0:T(1024)S(1)} %get-tuple-element.25, bf16[1024,1152]{1,0:T(8,128)(2,1)} %bitcast.15, s32[1024]{0:T(1024)S(1)} %get-tuple-element.23), kind=kOutput, calls=%fused_computation.7 | convolution fusion | flops 1094197248 | bytes 4235264 | tf_op jit(solution)/shard_map/dot_general | solution.py:121
  86.7 3.1 %fusion.14.part_ref = f32[520,1024]{1,0:T(8,128)S(1)} fusion(f32[520,1024]{1,0:T(8,128)S(1)} %fusion.2, f32[1024]{0:T(1024)S(1)} %get-tuple-element.24, bf16[1024,1152]{1,0:T(8,128)(2,1)} %bitcast.15, s32[1024]{0:T(1024)S(1)} %get-tuple-element.22), kind=kOutput, calls=%fused_computation.22 | convolution fusion | flops 1094729728 | bytes 6365184 | tf_op jit(solution)/shard_map/dot_general | solution.py:121
  90.1 3.3 %collective-permute-start.4 = (f32[4,4,1024]{2,1,0:T(4,128)S(1)}, f32[4,4,1024]{2,1,0:T(4,128)S(1)}, u32[]{:S(2)}, u32[]{:S(2)}) collective-permute-start(f32[4,4,1024]{2,1,0:T(4,128)S(1)} %pad_maximum_fusion.2), channel_id=1, source_target_pairs={{1,0},{2,1},{3,2},{4,3},{5,4},{6,5},{7,6},{8,7},{9,8},{10,9},{11,1... | collective-permute-start | bytes 196616 | tf_op jit(solution)/shard_map/ppermute | solution.py:25
  93.5 2.0 collective-permute-start.3
  95.6 5.6 %collective-permute-done.3.low_in_ref.pre_low_ref = f32[4,4,1024]{2,1,0:T(4,128)S(1)} collective-permute-done((f32[4,4,1024]{2,1,0:T(4,128)S(1)}, f32[4,4,1024]{2,1,0:T(4,128)S(1)}, u32[]{:S(2)}, u32[]{:S(2)}) %collective-permute-start.3) | collective-permute-done | bytes 65568 | tf_op jit(solution)/shard_map/ppermute | solution.py:25
  101.2 5.9 %shard_map.77 = bf16[4,2,528,256]{3,2,1,0:T(8,128)(2,1)S(1)} custom-call(s32[2]{0:T(128)S(1)} %add_convert_fusion.2.valid_ref, f32[520,1024]{1,0:T(8,128)S(1)} %fusion.14.part_ref, f32[4,4,1024]{2,1,0:T(4,128)S(1)} %collective-permute-done.3.low_in_ref.pre_low_ref, f32[4,4,1024]{2,1,0:T(4,128)S(1)} %collective-permute-done.4.high_in_ref.pre_high_ref, ...), custom_call_target="tpu_custom_call" | custom-call | flops 3321888768 | bytes 12582912 | tf_op jit(solution)/shard_map/pallas_call | solution.py:201
  107.0 1.4 copy-done
  108.4 4.4 %all-to-all-start.1 = ((bf16[4,1056,256]{2,1,0:T(8,128)(2,1)}), bf16[4,1056,256]{2,1,0:T(8,128)(2,1)S(1)}, u32[]{:S(2)}, u32[]{:S(2)}) async-start(bf16[4,1056,256]{2,1,0:T(8,128)(2,1)} %bitcast.77), calls=%async_computation.1 | async-start | bytes 4325376 | tf_op jit(solution)/shard_map/all_to_all | solution.py:34
  112.9 31.5 %all-to-all-done.1 = bf16[4,1056,256]{2,1,0:T(8,128)(2,1)S(1)} async-done(((bf16[4,1056,256]{2,1,0:T(8,128)(2,1)}), bf16[4,1056,256]{2,1,0:T(8,128)(2,1)S(1)}, u32[]{:S(2)}, u32[]{:S(2)}) %all-to-all-start.1) | async-done | bytes 2162720 | tf_op jit(solution)/shard_map/all_to_all | solution.py:34
  144.4 1.6 copy-done.5
  149.1 4.2 %shard_map.78 = (f32[32,16,768]{2,1,0:T(8,128)S(1)}, bf16[32,16,768]{2,1,0:T(8,128)(2,1)S(1)}) custom-call(s32[5]{0:T(128)S(1)} %stack.47.refs_0_, bf16[4,2,528,256]{3,2,1,0:T(8,128)(2,1)S(1)} %bitcast.75, bf16[1024,1024]{1,0:T(8,128)(2,1)S(1)} %copy-done.5, bf16[256,1024]{1,0:T(8,128)(2,1)S(1)} %bitcast.82, bf16[256,1024]{1,0:T(8,128)(2,1)S(1)} %copy-done.7, ...), custom_call_target="tpu_custom_call" | custom-call | flops 3221225472 | bytes 10485760 | tf_op jit(solution)/shard_map/pallas_call | solution.py:281
  154.5 2.2 copy-done.4
  156.7 4.0 %shard_map.79 = (f32[32,16,768]{2,1,0:T(8,128)S(1)}, bf16[32,16,768]{2,1,0:T(8,128)(2,1)S(1)}) custom-call(s32[5]{0:T(128)S(1)} %stack.47.refs_0_, bf16[4,2,528,256]{3,2,1,0:T(8,128)(2,1)S(1)} %bitcast.76, bf16[2048,1024]{1,0:T(8,128)(2,1)S(1)} %copy-done.4), custom_call_target="tpu_custom_call" | custom-call | flops 3221225472 | bytes 10485760 | tf_op jit(solution)/shard_map/pallas_call | solution.py:281
  161.4 1.3 add_convert_fusion.1
  163.7 24.4 %all_to_all.20 = bf16[4,256,768]{2,1,0:T(8,128)(2,1)S(1)} all-to-all(bf16[4,256,768]{2,1,0:T(8,128)(2,1)S(1)} %bitcast.86), channel_id=1, replica_groups=mesh['video'=4,'x'=4,'z'=8,'core'=2] {'x'}, dimensions={0} | all-to-all | bytes 3145728 | tf_op jit(solution)/shard_map/all_to_all | solution.py:34
  188.5 20.9 %all_to_all.21 = bf16[8,2,16,768]{3,2,1,0:T(8,128)(2,1)S(1)} all-to-all(bf16[8,2,16,768]{3,2,1,0:T(8,128)(2,1)S(1)} %copy.80), channel_id=1, replica_groups=mesh['video'=4,'x'=4,'z'=8,'core'=2] {'z'}, dimensions={0} | all-to-all | bytes 786432 | tf_op jit(solution)/shard_map/all_to_all | solution.py:34
  209.5 1.9 collective-permute-start.7
  211.3 1.5 collective-permute-start.8
  212.8 1.7 collective-permute-done.7
  214.6 2.9 %collective-permute-done.8 = f32[2,16,768]{2,1,0:T(8,128)S(1)} collective-permute-done((f32[2,16,768]{2,1,0:T(8,128)S(1)}, f32[2,16,768]{2,1,0:T(8,128)S(1)}, u32[]{:S(2)}, u32[]{:S(2)}) %collective-permute-start.8) | collective-permute-done | bytes 98336 | tf_op jit(solution)/shard_map/ppermute | solution.py:30
  217.5 1.2 collective-permute-done.9
  (101 shorter events, 13.7 us)
Async XLA Ops:
  7.2 2.3 copy-start.14
  7.2 2.9 %copy-start.13 = (f32[4,4,16,2]{2,3,1,0:T(2,128)S(1)}, f32[4,4,16,2]{2,3,1,0:T(2,128)}, u32[]{:S(2)}) copy-start(f32[4,4,16,2]{2,3,1,0:T(2,128)} %param.7) | copy-start | bytes 6148
  7.2 3.4 %copy-start.12 = (bf16[4,4,16,1024]{3,2,1,0:T(8,128)(2,1)S(1)}, bf16[4,4,16,1024]{3,2,1,0:T(8,128)(2,1)}, u32[]{:S(2)}) copy-start(bf16[4,4,16,1024]{3,2,1,0:T(8,128)(2,1)} %param.6) | copy-start | bytes 1572868
  7.2 105.7 %all-gather.3.cloned.1.call-start = ((), (), s32[]{:S(2)}) async-start(), calls=%async_computation.4 | async-start | bytes 2621440 | tf_op jit(solution)/shard_map/all_gather | solution.py:319
  12.9 12.4 %copy-start.3 = (bf16[4,128,1024]{2,1,0:T(8,128)(2,1)S(1)}, bf16[4,128,1024]{2,1,0:T(8,128)(2,1)}, u32[]{:S(2)}) copy-start(bf16[4,128,1024]{2,1,0:T(8,128)(2,1)} %param.10) | copy-start | bytes 3145732
  12.9 67.5 %all-to-all-start = ((bf16[64,16,1152]{2,1,0:T(8,128)(2,1)}), bf16[64,16,1152]{2,1,0:T(8,128)(2,1)}, u32[]{:S(2)}, u32[]{:S(2)}) async-start(bf16[64,16,1152]{2,1,0:T(8,128)(2,1)} %bitcast.85), calls=%async_computation | async-start | bytes 4718592 | tf_op jit(solution)/shard_map/all_to_all | solution.py:34
  25.2 129.3 %all-gather.5.cloned.1.call-start = ((), (), s32[]{:S(2)}) async-start(), calls=%async_computation.5 | async-start | bytes 5242880 | tf_op jit(solution)/shard_map/all_gather | solution.py:317
  26.9 27.0 %collective-permute-start = (bf16[256,1024]{1,0:T(8,128)(2,1)S(1)}, bf16[256,1024]{1,0:T(8,128)(2,1)S(1)}, u32[]{:S(2)}, u32[]{:S(2)}) collective-permute-start(bf16[256,1024]{1,0:T(8,128)(2,1)S(1)} %bitcast.79), channel_id=1, source_target_pairs={{0,64},{64,128},{128,192},{192,0},{1,65},{65,129},{129,193},{193,1... | collective-permute-start | bytes 1572872 | tf_op jit(solution)/shard_map/ppermute | solution.py:30
  28.6 40.0 %collective-permute-start.1 = (bf16[256,1024]{1,0:T(8,128)(2,1)S(1)}, bf16[256,1024]{1,0:T(8,128)(2,1)S(1)}, u32[]{:S(2)}, u32[]{:S(2)}) collective-permute-start(bf16[256,1024]{1,0:T(8,128)(2,1)S(1)} %bitcast.80), channel_id=1, source_target_pairs={{0,128},{64,192},{128,0},{192,64},{1,129},{65,193},{129,1},{193,65... | collective-permute-start | bytes 1572872 | tf_op jit(solution)/shard_map/ppermute | solution.py:30
  31.5 39.1 %collective-permute-start.2 = (bf16[256,1024]{1,0:T(8,128)(2,1)S(1)}, bf16[256,1024]{1,0:T(8,128)(2,1)S(1)}, u32[]{:S(2)}, u32[]{:S(2)}) collective-permute-start(bf16[256,1024]{1,0:T(8,128)(2,1)S(1)} %bitcast.81), channel_id=1, source_target_pairs={{0,192},{64,0},{128,64},{192,128},{1,193},{65,1},{129,65},{193,129... | collective-permute-start | bytes 1572872 | tf_op jit(solution)/shard_map/ppermute | solution.py:30
  53.9 29.5 %copy-start.6 = (bf16[256,1024]{1,0:T(8,128)(2,1)}, bf16[256,1024]{1,0:T(8,128)(2,1)S(1)}, u32[]{:S(2)}) copy-start(bf16[256,1024]{1,0:T(8,128)(2,1)S(1)} %collective-permute-done.refs_4_) | copy-start | bytes 1572868
  68.6 14.8 %copy-start.8 = (bf16[256,1024]{1,0:T(8,128)(2,1)}, bf16[256,1024]{1,0:T(8,128)(2,1)S(1)}, u32[]{:S(2)}) copy-start(bf16[256,1024]{1,0:T(8,128)(2,1)S(1)} %collective-permute-done.1.refs_5_) | copy-start | bytes 1572868
  70.5 12.9 %copy-start.10 = (bf16[256,1024]{1,0:T(8,128)(2,1)}, bf16[256,1024]{1,0:T(8,128)(2,1)S(1)}, u32[]{:S(2)}) copy-start(bf16[256,1024]{1,0:T(8,128)(2,1)S(1)} %collective-permute-done.2.refs_6_) | copy-start | bytes 1572868
  83.4 17.7 %slice-start = ((s8[6291456]{0:T(1024)(128)(4,1)}), s8[4194304]{0:T(1024)(128)(4,1)S(1)}, s32[]{:S(2)}) async-start(s8[6291456]{0:T(1024)(128)(4,1)} %bitcast.83), calls=%async_computation.6 | async-start | bytes 8388608
  86.7 14.5 %slice-start.1 = ((s8[6291456]{0:T(1024)(128)(4,1)}), s8[2097152]{0:T(1024)(128)(4,1)S(1)}, s32[]{:S(2)}) async-start(s8[6291456]{0:T(1024)(128)(4,1)} %bitcast.83), calls=%async_computation.7 | async-start | bytes 4194304
  90.1 5.5 %collective-permute-start.4 = (f32[4,4,1024]{2,1,0:T(4,128)S(1)}, f32[4,4,1024]{2,1,0:T(4,128)S(1)}, u32[]{:S(2)}, u32[]{:S(2)}) collective-permute-start(f32[4,4,1024]{2,1,0:T(4,128)S(1)} %pad_maximum_fusion.2), channel_id=1, source_target_pairs={{1,0},{2,1},{3,2},{4,3},{5,4},{6,5},{7,6},{8,7},{9,8},{10,9},{11,1... | collective-permute-start | bytes 196616 | tf_op jit(solution)/shard_map/ppermute | solution.py:25
  93.5 7.7 %collective-permute-start.3 = (f32[4,4,1024]{2,1,0:T(4,128)S(1)}, f32[4,4,1024]{2,1,0:T(4,128)S(1)}, u32[]{:S(2)}, u32[]{:S(2)}) collective-permute-start(f32[4,4,1024]{2,1,0:T(4,128)S(1)} %pad_maximum_fusion.1), channel_id=1, source_target_pairs={{0,1},{1,2},{2,3},{3,4},{4,5},{5,6},{6,7},{7,8},{8,9},{9,10},{10,1... | collective-permute-start | bytes 196616 | tf_op jit(solution)/shard_map/ppermute | solution.py:25
  107.0 1.4 copy-start
  108.4 36.0 %all-to-all-start.1 = ((bf16[4,1056,256]{2,1,0:T(8,128)(2,1)}), bf16[4,1056,256]{2,1,0:T(8,128)(2,1)S(1)}, u32[]{:S(2)}, u32[]{:S(2)}) async-start(bf16[4,1056,256]{2,1,0:T(8,128)(2,1)} %bitcast.77), calls=%async_computation.1 | async-start | bytes 4325376 | tf_op jit(solution)/shard_map/all_to_all | solution.py:34
  144.4 1.6 copy-start.5
  146.0 1.0 copy-start.7
  147.0 1.0 copy-start.9
  148.1 1.0 copy-start.11
  153.4 1.2 copy-start.1
  154.5 6.8 %collective-permute-start.5 = (bf16[32,16,768]{2,1,0:T(8,128)(2,1)S(1)}, bf16[32,16,768]{2,1,0:T(8,128)(2,1)}, u32[]{:S(2)}, u32[]{:S(2)}) collective-permute-start(bf16[32,16,768]{2,1,0:T(8,128)(2,1)S(1)} %get-tuple-element.7), channel_id=1, source_target_pairs={{0,1},{1,0},{2,3},{3,2},{4,5},{5,4},{6,7},{7,6},{8,9},{9,8},{10,11... | collective-permute-start | bytes 2359304 | tf_op jit(solution)/shard_map/ppermute | solution.py:30
  154.5 2.2 copy-start.4
  156.7 4.6 %copy-start.2 = (f32[32,16,768]{2,1,0:T(8,128)S(1)}, f32[32,16,768]{2,1,0:T(8,128)}, u32[]{:S(2)}) copy-start(f32[32,16,768]{2,1,0:T(8,128)} %copy-done.1) | copy-start | bytes 4718596
  160.8 2.5 %collective-permute-start.6 = (bf16[32,16,768]{2,1,0:T(8,128)(2,1)S(1)}, bf16[32,16,768]{2,1,0:T(8,128)(2,1)S(1)}, u32[]{:S(2)}, u32[]{:S(2)}) collective-permute-start(bf16[32,16,768]{2,1,0:T(8,128)(2,1)S(1)} %get-tuple-element.9), channel_id=1, source_target_pairs={{0,1},{1,0},{2,3},{3,2},{4,5},{5,4},{6,7},{7,6},{8,9},{9,8},{10,11... | collective-permute-start | bytes 2359304 | tf_op jit(solution)/shard_map/ppermute | solution.py:30
  209.5 5.1 %collective-permute-start.7 = (f32[2,16,768]{2,1,0:T(8,128)S(1)}, f32[2,16,768]{2,1,0:T(8,128)S(1)}, u32[]{:S(2)}, u32[]{:S(2)}) collective-permute-start(f32[2,16,768]{2,1,0:T(8,128)S(1)} %convert_reduce_fusion), channel_id=1, source_target_pairs={{0,192},{64,0},{128,64},{192,128},{1,193},{65,1},{129,65},{193,129... | collective-permute-start | bytes 294920 | tf_op jit(solution)/shard_map/ppermute | solution.py:30
  211.3 6.1 %collective-permute-start.8 = (f32[2,16,768]{2,1,0:T(8,128)S(1)}, f32[2,16,768]{2,1,0:T(8,128)S(1)}, u32[]{:S(2)}, u32[]{:S(2)}) collective-permute-start(f32[2,16,768]{2,1,0:T(8,128)S(1)} %convert_reduce_fusion), channel_id=1, source_target_pairs={{0,128},{64,192},{128,0},{192,64},{1,129},{65,193},{129,1},{193,65... | collective-permute-start | bytes 294920 | tf_op jit(solution)/shard_map/ppermute | solution.py:30
  212.8 5.8 %collective-permute-start.9 = (f32[2,16,768]{2,1,0:T(8,128)S(1)}, f32[2,16,768]{2,1,0:T(8,128)S(1)}, u32[]{:S(2)}, u32[]{:S(2)}) collective-permute-start(f32[2,16,768]{2,1,0:T(8,128)S(1)} %convert_reduce_fusion), channel_id=1, source_target_pairs={{0,64},{64,128},{128,192},{192,0},{1,65},{65,129},{129,193},{193,1... | collective-permute-start | bytes 294920 | tf_op jit(solution)/shard_map/ppermute | solution.py:30
Sparse Core Ops, SparseCore 0:
  9.8 55.5 all-gather.2
  67.2 59.9 all-gather.4

commit v5 on v4

--- a/solution.py
+++ b/solution.py
@@ -28,6 +28,17 @@
 def ring_shift(value, axis, shift):
     count = lax.axis_size(axis)
     return lax.ppermute(value, axis, [(i, (i + shift) % count) for i in range(count)])
+
+
+def around_video(rows):
+    count = lax.axis_size("video")
+    half = rows.shape[0] // 2
+    if count != 4:
+        held = [rows] + [ring_shift(rows, "video", shift) for shift in range(1, count)]
+        return [piece for part in held for piece in (part[:half], part[half:])]
+    below, above = ring_shift(rows, "video", 1), ring_shift(rows, "video", 3)
+    far = [ring_shift(below[:half], "video", 1), ring_shift(above[half:], "video", 3)]
+    return [rows, below] + far + [above]
 
 
 def exchange(value, axis):
@@ -228,48 +239,41 @@
     sources, width = grad_ref.shape[0], grad_ref.shape[3]
     main = grad_ref.shape[2] - 16
     rows = main // videos
-    groups, each, outs = keep_ref.shape
+    _, each, outs = keep_ref.shape
     core = order_ref[0]
-    row = lax.broadcasted_iota(jnp.int32, (rows, width), 0)
-    for source in range(sources):
-        edges = grad_ref[source, layer, main:, :].astype(jnp.float32)
-        for video in range(videos):
-            span = slice(video * rows, (video + 1) * rows)
-            grad = grad_ref[source, layer, span, :].astype(jnp.float32)
-            low, high = edges[video : video + 1], edges[videos + video : videos + video + 1]
-            after = jnp.where(row == rows - 1, high, pltpu.roll(grad, rows - 1, 0))
-            before = jnp.where(row == 0, low, pltpu.roll(grad, 1, 0))
-            for index, part in enumerate((after, grad, before)):
-                lag_ref[
-                    source * main + video * rows : source * main + (video + 1) * rows,
-                    index * width : (index + 1) * width,
-                ] = part.astype(jnp.bfloat16)
-    pieces = []
-    gathered = input_refs[0].shape[0] // sources
-    if gathered == main:
-        pieces.append((input_refs[0], 0, sources * main, 0))
-    else:
+
+    @pl.when(pl.program_id(0) == 0)
+    def _():
+        row = lax.broadcasted_iota(jnp.int32, (rows, width), 0)
         for source in range(sources):
-            pieces.append((input_refs[0], source * gathered, gathered, source * main))
-        for index, ref in enumerate(input_refs[1:]):
-            at = pl.multiple_of(order_ref[1 + index] * main + gathered, gathered)
-            pieces.append((ref, 0, main - gathered, at))
-    channels = groups * 2 * each
-    step = min(256, channels)
-    for start in range(0, channels, step):
-        total = jnp.zeros((step, outs), jnp.float32)
-        for ref, first, count, at in pieces:
-            total = total + lax.dot_general(
-                ref[first : first + count, start : start + step],
-                lag_ref[pl.ds(at, count), :],
-                (((0,), (0,)), ((), ())),
-                preferred_element_type=jnp.float32,
-            )
-        total = total.reshape(step // (2 * each), 2, each, outs)
-        first, second = total[:, 0], total[:, 1]
-        span = slice(start // (2 * each), (start + step) // (2 * each))
-        keep_ref[span] = jnp.where(core == 0, first, second)
-        give_ref[span] = jnp.where(core == 0, second, first).astype(jnp.bfloat16)
+            at = order_ref[1 + source]
+            edges = grad_ref[at, layer, main:, :].astype(jnp.float32)
+            for video in range(videos):
+                span = slice(video * rows, (video + 1) * rows)
+                grad = grad_ref[at, layer, span, :].astype(jnp.float32)
+                low, high = edges[video : video + 1], edges[videos + video : videos + video + 1]
+                after = jnp.where(row == rows - 1, high, pltpu.roll(grad, rows - 1, 0))
+                before = jnp.where(row == 0, low, pltpu.roll(grad, 1, 0))
+                for index, part in enumerate((after, grad, before)):
+                    lag_ref[
+                        source * main + video * rows : source * main + (video + 1) * rows,
+                        index * width : (index + 1) * width,
+                    ] = part.astype(jnp.bfloat16)
+
+    total = jnp.zeros((input_refs[0].shape[1], outs), jnp.float32)
+    offset = 0
+    for ref in input_refs:
+        total = total + lax.dot_general(
+            ref[...],
+            lag_ref[offset : offset + ref.shape[0], :],
+            (((0,), (0,)), ((), ())),
+            preferred_element_type=jnp.float32,
+        )
+        offset += ref.shape[0]
+    total = total.reshape(-1, 2, each, outs)
+    first, second = total[:, 0], total[:, 1]
+    keep_ref[...] = jnp.where(core == 0, first, second)
+    give_ref[...] = jnp.where(core == 0, second, first).astype(jnp.bfloat16)
 
 
 def filter_terms(inputs, gradients, layer, order, videos, lag_count, each):
@@ -277,15 +281,21 @@
     channels = inputs[0].shape[-1]
     shape = (channels // (2 * each), each, lag_count * width)
     rows = sources * (block - 16)
-    vmem = pl.BlockSpec(memory_space=pltpu.VMEM)
+    step = min(256, channels)
+    out_spec = pl.BlockSpec((step // (2 * each),) + shape[1:], lambda i: (i, 0, 0))
     return pl.pallas_call(
         lambda *refs: terms_kernel(videos, layer, *refs),
+        grid=(channels // step,),
         out_shape=(
             jax.ShapeDtypeStruct(shape, jnp.float32),
             jax.ShapeDtypeStruct(shape, jnp.bfloat16),
         ),
-        in_specs=[pl.BlockSpec(memory_space=pltpu.SMEM)] + [vmem] * (1 + len(inputs)),
-        out_specs=(vmem, vmem),
+        in_specs=[
+            pl.BlockSpec(memory_space=pltpu.SMEM),
+            pl.BlockSpec(gradients.shape, lambda i: (0, 0, 0, 0)),
+        ]
+        + [pl.BlockSpec((piece.shape[0], step), lambda i: (0, i)) for piece in inputs],
+        out_specs=(out_spec, out_spec),
         scratch_shapes=[pltpu.VMEM((rows, lag_count * width), jnp.bfloat16)],
         compiler_params=pltpu.CompilerParams(vmem_limit_bytes=24 * 2**20),
         cost_estimate=pl.CostEstimate(
@@ -315,16 +325,13 @@
     pre_values = preact.astype(jnp.float32).reshape(main_rows, channels)
     activation = jax.nn.silu(pre_values).astype(jnp.bfloat16)
     act_all = lax.all_gather(activation, "video", axis=0, tiled=True)
-    halves = features.reshape(2, main_rows // 2, channels)
-    feature_all = [lax.all_gather(halves[0], "video", axis=0, tiled=True), halves[1]]
-    for shift in range(1, quarters):
-        feature_all.append(ring_shift(halves[1], "video", shift))
+    feature_all = around_video(features.reshape(main_rows, channels))
 
     partial = collect(got, channels, main_rows + 2 * video_count)
     ends = partial[:main_rows].reshape(video_count, snip_count, channels)
     low = partial[main_rows : main_rows + video_count]
     high = partial[main_rows + video_count :]
-    arrived = sum(piece[0, 0] * 0 for piece in feature_all[2:]).astype(jnp.float32)
+    arrived = sum(piece[0, 0] * 0 for piece in feature_all[1:]).astype(jnp.float32)
     pre_ends = pre_values.reshape(ends.shape)[:, :: snip_count - 1] + arrived
     from_low = neighbours(jnp.stack([ends[:, -2], ends[:, -1], high, pre_ends[:, 1]]), True)
     from_high = neighbours(jnp.stack([low, ends[:, 0], ends[:, 1], pre_ends[:, 0]]), False)
@@ -336,12 +343,13 @@
     shares = exchange(shares.reshape(quarters, 2 * block, width), "video")
     shares = shares.reshape(quarters, 2, block, width)
 
-    order = jnp.stack([core] + [(place + quarters - source) % quarters for source in range(quarters)])
+    in_order = jnp.stack([core] + [jnp.int32(source) for source in range(quarters)])
+    around = jnp.stack([core] + [(place + quarters - source) % quarters for source in range(quarters)])
     second = share_by_core(
-        *filter_terms([act_all], shares, 0, order, video_count, lag_count, each)
+        *filter_terms([act_all], shares, 0, in_order, video_count, lag_count, each)
     )
     first = share_by_core(
-        *filter_terms(feature_all, shares, 1, order, video_count, lag_count, each)
+        *filter_terms(feature_all, shares, 1, around, video_count, lag_count, each)
     )
     x_total, z_total = lax.axis_size("x"), lax.axis_size("z")
     both = jnp.stack([part.reshape(x_total, -1, lag_count * width) for part in (first, second)], 1)

time: 228 us -> 228 us (level)
  Pallas kernels: 14.1 us -> 18 us
  waiting for transfers between devices: 87.3 us -> 84.6 us
    all_to_all x2, waiting for transfers between devices: 40.2 us -> 24.3 us  [exchange(): return lax.all_to_all(value, axis, split_axis=0, concat_axis=0, tiled=True)]
    ppermute x8 -> x9, waiting for transfers between devices: 41.5 us -> 55.3 us  [ring_shift(): lax.ppermute(value, axis, [(i, (i + shift) % count) for i in range(count)])]
    pallas_call x2, Pallas kernels: 8.25 us -> 12.1 us  [filter_terms(): pl.pallas_call(lambda *refs: terms_kernel(videos, layer, *refs), grid=(ch...]
    unnamed x44 -> x28, local copies, waits for them, and re-layouts: 11.2 us -> 8.43 us
    ppermute x8 -> x9, starting transfers between devices: 9.87 us -> 11.6 us  [ring_shift(): lax.ppermute(value, axis, [(i, (i + shift) % count) for i in range(count)])]
  transfers between devices with their start and end apart: 14 -> 14, of which waited for: 9 -> 7; matrix products, arithmetic and copies ran while one was open for 8% -> 7% of each run, Pallas kernels for 6% -> 8%
where the time goes in v5:
time: 228 us
  waiting for transfers between devices  84.6 us (37%)
  blocking collectives  44 us (19%)
  starting transfers between devices  32.1 us (14%)
  Pallas kernels  18 us (8%)
  between operations  17 us (7%)
  local copies, waits for them, and re-layouts  15.5 us (7%)
  matrix products  9.65 us (4%)
  other arithmetic  6.66 us (3%)
    ppermute x9, waiting for transfers between devices, ring_shift(): lax.ppermute(value, axis, [(i, (i + shift) % count) for i in range(count)])  55.3 us
    all_to_all x2, blocking collectives, exchange(): return lax.all_to_all(value, axis, split_axis=0, concat_axis=0, tiled=True)  44 us
    all_to_all x2, waiting for transfers between devices, exchange(): return lax.all_to_all(value, axis, split_axis=0, concat_axis=0, tiled=True)  24.3 us
    all_to_all x2, starting transfers between devices, exchange(): return lax.all_to_all(value, axis, split_axis=0, concat_axis=0, tiled=True)  16 us
    pallas_call x2, Pallas kernels, filter_terms(): pl.pallas_call(lambda *refs: terms_kernel(videos, layer, *refs), grid=(ch...  12.1 us
    ppermute x9, starting transfers between devices, ring_shift(): lax.ppermute(value, axis, [(i, (i + shift) % count) for i in range(count)])  11.6 us
    unnamed x28, local copies, waits for them, and re-layouts  8.43 us
    dot_general x2, matrix products, collect(): total = total + jnp.dot(table, tap_rows, preferred_element_type=jnp.float32)  6.27 us
  transfers between devices with their start and end apart: 14, of which 7 were waited for; matrix products, arithmetic and copies ran while one was open for 7% of the time, Pallas kernels for 8%

profile of v5, /device:TPU:2, one launch (start us, length us, event | category | flops | bytes accessed | tf_op | source)
XLA Modules:
  0.0 227.6 jit_solution(3065357686996556445)
XLA Ops:
  9.7 3.4 %convolution_convert_fusion = bf16[1024,1152]{1,0:T(8,128)(2,1)} fusion(bf16[256,128]{1,0:T(8,128)(2,1)S(1)} %select_convert_fusion, bf16[256,1024]{1,0:T(8,128)(2,1)} %bitcast.85, s32[256]{0:T(256)S(1)} %get-tuple-element.54), kind=kOutput, calls=%fused_computation.4 | convolution fusion | flops 606601216 | bytes 2950144 | tf_op jit(solution)/shard_map/dot_general | solution.py:114
  13.1 12.3 %all-to-all-start = ((bf16[64,16,1152]{2,1,0:T(8,128)(2,1)}), bf16[64,16,1152]{2,1,0:T(8,128)(2,1)}, u32[]{:S(2)}, u32[]{:S(2)}) async-start(bf16[64,16,1152]{2,1,0:T(8,128)(2,1)} %bitcast.14), calls=%async_computation | async-start | bytes 4718592 | tf_op jit(solution)/shard_map/all_to_all | solution.py:45
  25.5 1.7 collective-permute-start
  27.1 1.7 collective-permute-start.2
  28.8 1.6 fusion.11
  30.4 27.3 %collective-permute-done.refs_3_ = bf16[512,1024]{1,0:T(8,128)(2,1)S(1)} collective-permute-done((bf16[512,1024]{1,0:T(8,128)(2,1)}, bf16[512,1024]{1,0:T(8,128)(2,1)S(1)}, u32[]{:S(2)}, u32[]{:S(2)}) %collective-permute-start) | collective-permute-done | bytes 1048608 | tf_op jit(solution)/shard_map/ppermute | solution.py:30
  58.6 1.4 collective-permute-start.1
  60.9 2.9 %collective-permute-start.3 = (bf16[256,1024]{1,0:T(8,128)(2,1)}, bf16[256,1024]{1,0:T(8,128)(2,1)}, u32[]{:S(2)}, u32[]{:S(2)}) collective-permute-start(bf16[256,1024]{1,0:T(8,128)(2,1)} %slice.158), channel_id=1, source_target_pairs={{0,192},{64,0},{128,64},{192,128},{1,193},{65,1},{129,65},{193,129... | collective-permute-start | bytes 1572872 | tf_op jit(solution)/shard_map/ppermute | solution.py:30
  65.1 20.1 %collective-permute-done.1.refs_4_ = bf16[256,1024]{1,0:T(8,128)(2,1)} collective-permute-done((bf16[256,1024]{1,0:T(8,128)(2,1)}, bf16[256,1024]{1,0:T(8,128)(2,1)}, u32[]{:S(2)}, u32[]{:S(2)}) %collective-permute-start.1) | collective-permute-done | bytes 524320 | tf_op jit(solution)/shard_map/ppermute | solution.py:30
  85.2 1.2 slice.157
  87.7 1.1 slice.159
  92.0 1.2 fusion.22
  93.2 3.1 %fusion.2 = f32[520,1024]{1,0:T(8,128)S(1)} fusion(f32[1024]{0:T(1024)S(1)} %get-tuple-element.25, bf16[1024,1152]{1,0:T(8,128)(2,1)} %bitcast.15, s32[1024]{0:T(1024)S(1)} %get-tuple-element.23), kind=kOutput, calls=%fused_computation.7 | convolution fusion | flops 1094197248 | bytes 4235264 | tf_op jit(solution)/shard_map/dot_general | solution.py:132
  96.3 3.2 %fusion.14.part_ref = f32[520,1024]{1,0:T(8,128)S(1)} fusion(f32[520,1024]{1,0:T(8,128)S(1)} %fusion.2, f32[1024]{0:T(1024)S(1)} %get-tuple-element.24, bf16[1024,1152]{1,0:T(8,128)(2,1)} %bitcast.15, s32[1024]{0:T(1024)S(1)} %get-tuple-element.22), kind=kOutput, calls=%fused_computation.22 | convolution fusion | flops 1094729728 | bytes 6365184 | tf_op jit(solution)/shard_map/dot_general | solution.py:132
  99.8 1.9 collective-permute-start.5
  101.8 2.6 %collective-permute-start.4 = (f32[4,4,1024]{2,1,0:T(4,128)S(1)}, f32[4,4,1024]{2,1,0:T(4,128)S(1)}, u32[]{:S(2)}, u32[]{:S(2)}) collective-permute-start(f32[4,4,1024]{2,1,0:T(4,128)S(1)} %pad_maximum_fusion.1), channel_id=1, source_target_pairs={{0,1},{1,2},{2,3},{3,4},{4,5},{5,6},{6,7},{7,8},{8,9},{9,10},{10,1... | collective-permute-start | bytes 196616 | tf_op jit(solution)/shard_map/ppermute | solution.py:25
  104.5 5.0 %collective-permute-done.4.low_in_ref.pre_low_ref = f32[4,4,1024]{2,1,0:T(4,128)S(1)} collective-permute-done((f32[4,4,1024]{2,1,0:T(4,128)S(1)}, f32[4,4,1024]{2,1,0:T(4,128)S(1)}, u32[]{:S(2)}, u32[]{:S(2)}) %collective-permute-start.4) | collective-permute-done | bytes 65568 | tf_op jit(solution)/shard_map/ppermute | solution.py:25
  109.5 5.9 %shard_map.77 = bf16[4,2,528,256]{3,2,1,0:T(8,128)(2,1)S(1)} custom-call(s32[2]{0:T(128)S(1)} %add_convert_fusion.2.valid_ref, f32[520,1024]{1,0:T(8,128)S(1)} %fusion.14.part_ref, f32[4,4,1024]{2,1,0:T(4,128)S(1)} %collective-permute-done.4.low_in_ref.pre_low_ref, f32[4,4,1024]{2,1,0:T(4,128)S(1)} %collective-permute-done.5.high_in_ref.pre_high_ref, ...), custom_call_target="tpu_custom_call" | custom-call | flops 3321888768 | bytes 12582912 | tf_op jit(solution)/shard_map/pallas_call | solution.py:212
  115.4 1.4 copy-done
  116.8 3.7 %all-to-all-start.1 = ((bf16[4,1056,256]{2,1,0:T(8,128)(2,1)}), bf16[4,1056,256]{2,1,0:T(8,128)(2,1)S(1)}, u32[]{:S(2)}, u32[]{:S(2)}) async-start(bf16[4,1056,256]{2,1,0:T(8,128)(2,1)} %bitcast.76), calls=%async_computation.1 | async-start | bytes 4325376 | tf_op jit(solution)/shard_map/all_to_all | solution.py:45
  120.6 24.3 %all-to-all-done.1 = bf16[4,1056,256]{2,1,0:T(8,128)(2,1)S(1)} async-done(((bf16[4,1056,256]{2,1,0:T(8,128)(2,1)}), bf16[4,1056,256]{2,1,0:T(8,128)(2,1)S(1)}, u32[]{:S(2)}, u32[]{:S(2)}) %all-to-all-start.1) | async-done | bytes 2162720 | tf_op jit(solution)/shard_map/all_to_all | solution.py:45
  144.9 1.2 copy-done.5
  146.1 6.5 %shard_map.78 = (f32[32,16,768]{2,1,0:T(8,128)S(1)}, bf16[32,16,768]{2,1,0:T(8,128)(2,1)}) custom-call(s32[5]{0:T(128)S(1)} %stack.51.refs_0_, bf16[4,2,528,256]{3,2,1,0:T(8,128)(2,1)S(1)} %bitcast.74, bf16[512,1024]{1,0:T(8,128)(2,1)} %bitcast.21.refs_2_, bf16[512,1024]{1,0:T(8,128)(2,1)S(1)} %collective-permute-done.refs_3_, ...), custom_call_target="tpu_custom_call" | custom-call | flops 3221225472 | bytes 10485760 | tf_op jit(solution)/shard_map/pallas_call | solution.py:286
  152.6 1.2 copy-done.1
  153.9 2.2 copy-done.6
  156.1 5.6 %shard_map.79 = (f32[32,16,768]{2,1,0:T(8,128)S(1)}, bf16[32,16,768]{2,1,0:T(8,128)(2,1)S(1)}) custom-call(s32[5]{0:T(128)S(1)} %stack.59.refs_0_, bf16[4,2,528,256]{3,2,1,0:T(8,128)(2,1)S(1)} %bitcast.75, bf16[2048,1024]{1,0:T(8,128)(2,1)S(1)} %copy-done.6), custom_call_target="tpu_custom_call" | custom-call | flops 3221225472 | bytes 10485760 | tf_op jit(solution)/shard_map/pallas_call | solution.py:286
  162.5 1.7 collective-permute-done.7
  164.6 24.6 %all_to_all.20 = bf16[4,256,768]{2,1,0:T(8,128)(2,1)S(1)} all-to-all(bf16[4,256,768]{2,1,0:T(8,128)(2,1)S(1)} %bitcast.80), channel_id=1, replica_groups=mesh['video'=4,'x'=4,'z'=8,'core'=2] {'x'}, dimensions={0} | all-to-all | bytes 3145728 | tf_op jit(solution)/shard_map/all_to_all | solution.py:45
  189.6 19.4 %all_to_all.21 = bf16[8,2,16,768]{3,2,1,0:T(8,128)(2,1)S(1)} all-to-all(bf16[8,2,16,768]{3,2,1,0:T(8,128)(2,1)S(1)} %copy.80), channel_id=1, replica_groups=mesh['video'=4,'x'=4,'z'=8,'core'=2] {'z'}, dimensions={0} | all-to-all | bytes 786432 | tf_op jit(solution)/shard_map/all_to_all | solution.py:45
  209.8 2.7 %collective-permute-start.8 = (f32[2,16,768]{2,1,0:T(8,128)S(1)}, f32[2,16,768]{2,1,0:T(8,128)S(1)}, u32[]{:S(2)}, u32[]{:S(2)}) collective-permute-start(f32[2,16,768]{2,1,0:T(8,128)S(1)} %convert_reduce_fusion), channel_id=1, source_target_pairs={{0,192},{64,0},{128,64},{192,128},{1,193},{65,1},{129,65},{193,129... | collective-permute-start | bytes 294920 | tf_op jit(solution)/shard_map/ppermute | solution.py:30
  212.5 3.6 %collective-permute-done.10 = f32[2,16,768]{2,1,0:T(8,128)S(1)} collective-permute-done((f32[2,16,768]{2,1,0:T(8,128)S(1)}, f32[2,16,768]{2,1,0:T(8,128)S(1)}, u32[]{:S(2)}, u32[]{:S(2)}) %collective-permute-start.10) | collective-permute-done | bytes 98336 | tf_op jit(solution)/shard_map/ppermute | solution.py:30
  216.0 2.6 %collective-permute-done.9 = f32[2,16,768]{2,1,0:T(8,128)S(1)} collective-permute-done((f32[2,16,768]{2,1,0:T(8,128)S(1)}, f32[2,16,768]{2,1,0:T(8,128)S(1)}, u32[]{:S(2)}, u32[]{:S(2)}) %collective-permute-start.9) | collective-permute-done | bytes 98336 | tf_op jit(solution)/shard_map/ppermute | solution.py:30
  (87 shorter events, 12.4 us)
Async XLA Ops:
  13.1 15.7 %copy-start.3 = (bf16[4,128,1024]{2,1,0:T(8,128)(2,1)S(1)}, bf16[4,128,1024]{2,1,0:T(8,128)(2,1)}, u32[]{:S(2)}) copy-start(bf16[4,128,1024]{2,1,0:T(8,128)(2,1)} %param.10) | copy-start | bytes 3145732
  13.1 77.0 %all-to-all-start = ((bf16[64,16,1152]{2,1,0:T(8,128)(2,1)}), bf16[64,16,1152]{2,1,0:T(8,128)(2,1)}, u32[]{:S(2)}, u32[]{:S(2)}) async-start(bf16[64,16,1152]{2,1,0:T(8,128)(2,1)} %bitcast.14), calls=%async_computation | async-start | bytes 4718592 | tf_op jit(solution)/shard_map/all_to_all | solution.py:45
  25.4 128.4 %all-gather.2.cloned.1.call-start = ((), (), s32[]{:S(2)}) async-start(), calls=%async_computation.4 | async-start | bytes 5242880 | tf_op jit(solution)/shard_map/all_gather | solution.py:327
  25.5 32.3 %collective-permute-start = (bf16[512,1024]{1,0:T(8,128)(2,1)}, bf16[512,1024]{1,0:T(8,128)(2,1)S(1)}, u32[]{:S(2)}, u32[]{:S(2)}) collective-permute-start(bf16[512,1024]{1,0:T(8,128)(2,1)} %bitcast.21.refs_2_), channel_id=1, source_target_pairs={{0,64},{64,128},{128,192},{192,0},{1,65},{65,129},{129,193},{193,1... | collective-permute-start | bytes 3145736 | tf_op jit(solution)/shard_map/ppermute | solution.py:30
  27.1 32.9 %collective-permute-start.2 = (bf16[512,1024]{1,0:T(8,128)(2,1)}, bf16[512,1024]{1,0:T(8,128)(2,1)S(1)}, u32[]{:S(2)}, u32[]{:S(2)}) collective-permute-start(bf16[512,1024]{1,0:T(8,128)(2,1)} %bitcast.21.refs_2_), channel_id=1, source_target_pairs={{0,192},{64,0},{128,64},{192,128},{1,193},{65,1},{129,65},{193,129... | collective-permute-start | bytes 3145736 | tf_op jit(solution)/shard_map/ppermute | solution.py:30
  58.6 26.6 %collective-permute-start.1 = (bf16[256,1024]{1,0:T(8,128)(2,1)}, bf16[256,1024]{1,0:T(8,128)(2,1)}, u32[]{:S(2)}, u32[]{:S(2)}) collective-permute-start(bf16[256,1024]{1,0:T(8,128)(2,1)} %slice.156), channel_id=1, source_target_pairs={{0,64},{64,128},{128,192},{192,0},{1,65},{65,129},{129,193},{193,1... | collective-permute-start | bytes 1572872 | tf_op jit(solution)/shard_map/ppermute | solution.py:30
  60.0 31.9 %copy-start.4 = (bf16[512,1024]{1,0:T(8,128)(2,1)}, bf16[512,1024]{1,0:T(8,128)(2,1)S(1)}, u32[]{:S(2)}) copy-start(bf16[512,1024]{1,0:T(8,128)(2,1)S(1)} %collective-permute-done.2.refs_6_) | copy-start | bytes 3145732
  60.9 26.8 %collective-permute-start.3 = (bf16[256,1024]{1,0:T(8,128)(2,1)}, bf16[256,1024]{1,0:T(8,128)(2,1)}, u32[]{:S(2)}, u32[]{:S(2)}) collective-permute-start(bf16[256,1024]{1,0:T(8,128)(2,1)} %slice.158), channel_id=1, source_target_pairs={{0,192},{64,0},{128,64},{192,128},{1,193},{65,1},{129,65},{193,129... | collective-permute-start | bytes 1572872 | tf_op jit(solution)/shard_map/ppermute | solution.py:30
  93.1 16.4 %slice-start = ((s8[6291456]{0:T(1024)(128)(4,1)}), s8[4194304]{0:T(1024)(128)(4,1)S(1)}, s32[]{:S(2)}) async-start(s8[6291456]{0:T(1024)(128)(4,1)} %bitcast.78), calls=%async_computation.5 | async-start | bytes 8388608
  96.3 13.2 %slice-start.1 = ((s8[6291456]{0:T(1024)(128)(4,1)}), s8[2097152]{0:T(1024)(128)(4,1)S(1)}, s32[]{:S(2)}) async-start(s8[6291456]{0:T(1024)(128)(4,1)} %bitcast.78), calls=%async_computation.6 | async-start | bytes 4194304
  99.8 4.7 %collective-permute-start.5 = (f32[4,4,1024]{2,1,0:T(4,128)S(1)}, f32[4,4,1024]{2,1,0:T(4,128)S(1)}, u32[]{:S(2)}, u32[]{:S(2)}) collective-permute-start(f32[4,4,1024]{2,1,0:T(4,128)S(1)} %pad_maximum_fusion.2), channel_id=1, source_target_pairs={{1,0},{2,1},{3,2},{4,3},{5,4},{6,5},{7,6},{8,7},{9,8},{10,9},{11,1... | collective-permute-start | bytes 196616 | tf_op jit(solution)/shard_map/ppermute | solution.py:25
  101.8 7.7 %collective-permute-start.4 = (f32[4,4,1024]{2,1,0:T(4,128)S(1)}, f32[4,4,1024]{2,1,0:T(4,128)S(1)}, u32[]{:S(2)}, u32[]{:S(2)}) collective-permute-start(f32[4,4,1024]{2,1,0:T(4,128)S(1)} %pad_maximum_fusion.1), channel_id=1, source_target_pairs={{0,1},{1,2},{2,3},{3,4},{4,5},{5,6},{6,7},{7,8},{8,9},{9,10},{10,1... | collective-permute-start | bytes 196616 | tf_op jit(solution)/shard_map/ppermute | solution.py:25
  115.4 1.4 copy-start
  116.8 28.1 %all-to-all-start.1 = ((bf16[4,1056,256]{2,1,0:T(8,128)(2,1)}), bf16[4,1056,256]{2,1,0:T(8,128)(2,1)S(1)}, u32[]{:S(2)}, u32[]{:S(2)}) async-start(bf16[4,1056,256]{2,1,0:T(8,128)(2,1)} %bitcast.76), calls=%async_computation.1 | async-start | bytes 4325376 | tf_op jit(solution)/shard_map/all_to_all | solution.py:45
  144.9 1.2 copy-start.5
  152.6 1.2 copy-start.1
  153.8 8.5 %collective-permute-start.6 = (bf16[32,16,768]{2,1,0:T(8,128)(2,1)}, bf16[32,16,768]{2,1,0:T(8,128)(2,1)S(1)}, u32[]{:S(2)}, u32[]{:S(2)}) collective-permute-start(bf16[32,16,768]{2,1,0:T(8,128)(2,1)} %get-tuple-element.7), channel_id=1, source_target_pairs={{0,1},{1,0},{2,3},{3,2},{4,5},{5,4},{6,7},{7,6},{8,9},{9,8},{10,11... | collective-permute-start | bytes 2359304 | tf_op jit(solution)/shard_map/ppermute | solution.py:30
  153.9 2.2 copy-start.6
  156.1 6.2 %copy-start.2 = (f32[32,16,768]{2,1,0:T(8,128)S(1)}, f32[32,16,768]{2,1,0:T(8,128)}, u32[]{:S(2)}) copy-start(f32[32,16,768]{2,1,0:T(8,128)} %copy-done.1) | copy-start | bytes 4718596
  161.7 2.5 %collective-permute-start.7 = (bf16[32,16,768]{2,1,0:T(8,128)(2,1)S(1)}, bf16[32,16,768]{2,1,0:T(8,128)(2,1)S(1)}, u32[]{:S(2)}, u32[]{:S(2)}) collective-permute-start(bf16[32,16,768]{2,1,0:T(8,128)(2,1)S(1)} %get-tuple-element.9), channel_id=1, source_target_pairs={{0,1},{1,0},{2,3},{3,2},{4,5},{5,4},{6,7},{7,6},{8,9},{9,8},{10,11... | collective-permute-start | bytes 2359304 | tf_op jit(solution)/shard_map/ppermute | solution.py:30
  209.1 6.9 %collective-permute-start.10 = (f32[2,16,768]{2,1,0:T(8,128)S(1)}, f32[2,16,768]{2,1,0:T(8,128)S(1)}, u32[]{:S(2)}, u32[]{:S(2)}) collective-permute-start(f32[2,16,768]{2,1,0:T(8,128)S(1)} %convert_reduce_fusion), channel_id=1, source_target_pairs={{0,64},{64,128},{128,192},{192,0},{1,65},{65,129},{129,193},{193,1... | collective-permute-start | bytes 294920 | tf_op jit(solution)/shard_map/ppermute | solution.py:30
  209.8 6.2 %collective-permute-start.8 = (f32[2,16,768]{2,1,0:T(8,128)S(1)}, f32[2,16,768]{2,1,0:T(8,128)S(1)}, u32[]{:S(2)}, u32[]{:S(2)}) collective-permute-start(f32[2,16,768]{2,1,0:T(8,128)S(1)} %convert_reduce_fusion), channel_id=1, source_target_pairs={{0,192},{64,0},{128,64},{192,128},{1,193},{65,1},{129,65},{193,129... | collective-permute-start | bytes 294920 | tf_op jit(solution)/shard_map/ppermute | solution.py:30
  212.4 6.1 %collective-permute-start.9 = (f32[2,16,768]{2,1,0:T(8,128)S(1)}, f32[2,16,768]{2,1,0:T(8,128)S(1)}, u32[]{:S(2)}, u32[]{:S(2)}) collective-permute-start(f32[2,16,768]{2,1,0:T(8,128)S(1)} %convert_reduce_fusion), channel_id=1, source_target_pairs={{0,128},{64,192},{128,0},{192,64},{1,129},{65,193},{129,1},{193,65... | collective-permute-start | bytes 294920 | tf_op jit(solution)/shard_map/ppermute | solution.py:30
Sparse Core Ops, SparseCore 0:
  30.5 67.0 all-gather.1

commit v6 on v5

--- a/solution.py
+++ b/solution.py
@@ -115,22 +115,50 @@
     return rows.reshape(peers, capacity, channels + META)
 
 
+def collect_kernel(grad_ref, meta_ref, out_ref, table_ref):
+    meta = meta_ref[...].astype(jnp.float32)
+
+    @pl.when(pl.program_id(0) == 0)
+    def _():
+        across = meta.T
+        row = lax.broadcasted_iota(jnp.int32, table_ref.shape[1:], 0)
+        for step in range(2):
+            base = 5 * step
+            where_to = across[base : base + 1] * 256.0 + across[base + 1 : base + 2]
+            hit = row == where_to.astype(jnp.int32)
+            table_ref[step] = jnp.where(hit, 1.0, 0.0).astype(jnp.bfloat16)
+
+    grads = grad_ref[...].astype(jnp.float32)
+    total = jnp.zeros(out_ref.shape, jnp.float32)
+    for step in range(2):
+        base = 5 * step + 2
+        weight = meta[:, base : base + 1] + meta[:, base + 1 : base + 2] + meta[:, base + 2 : base + 3]
+        tap_rows = (weight * grads).astype(jnp.bfloat16)
+        total = total + jnp.dot(table_ref[step], tap_rows, preferred_element_type=jnp.float32)
+    out_ref[...] = total
+
+
 def collect(got, channels, row_count):
     rows = got.reshape(-1, channels + META)
-    grads = rows[:, :channels].astype(jnp.float32)
-    meta = rows[:, channels:].astype(jnp.float32)
-    meta_t = meta[:, :16].T
-    total = jnp.zeros((row_count, channels), jnp.float32)
-    for step in range(2):
-        base = 5 * step
-        where_to = (meta_t[base : base + 1] * 256.0 + meta_t[base + 1 : base + 2]).astype(jnp.int32)
-        weight = meta[:, base + 2 : base + 3] + meta[:, base + 3 : base + 4] + meta[:, base + 4 : base + 5]
-        tap_rows = (weight * grads).astype(jnp.bfloat16)
-        table = (
-            lax.broadcasted_iota(jnp.int32, (row_count, rows.shape[0]), 0) == where_to
-        ).astype(jnp.bfloat16)
-        total = total + jnp.dot(table, tap_rows, preferred_element_type=jnp.float32)
-    return total
+    slots = rows.shape[0]
+    step = min(256, channels)
+    return pl.pallas_call(
+        collect_kernel,
+        grid=(channels // step,),
+        out_shape=jax.ShapeDtypeStruct((row_count, channels), jnp.float32),
+        in_specs=[
+            pl.BlockSpec((slots, step), lambda q: (0, q)),
+            pl.BlockSpec((slots, META), lambda q: (0, channels // META)),
+        ],
+        out_specs=pl.BlockSpec((row_count, step), lambda q: (0, q)),
+        scratch_shapes=[pltpu.VMEM((2, row_count, slots), jnp.bfloat16)],
+        compiler_params=pltpu.CompilerParams(vmem_limit_bytes=20 * 2**20),
+        cost_estimate=pl.CostEstimate(
+            flops=4 * row_count * channels * slots,
+            bytes_accessed=5 * 2**20,
+            transcendentals=0,
+        ),
+    )(rows, rows)
 
 
 def grads_kernel(
@@ -147,7 +175,7 @@
 ):
     videos = low_in_ref.shape[1]
     width = share_ref.shape[3]
-    edges = part_ref.shape[0] - 2 * videos
+    edges = windows_ref.shape[1] - 16
     rows = edges // videos
     channels = part_ref.shape[1]
     quarter = pl.program_id(0)
@@ -319,19 +347,20 @@
     lag_count = filter_second.shape[0]
     main_rows = video_count * snip_count
     each = channels // peers
+    pre_values = preact.astype(jnp.float32).reshape(main_rows, channels)
+    activation = jax.nn.silu(pre_values).astype(jnp.bfloat16)
+    tap_weight = tap_weight + (activation[0, 0] * 0).astype(jnp.float32)
     sent = send_slots(bin_grad, tap_weight, tap_index, snip_count, peers)
     got = exchange(sent, TM)
 
-    pre_values = preact.astype(jnp.float32).reshape(main_rows, channels)
-    activation = jax.nn.silu(pre_values).astype(jnp.bfloat16)
     act_all = lax.all_gather(activation, "video", axis=0, tiled=True)
     feature_all = around_video(features.reshape(main_rows, channels))
 
-    partial = collect(got, channels, main_rows + 2 * video_count)
+    partial = collect(got, channels, main_rows + 16)
     ends = partial[:main_rows].reshape(video_count, snip_count, channels)
     low = partial[main_rows : main_rows + video_count]
-    high = partial[main_rows + video_count :]
-    arrived = sum(piece[0, 0] * 0 for piece in feature_all[1:]).astype(jnp.float32)
+    high = partial[main_rows + video_count : main_rows + 2 * video_count]
+    arrived = sum(piece[0, 0] * 0 for piece in feature_all[2:4]).astype(jnp.float32)
     pre_ends = pre_values.reshape(ends.shape)[:, :: snip_count - 1] + arrived
     from_low = neighbours(jnp.stack([ends[:, -2], ends[:, -1], high, pre_ends[:, 1]]), True)
     from_high = neighbours(jnp.stack([low, ends[:, 0], ends[:, 1], pre_ends[:, 0]]), False)

time: 228 us -> 234 us (1.026)
  matrix products: 9.65 us -> 2.32 us
  Pallas kernels: 18 us -> 24.1 us
  waiting for transfers between devices: 84.6 us -> 90.5 us
  local copies, waits for them, and re-layouts: 15.5 us -> 20.2 us
  other arithmetic: 6.66 us -> 4.01 us
    dot_general x2 -> x0, matrix products: 6.27 us -> none  [collect(): total = total + jnp.dot(table, tap_rows, preferred_element_type=jnp.float32)]
    pallas_call x0 -> x1, Pallas kernels: none -> 6.03 us  [collect(): pl.pallas_call(collect_kernel, grid=(channels // step,), out_shape=jax.Sh...]
    unnamed x28 -> x37, local copies, waits for them, and re-layouts: 8.43 us -> 13.7 us
    ppermute x9, waiting for transfers between devices: 55.3 us -> 60.5 us  [ring_shift(): lax.ppermute(value, axis, [(i, (i + shift) % count) for i in range(count)])]
  transfers between devices with their start and end apart: 14 -> 14, of which waited for: 7 -> 8; matrix products, arithmetic and copies ran while one was open for 7% -> 2% of each run, Pallas kernels for 8% -> 10%
where the time goes in v6:
time: 234 us; the launch traced here: 233 us
  waiting for transfers between devices  90.5 us (39%)
  blocking collectives  44 us (19%)
  starting transfers between devices  31.5 us (13%)
  Pallas kernels  24.1 us (10%)
  local copies, waits for them, and re-layouts  20.2 us (9%)
  between operations  16.4 us (7%)
  other arithmetic  4.01 us (2%)
    ppermute x9, waiting for transfers between devices, ring_shift(): lax.ppermute(value, axis, [(i, (i + shift) % count) for i in range(count)])  60.5 us
    all_to_all x2, blocking collectives, exchange(): return lax.all_to_all(value, axis, split_axis=0, concat_axis=0, tiled=True)  44 us
    all_to_all x2, waiting for transfers between devices, exchange(): return lax.all_to_all(value, axis, split_axis=0, concat_axis=0, tiled=True)  24.1 us
    all_to_all x2, starting transfers between devices, exchange(): return lax.all_to_all(value, axis, split_axis=0, concat_axis=0, tiled=True)  16.6 us
    unnamed x37, local copies, waits for them, and re-layouts  13.7 us
    pallas_call x2, Pallas kernels, filter_terms(): pl.pallas_call(lambda *refs: terms_kernel(videos, layer, *refs), grid=(ch...  12.2 us
    ppermute x9, starting transfers between devices, ring_shift(): lax.ppermute(value, axis, [(i, (i + shift) % count) for i in range(count)])  10.5 us
    pallas_call x1, Pallas kernels, collect(): pl.pallas_call(collect_kernel, grid=(channels // step,), out_shape=jax.Sh...  6.03 us
  transfers between devices with their start and end apart: 14, of which 8 were waited for; matrix products, arithmetic and copies ran while one was open for 2% of the time, Pallas kernels for 10%

profile of v6, /device:TPU:2, one launch (start us, length us, event | category | flops | bytes accessed | tf_op | source)
XLA Modules:
  0.0 233.1 jit_solution(16924663336906346507)
XLA Ops:
  8.6 1.8 fusion.3
  12.2 2.3 convolution_convert_fusion
  14.5 12.0 %all-to-all-start = ((bf16[64,16,1152]{2,1,0:T(8,128)(2,1)}), bf16[64,16,1152]{2,1,0:T(8,128)(2,1)S(1)}, u32[]{:S(2)}, u32[]{:S(2)}) async-start(bf16[64,16,1152]{2,1,0:T(8,128)(2,1)} %bitcast.85), calls=%async_computation | async-start | bytes 4718592 | tf_op jit(solution)/shard_map/all_to_all | solution.py:45
  27.3 1.6 collective-permute-start
  29.0 1.7 collective-permute-start.2
  30.6 30.9 %collective-permute-done.refs_3_ = bf16[512,1024]{1,0:T(8,128)(2,1)S(1)} collective-permute-done((bf16[512,1024]{1,0:T(8,128)(2,1)}, bf16[512,1024]{1,0:T(8,128)(2,1)S(1)}, u32[]{:S(2)}, u32[]{:S(2)}) %collective-permute-start) | collective-permute-done | bytes 1048608 | tf_op jit(solution)/shard_map/ppermute | solution.py:30
  63.4 1.4 collective-permute-start.1
  66.6 1.9 collective-permute-start.3
  68.6 21.3 %collective-permute-done.1.refs_4_ = bf16[256,1024]{1,0:T(8,128)(2,1)} collective-permute-done((bf16[256,1024]{1,0:T(8,128)(2,1)}, bf16[256,1024]{1,0:T(8,128)(2,1)}, u32[]{:S(2)}, u32[]{:S(2)}) %collective-permute-start.1) | collective-permute-done | bytes 524320 | tf_op jit(solution)/shard_map/ppermute | solution.py:30
  89.9 1.3 slice.88
  91.7 1.2 slice.90
  94.3 6.0 %shard_map.77.part_ref = f32[528,1024]{1,0:T(8,128)S(1)} custom-call(bf16[1024,1152]{1,0:T(8,128)(2,1)S(1)} %bitcast.76, bf16[1024,1152]{1,0:T(8,128)(2,1)S(1)} %bitcast.77), custom_call_target="tpu_custom_call" | custom-call | flops 2214592512 | bytes 5242880 | tf_op jit(solution)/shard_map/pallas_call | solution.py:145
  100.6 1.9 collective-permute-start.5
  102.6 2.4 %collective-permute-start.4 = (f32[4,4,1024]{2,1,0:T(4,128)S(1)}, f32[4,4,1024]{2,1,0:T(4,128)S(1)}, u32[]{:S(2)}, u32[]{:S(2)}) collective-permute-start(f32[4,4,1024]{2,1,0:T(4,128)S(1)} %pad_maximum_fusion.1), channel_id=1, source_target_pairs={{0,1},{1,2},{2,3},{3,4},{4,5},{5,6},{6,7},{7,8},{8,9},{9,10},{10,1... | collective-permute-start | bytes 196616 | tf_op jit(solution)/shard_map/ppermute | solution.py:25
  105.1 5.2 %collective-permute-done.4.low_in_ref.pre_low_ref = f32[4,4,1024]{2,1,0:T(4,128)S(1)} collective-permute-done((f32[4,4,1024]{2,1,0:T(4,128)S(1)}, f32[4,4,1024]{2,1,0:T(4,128)S(1)}, u32[]{:S(2)}, u32[]{:S(2)}) %collective-permute-start.4) | collective-permute-done | bytes 65568 | tf_op jit(solution)/shard_map/ppermute | solution.py:25
  110.3 2.8 %copy-done.8 = bf16[3,1024,1024]{2,1,0:T(8,128)(2,1)S(1)} copy-done((bf16[3,1024,1024]{2,1,0:T(8,128)(2,1)S(1)}, bf16[3,1024,1024]{2,1,0:T(8,128)(2,1)}, u32[]{:S(2)}) %copy-start.8) | copy-done | bytes 6291480
  113.1 5.9 %shard_map.78 = bf16[4,2,528,256]{3,2,1,0:T(8,128)(2,1)S(1)} custom-call(s32[2]{0:T(128)S(1)} %add_convert_fusion.2.valid_ref, f32[528,1024]{1,0:T(8,128)S(1)} %shard_map.77.part_ref, f32[4,4,1024]{2,1,0:T(4,128)S(1)} %collective-permute-done.4.low_in_ref.pre_low_ref, f32[4,4,1024]{2,1,0:T(4,128)S(1)} %collective-permute-done.5.high_in_ref.pre_high_ref, ...), custom_call_target="tpu_custom_call" | custom-call | flops 3321888768 | bytes 12582912 | tf_op jit(solution)/shard_map/pallas_call | solution.py:240
  118.9 1.4 copy-done
  120.3 4.6 %all-to-all-start.1 = ((bf16[4,1056,256]{2,1,0:T(8,128)(2,1)}), bf16[4,1056,256]{2,1,0:T(8,128)(2,1)S(1)}, u32[]{:S(2)}, u32[]{:S(2)}) async-start(bf16[4,1056,256]{2,1,0:T(8,128)(2,1)} %bitcast.80), calls=%async_computation.1 | async-start | bytes 4325376 | tf_op jit(solution)/shard_map/all_to_all | solution.py:45
  125.0 24.1 %all-to-all-done.1 = bf16[4,1056,256]{2,1,0:T(8,128)(2,1)S(1)} async-done(((bf16[4,1056,256]{2,1,0:T(8,128)(2,1)}), bf16[4,1056,256]{2,1,0:T(8,128)(2,1)S(1)}, u32[]{:S(2)}, u32[]{:S(2)}) %all-to-all-start.1) | async-done | bytes 2162720 | tf_op jit(solution)/shard_map/all_to_all | solution.py:45
  149.2 1.2 copy-done.7
  150.4 1.2 copy-done.10
  151.6 6.6 %shard_map.79 = (f32[32,16,768]{2,1,0:T(8,128)S(1)}, bf16[32,16,768]{2,1,0:T(8,128)(2,1)}) custom-call(s32[5]{0:T(128)S(1)} %stack.51.refs_0_, bf16[4,2,528,256]{3,2,1,0:T(8,128)(2,1)S(1)} %bitcast.78, bf16[512,1024]{1,0:T(8,128)(2,1)S(1)} %bitcast.84, bf16[512,1024]{1,0:T(8,128)(2,1)S(1)} %copy-done.5, bf16[256,1024]{1,0:T(8,128)(2,1)} %collective-permute-done.1.refs_4_, ...), custom_call_target="tpu_custom_call" | custom-call | flops 3221225472 | bytes 10485760 | tf_op jit(solution)/shard_map/pallas_call | solution.py:314
  158.2 1.2 copy-done.1
  159.5 2.2 copy-done.9
  161.6 5.6 %shard_map.80 = (f32[32,16,768]{2,1,0:T(8,128)S(1)}, bf16[32,16,768]{2,1,0:T(8,128)(2,1)S(1)}) custom-call(s32[5]{0:T(128)S(1)} %stack.59.refs_0_, bf16[4,2,528,256]{3,2,1,0:T(8,128)(2,1)S(1)} %bitcast.79, bf16[2048,1024]{1,0:T(8,128)(2,1)S(1)} %copy-done.9), custom_call_target="tpu_custom_call" | custom-call | flops 3221225472 | bytes 10485760 | tf_op jit(solution)/shard_map/pallas_call | solution.py:314
  168.1 1.6 collective-permute-done.7
  170.2 24.6 %all_to_all.20 = bf16[4,256,768]{2,1,0:T(8,128)(2,1)S(1)} all-to-all(bf16[4,256,768]{2,1,0:T(8,128)(2,1)S(1)} %bitcast.86), channel_id=1, replica_groups=mesh['video'=4,'x'=4,'z'=8,'core'=2] {'x'}, dimensions={0} | all-to-all | bytes 3145728 | tf_op jit(solution)/shard_map/all_to_all | solution.py:45
  195.2 19.4 %all_to_all.21 = bf16[8,2,16,768]{3,2,1,0:T(8,128)(2,1)S(1)} all-to-all(bf16[8,2,16,768]{3,2,1,0:T(8,128)(2,1)S(1)} %copy.64), channel_id=1, replica_groups=mesh['video'=4,'x'=4,'z'=8,'core'=2] {'z'}, dimensions={0} | all-to-all | bytes 786432 | tf_op jit(solution)/shard_map/all_to_all | solution.py:45
  215.3 2.7 %collective-permute-start.8 = (f32[2,16,768]{2,1,0:T(8,128)S(1)}, f32[2,16,768]{2,1,0:T(8,128)S(1)}, u32[]{:S(2)}, u32[]{:S(2)}) collective-permute-start(f32[2,16,768]{2,1,0:T(8,128)S(1)} %convert_reduce_fusion), channel_id=1, source_target_pairs={{0,192},{64,0},{128,64},{192,128},{1,193},{65,1},{129,65},{193,129... | collective-permute-start | bytes 294920 | tf_op jit(solution)/shard_map/ppermute | solution.py:30
  218.0 3.6 %collective-permute-done.10 = f32[2,16,768]{2,1,0:T(8,128)S(1)} collective-permute-done((f32[2,16,768]{2,1,0:T(8,128)S(1)}, f32[2,16,768]{2,1,0:T(8,128)S(1)}, u32[]{:S(2)}, u32[]{:S(2)}) %collective-permute-start.10) | collective-permute-done | bytes 98336 | tf_op jit(solution)/shard_map/ppermute | solution.py:30
  221.6 2.6 %collective-permute-done.9 = f32[2,16,768]{2,1,0:T(8,128)S(1)} collective-permute-done((f32[2,16,768]{2,1,0:T(8,128)S(1)}, f32[2,16,768]{2,1,0:T(8,128)S(1)}, u32[]{:S(2)}, u32[]{:S(2)}) %collective-permute-start.9) | collective-permute-done | bytes 98336 | tf_op jit(solution)/shard_map/ppermute | solution.py:30
  (91 shorter events, 12.5 us)
Async XLA Ops:
  7.2 4.5 %copy-start.13 = (f32[4,4,16,2]{2,3,1,0:T(2,128)S(1)}, f32[4,4,16,2]{2,3,1,0:T(2,128)}, u32[]{:S(2)}) copy-start(f32[4,4,16,2]{2,3,1,0:T(2,128)} %param.7) | copy-start | bytes 6148
  7.2 5.0 %copy-start.12 = (bf16[4,4,16,1024]{3,2,1,0:T(8,128)(2,1)S(1)}, bf16[4,4,16,1024]{3,2,1,0:T(8,128)(2,1)}, u32[]{:S(2)}) copy-start(bf16[4,4,16,1024]{3,2,1,0:T(8,128)(2,1)} %param.6) | copy-start | bytes 1572868
  10.4 4.1 %copy-start.11 = (bf16[512,1024]{1,0:T(8,128)(2,1)}, bf16[512,1024]{1,0:T(8,128)(2,1)S(1)}, u32[]{:S(2)}) copy-start(bf16[512,1024]{1,0:T(8,128)(2,1)S(1)} %fusion.3) | copy-start | bytes 3145732
  14.5 79.8 %all-to-all-start = ((bf16[64,16,1152]{2,1,0:T(8,128)(2,1)}), bf16[64,16,1152]{2,1,0:T(8,128)(2,1)S(1)}, u32[]{:S(2)}, u32[]{:S(2)}) async-start(bf16[64,16,1152]{2,1,0:T(8,128)(2,1)} %bitcast.85), calls=%async_computation | async-start | bytes 4718592 | tf_op jit(solution)/shard_map/all_to_all | solution.py:45
  26.6 42.0 %copy-start.3 = (bf16[4,128,1024]{2,1,0:T(8,128)(2,1)S(1)}, bf16[4,128,1024]{2,1,0:T(8,128)(2,1)}, u32[]{:S(2)}) copy-start(bf16[4,128,1024]{2,1,0:T(8,128)(2,1)} %param.10) | copy-start | bytes 3145732
  26.6 132.9 %all-gather.2.cloned.1.call-start = ((), (), s32[]{:S(2)}) async-start(), calls=%async_computation.4 | async-start | bytes 5242880 | tf_op jit(solution)/shard_map/all_gather | solution.py:356
  27.3 34.2 %collective-permute-start = (bf16[512,1024]{1,0:T(8,128)(2,1)}, bf16[512,1024]{1,0:T(8,128)(2,1)S(1)}, u32[]{:S(2)}, u32[]{:S(2)}) collective-permute-start(bf16[512,1024]{1,0:T(8,128)(2,1)} %bitcast.82), channel_id=1, source_target_pairs={{0,64},{64,128},{128,192},{192,0},{1,65},{65,129},{129,193},{193,1... | collective-permute-start | bytes 3145736 | tf_op jit(solution)/shard_map/ppermute | solution.py:30
  29.0 35.8 %collective-permute-start.2 = (bf16[512,1024]{1,0:T(8,128)(2,1)}, bf16[512,1024]{1,0:T(8,128)(2,1)S(1)}, u32[]{:S(2)}, u32[]{:S(2)}) collective-permute-start(bf16[512,1024]{1,0:T(8,128)(2,1)} %bitcast.83), channel_id=1, source_target_pairs={{0,192},{64,0},{128,64},{192,128},{1,193},{65,1},{129,65},{193,129... | collective-permute-start | bytes 3145736 | tf_op jit(solution)/shard_map/ppermute | solution.py:30
  62.3 1.0 copy-start.4
  63.4 26.5 %collective-permute-start.1 = (bf16[256,1024]{1,0:T(8,128)(2,1)}, bf16[256,1024]{1,0:T(8,128)(2,1)}, u32[]{:S(2)}, u32[]{:S(2)}) collective-permute-start(bf16[256,1024]{1,0:T(8,128)(2,1)} %slice.87), channel_id=1, source_target_pairs={{0,64},{64,128},{128,192},{192,0},{1,65},{65,129},{129,193},{193,1... | collective-permute-start | bytes 1572872 | tf_op jit(solution)/shard_map/ppermute | solution.py:30
  65.6 1.0 copy-start.6
  66.6 25.2 %collective-permute-start.3 = (bf16[256,1024]{1,0:T(8,128)(2,1)}, bf16[256,1024]{1,0:T(8,128)(2,1)}, u32[]{:S(2)}, u32[]{:S(2)}) collective-permute-start(bf16[256,1024]{1,0:T(8,128)(2,1)} %slice.89), channel_id=1, source_target_pairs={{0,192},{64,0},{128,64},{192,128},{1,193},{65,1},{129,65},{193,129... | collective-permute-start | bytes 1572872 | tf_op jit(solution)/shard_map/ppermute | solution.py:30
  100.6 4.5 %collective-permute-start.5 = (f32[4,4,1024]{2,1,0:T(4,128)S(1)}, f32[4,4,1024]{2,1,0:T(4,128)S(1)}, u32[]{:S(2)}, u32[]{:S(2)}) collective-permute-start(f32[4,4,1024]{2,1,0:T(4,128)S(1)} %pad_maximum_fusion.2), channel_id=1, source_target_pairs={{1,0},{2,1},{3,2},{4,3},{5,4},{6,5},{7,6},{8,7},{9,8},{10,9},{11,1... | collective-permute-start | bytes 196616 | tf_op jit(solution)/shard_map/ppermute | solution.py:25
  102.6 7.7 %collective-permute-start.4 = (f32[4,4,1024]{2,1,0:T(4,128)S(1)}, f32[4,4,1024]{2,1,0:T(4,128)S(1)}, u32[]{:S(2)}, u32[]{:S(2)}) collective-permute-start(f32[4,4,1024]{2,1,0:T(4,128)S(1)} %pad_maximum_fusion.1), channel_id=1, source_target_pairs={{0,1},{1,2},{2,3},{3,4},{4,5},{5,6},{6,7},{7,8},{8,9},{9,10},{10,1... | collective-permute-start | bytes 196616 | tf_op jit(solution)/shard_map/ppermute | solution.py:25
  110.3 2.8 %copy-start.8 = (bf16[3,1024,1024]{2,1,0:T(8,128)(2,1)S(1)}, bf16[3,1024,1024]{2,1,0:T(8,128)(2,1)}, u32[]{:S(2)}) copy-start(bf16[3,1024,1024]{2,1,0:T(8,128)(2,1)} %taps_ref.1) | copy-start | bytes 18874372
  118.9 1.4 copy-start
  120.3 28.8 %copy-start.5 = (bf16[512,1024]{1,0:T(8,128)(2,1)S(1)}, bf16[512,1024]{1,0:T(8,128)(2,1)}, u32[]{:S(2)}) copy-start(bf16[512,1024]{1,0:T(8,128)(2,1)} %copy-done.4) | copy-start | bytes 3145732
  120.3 28.8 %all-to-all-start.1 = ((bf16[4,1056,256]{2,1,0:T(8,128)(2,1)}), bf16[4,1056,256]{2,1,0:T(8,128)(2,1)S(1)}, u32[]{:S(2)}, u32[]{:S(2)}) async-start(bf16[4,1056,256]{2,1,0:T(8,128)(2,1)} %bitcast.80), calls=%async_computation.1 | async-start | bytes 4325376 | tf_op jit(solution)/shard_map/all_to_all | solution.py:45
  149.2 1.2 copy-start.7
  150.4 1.2 copy-start.10
  158.2 1.2 copy-start.1
  159.4 8.5 %collective-permute-start.6 = (bf16[32,16,768]{2,1,0:T(8,128)(2,1)}, bf16[32,16,768]{2,1,0:T(8,128)(2,1)S(1)}, u32[]{:S(2)}, u32[]{:S(2)}) collective-permute-start(bf16[32,16,768]{2,1,0:T(8,128)(2,1)} %get-tuple-element.7), channel_id=1, source_target_pairs={{0,1},{1,0},{2,3},{3,2},{4,5},{5,4},{6,7},{7,6},{8,9},{9,8},{10,11... | collective-permute-start | bytes 2359304 | tf_op jit(solution)/shard_map/ppermute | solution.py:30
  159.5 2.2 copy-start.9
  161.6 6.2 %copy-start.2 = (f32[32,16,768]{2,1,0:T(8,128)S(1)}, f32[32,16,768]{2,1,0:T(8,128)}, u32[]{:S(2)}) copy-start(f32[32,16,768]{2,1,0:T(8,128)} %copy-done.1) | copy-start | bytes 4718596
  167.2 2.5 %collective-permute-start.7 = (bf16[32,16,768]{2,1,0:T(8,128)(2,1)S(1)}, bf16[32,16,768]{2,1,0:T(8,128)(2,1)S(1)}, u32[]{:S(2)}, u32[]{:S(2)}) collective-permute-start(bf16[32,16,768]{2,1,0:T(8,128)(2,1)S(1)} %get-tuple-element.9), channel_id=1, source_target_pairs={{0,1},{1,0},{2,3},{3,2},{4,5},{5,4},{6,7},{7,6},{8,9},{9,8},{10,11... | collective-permute-start | bytes 2359304 | tf_op jit(solution)/shard_map/ppermute | solution.py:30
  214.7 6.9 %collective-permute-start.10 = (f32[2,16,768]{2,1,0:T(8,128)S(1)}, f32[2,16,768]{2,1,0:T(8,128)S(1)}, u32[]{:S(2)}, u32[]{:S(2)}) collective-permute-start(f32[2,16,768]{2,1,0:T(8,128)S(1)} %convert_reduce_fusion), channel_id=1, source_target_pairs={{0,64},{64,128},{128,192},{192,0},{1,65},{65,129},{129,193},{193,1... | collective-permute-start | bytes 294920 | tf_op jit(solution)/shard_map/ppermute | solution.py:30
  215.3 6.2 %collective-permute-start.8 = (f32[2,16,768]{2,1,0:T(8,128)S(1)}, f32[2,16,768]{2,1,0:T(8,128)S(1)}, u32[]{:S(2)}, u32[]{:S(2)}) collective-permute-start(f32[2,16,768]{2,1,0:T(8,128)S(1)} %convert_reduce_fusion), channel_id=1, source_target_pairs={{0,192},{64,0},{128,64},{192,128},{1,193},{65,1},{129,65},{193,129... | collective-permute-start | bytes 294920 | tf_op jit(solution)/shard_map/ppermute | solution.py:30
  218.0 6.1 %collective-permute-start.9 = (f32[2,16,768]{2,1,0:T(8,128)S(1)}, f32[2,16,768]{2,1,0:T(8,128)S(1)}, u32[]{:S(2)}, u32[]{:S(2)}) collective-permute-start(f32[2,16,768]{2,1,0:T(8,128)S(1)} %convert_reduce_fusion), channel_id=1, source_target_pairs={{0,128},{64,192},{128,0},{192,64},{1,129},{65,193},{129,1},{193,65... | collective-permute-start | bytes 294920 | tf_op jit(solution)/shard_map/ppermute | solution.py:30
Sparse Core Ops, SparseCore 0:
  29.2 70.1 all-gather.1

commit v7 on v6

--- a/solution.py
+++ b/solution.py
@@ -152,7 +152,7 @@
         ],
         out_specs=pl.BlockSpec((row_count, step), lambda q: (0, q)),
         scratch_shapes=[pltpu.VMEM((2, row_count, slots), jnp.bfloat16)],
-        compiler_params=pltpu.CompilerParams(vmem_limit_bytes=20 * 2**20),
+        compiler_params=pltpu.CompilerParams(vmem_limit_bytes=12 * 2**20),
         cost_estimate=pl.CostEstimate(
             flops=4 * row_count * channels * slots,
             bytes_accessed=5 * 2**20,
@@ -349,7 +349,6 @@
     each = channels // peers
     pre_values = preact.astype(jnp.float32).reshape(main_rows, channels)
     activation = jax.nn.silu(pre_values).astype(jnp.bfloat16)
-    tap_weight = tap_weight + (activation[0, 0] * 0).astype(jnp.float32)
     sent = send_slots(bin_grad, tap_weight, tap_index, snip_count, peers)
     got = exchange(sent, TM)
 
@@ -360,8 +359,8 @@
     ends = partial[:main_rows].reshape(video_count, snip_count, channels)
     low = partial[main_rows : main_rows + video_count]
     high = partial[main_rows + video_count : main_rows + 2 * video_count]
-    arrived = sum(piece[0, 0] * 0 for piece in feature_all[2:4]).astype(jnp.float32)
-    pre_ends = pre_values.reshape(ends.shape)[:, :: snip_count - 1] + arrived
+    begun = ((feature_all[1][0, 0] + feature_all[-1][0, 0]) * 0).astype(jnp.float32)
+    pre_ends = pre_values.reshape(ends.shape)[:, :: snip_count - 1] + begun
     from_low = neighbours(jnp.stack([ends[:, -2], ends[:, -1], high, pre_ends[:, 1]]), True)
     from_high = neighbours(jnp.stack([low, ends[:, 0], ends[:, 1], pre_ends[:, 0]]), False)
     at = lax.axis_index(TM)

time: 234 us -> 228 us (0.974)
  blocking collectives: 44 us -> 41.3 us
  waiting for transfers between devices: 90.5 us -> 88 us
    all_to_all x2, waiting for transfers between devices: 24.1 us -> 14.3 us  [exchange(): return lax.all_to_all(value, axis, split_axis=0, concat_axis=0, tiled=True)]
    ppermute x9, waiting for transfers between devices: 60.5 us -> 68.2 us  [ring_shift(): lax.ppermute(value, axis, [(i, (i + shift) % count) for i in range(count)])]
    unnamed x37 -> x24, local copies, waits for them, and re-layouts: 13.7 us -> 9.98 us
    all_to_all x2, blocking collectives: 44 us -> 41.3 us  [exchange(): return lax.all_to_all(value, axis, split_axis=0, concat_axis=0, tiled=True)]
  transfers between devices with their start and end apart: 14 -> 14, of which waited for: 8 -> 8; matrix products, arithmetic and copies ran while one was open for 2% -> 4% of each run, Pallas kernels for 10% -> 11%
where the time goes in v7:
time: 228 us; the launch traced here: 227 us
  waiting for transfers between devices  88 us (39%)
  blocking collectives  41.3 us (18%)
  starting transfers between devices  32.6 us (14%)
  Pallas kernels  24.2 us (11%)
  local copies, waits for them, and re-layouts  18 us (8%)
  between operations  15.7 us (7%)
  other arithmetic  3.76 us (2%)
  matrix products  3.38 us (1%)
    ppermute x9, waiting for transfers between devices, ring_shift(): lax.ppermute(value, axis, [(i, (i + shift) % count) for i in range(count)])  68.2 us
    all_to_all x2, blocking collectives, exchange(): return lax.all_to_all(value, axis, split_axis=0, concat_axis=0, tiled=True)  41.3 us
    all_to_all x2, starting transfers between devices, exchange(): return lax.all_to_all(value, axis, split_axis=0, concat_axis=0, tiled=True)  16.6 us
    all_to_all x2, waiting for transfers between devices, exchange(): return lax.all_to_all(value, axis, split_axis=0, concat_axis=0, tiled=True)  14.3 us
    pallas_call x2, Pallas kernels, filter_terms(): pl.pallas_call(lambda *refs: terms_kernel(videos, layer, *refs), grid=(ch...  12.3 us
    ppermute x9, starting transfers between devices, ring_shift(): lax.ppermute(value, axis, [(i, (i + shift) % count) for i in range(count)])  10.7 us
    unnamed x24, local copies, waits for them, and re-layouts  9.98 us
    pallas_call x1, Pallas kernels, collect(): pl.pallas_call(collect_kernel, grid=(channels // step,), out_shape=jax.Sh...  6 us
  transfers between devices with their start and end apart: 14, of which 8 were waited for; matrix products, arithmetic and copies ran while one was open for 4% of the time, Pallas kernels for 11%

profile of v7, /device:TPU:2, one launch (start us, length us, event | category | flops | bytes accessed | tf_op | source)
XLA Modules:
  0.0 226.8 jit_solution(1894452113609408979)
XLA Ops:
  9.7 3.4 %convolution_convert_fusion = bf16[1024,1152]{1,0:T(8,128)(2,1)} fusion(bf16[256,128]{1,0:T(8,128)(2,1)S(1)} %select_convert_fusion, bf16[256,1024]{1,0:T(8,128)(2,1)} %bitcast.87, s32[256]{0:T(256)S(1)} %get-tuple-element.48), kind=kOutput, calls=%fused_computation | convolution fusion | flops 606601216 | bytes 2950144 | tf_op jit(solution)/shard_map/dot_general | solution.py:114
  13.1 12.2 %all-to-all-start = ((bf16[64,16,1152]{2,1,0:T(8,128)(2,1)}), bf16[64,16,1152]{2,1,0:T(8,128)(2,1)S(1)}, u32[]{:S(2)}, u32[]{:S(2)}) async-start(bf16[64,16,1152]{2,1,0:T(8,128)(2,1)} %bitcast.81), calls=%async_computation | async-start | bytes 4718592 | tf_op jit(solution)/shard_map/all_to_all | solution.py:45
  25.3 1.6 fusion.3
  27.0 1.7 collective-permute-start
  28.6 1.7 collective-permute-start.1
  30.4 31.8 %collective-permute-done.refs_3_ = bf16[512,1024]{1,0:T(8,128)(2,1)} collective-permute-done((bf16[512,1024]{1,0:T(8,128)(2,1)}, bf16[512,1024]{1,0:T(8,128)(2,1)}, u32[]{:S(2)}, u32[]{:S(2)}) %collective-permute-start) | collective-permute-done | bytes 1048608 | tf_op jit(solution)/shard_map/ppermute | solution.py:30
  62.2 1.2 slice.82
  63.7 1.2 slice.83
  66.2 14.3 %all-to-all-done = bf16[64,16,1152]{2,1,0:T(8,128)(2,1)S(1)} async-done(((bf16[64,16,1152]{2,1,0:T(8,128)(2,1)}), bf16[64,16,1152]{2,1,0:T(8,128)(2,1)S(1)}, u32[]{:S(2)}, u32[]{:S(2)}) %all-to-all-start) | async-done | bytes 2359328 | tf_op jit(solution)/shard_map/all_to_all | solution.py:45
  80.5 6.0 %shard_map.77.part_ref = f32[528,1024]{1,0:T(8,128)S(1)} custom-call(bf16[1024,1152]{1,0:T(8,128)(2,1)S(1)} %bitcast.72, bf16[1024,1152]{1,0:T(8,128)(2,1)S(1)} %bitcast.73), custom_call_target="tpu_custom_call" | custom-call | flops 2214592512 | bytes 5242880 | tf_op jit(solution)/shard_map/pallas_call | solution.py:145
  86.8 3.0 %collective-permute-start.3 = (f32[4,4,1024]{2,1,0:T(4,128)S(1)}, f32[4,4,1024]{2,1,0:T(4,128)S(1)}, u32[]{:S(2)}, u32[]{:S(2)}) collective-permute-start(f32[4,4,1024]{2,1,0:T(4,128)S(1)} %pad_maximum_fusion.2), channel_id=1, source_target_pairs={{1,0},{2,1},{3,2},{4,3},{5,4},{6,5},{7,6},{8,7},{9,8},{10,9},{11,1... | collective-permute-start | bytes 196616 | tf_op jit(solution)/shard_map/ppermute | solution.py:25
  89.9 2.2 collective-permute-start.2
  92.2 5.4 %collective-permute-done.2.low_in_ref.pre_low_ref = f32[4,4,1024]{2,1,0:T(4,128)S(1)} collective-permute-done((f32[4,4,1024]{2,1,0:T(4,128)S(1)}, f32[4,4,1024]{2,1,0:T(4,128)S(1)}, u32[]{:S(2)}, u32[]{:S(2)}) %collective-permute-start.2) | collective-permute-done | bytes 65568 | tf_op jit(solution)/shard_map/ppermute | solution.py:25
  97.6 2.8 %copy-done.4 = bf16[3,1024,1024]{2,1,0:T(8,128)(2,1)S(1)} copy-done((bf16[3,1024,1024]{2,1,0:T(8,128)(2,1)S(1)}, bf16[3,1024,1024]{2,1,0:T(8,128)(2,1)}, u32[]{:S(2)}) %copy-start.4) | copy-done | bytes 6291480
  100.4 5.9 %shard_map.78 = bf16[4,2,528,256]{3,2,1,0:T(8,128)(2,1)S(1)} custom-call(s32[2]{0:T(128)S(1)} %add_convert_fusion.2.valid_ref, f32[528,1024]{1,0:T(8,128)S(1)} %shard_map.77.part_ref, f32[4,4,1024]{2,1,0:T(4,128)S(1)} %collective-permute-done.2.low_in_ref.pre_low_ref, f32[4,4,1024]{2,1,0:T(4,128)S(1)} %collective-permute-done.3.high_in_ref.pre_high_ref, ...), custom_call_target="tpu_custom_call" | custom-call | flops 3321888768 | bytes 12582912 | tf_op jit(solution)/shard_map/pallas_call | solution.py:240
  106.3 1.4 copy-done
  107.7 4.5 %all-to-all-start.1 = ((bf16[4,1056,256]{2,1,0:T(8,128)(2,1)}), bf16[4,1056,256]{2,1,0:T(8,128)(2,1)S(1)}, u32[]{:S(2)}, u32[]{:S(2)}) async-start(bf16[4,1056,256]{2,1,0:T(8,128)(2,1)} %bitcast.76), calls=%async_computation.1 | async-start | bytes 4325376 | tf_op jit(solution)/shard_map/all_to_all | solution.py:45
  112.1 2.0 slice.89
  114.1 2.0 collective-permute-start.4
  116.1 1.9 slice.90
  118.0 1.2 collective-permute-start.5
  119.3 28.6 %collective-permute-done.4.refs_4_ = bf16[256,1024]{1,0:T(8,128)(2,1)} collective-permute-done((bf16[256,1024]{1,0:T(8,128)(2,1)}, bf16[256,1024]{1,0:T(8,128)(2,1)}, u32[]{:S(2)}, u32[]{:S(2)}) %collective-permute-start.4) | collective-permute-done | bytes 524320 | tf_op jit(solution)/shard_map/ppermute | solution.py:30
  147.9 6.8 %shard_map.79 = (f32[32,16,768]{2,1,0:T(8,128)S(1)}, bf16[32,16,768]{2,1,0:T(8,128)(2,1)}) custom-call(s32[5]{0:T(128)S(1)} %stack.51.refs_0_, bf16[4,2,528,256]{3,2,1,0:T(8,128)(2,1)S(1)} %bitcast.74, bf16[512,1024]{1,0:T(8,128)(2,1)S(1)} %bitcast.80, bf16[512,1024]{1,0:T(8,128)(2,1)} %collective-permute-done.refs_3_, ...), custom_call_target="tpu_custom_call" | custom-call | flops 3221225472 | bytes 10485760 | tf_op jit(solution)/shard_map/pallas_call | solution.py:314
  154.7 1.2 copy-done.1
  155.9 2.2 copy-done.5
  158.1 5.6 %shard_map.80 = (f32[32,16,768]{2,1,0:T(8,128)S(1)}, bf16[32,16,768]{2,1,0:T(8,128)(2,1)S(1)}) custom-call(s32[5]{0:T(128)S(1)} %stack.59.refs_0_, bf16[4,2,528,256]{3,2,1,0:T(8,128)(2,1)S(1)} %bitcast.75, bf16[2048,1024]{1,0:T(8,128)(2,1)S(1)} %copy-done.5), custom_call_target="tpu_custom_call" | custom-call | flops 3221225472 | bytes 10485760 | tf_op jit(solution)/shard_map/pallas_call | solution.py:314
  164.6 1.6 collective-permute-done.7
  166.6 24.5 %all_to_all.20 = bf16[4,256,768]{2,1,0:T(8,128)(2,1)S(1)} all-to-all(bf16[4,256,768]{2,1,0:T(8,128)(2,1)S(1)} %bitcast.82), channel_id=1, replica_groups=mesh['video'=4,'x'=4,'z'=8,'core'=2] {'x'}, dimensions={0} | all-to-all | bytes 3145728 | tf_op jit(solution)/shard_map/all_to_all | solution.py:45
  191.6 16.8 %all_to_all.21 = bf16[8,2,16,768]{3,2,1,0:T(8,128)(2,1)S(1)} all-to-all(bf16[8,2,16,768]{3,2,1,0:T(8,128)(2,1)S(1)} %copy.64), channel_id=1, replica_groups=mesh['video'=4,'x'=4,'z'=8,'core'=2] {'z'}, dimensions={0} | all-to-all | bytes 786432 | tf_op jit(solution)/shard_map/all_to_all | solution.py:45
  208.7 3.0 %collective-permute-start.8 = (f32[2,16,768]{2,1,0:T(8,128)S(1)}, f32[2,16,768]{2,1,0:T(8,128)S(1)}, u32[]{:S(2)}, u32[]{:S(2)}) collective-permute-start(f32[2,16,768]{2,1,0:T(8,128)S(1)} %convert_reduce_fusion), channel_id=1, source_target_pairs={{0,192},{64,0},{128,64},{192,128},{1,193},{65,1},{129,65},{193,129... | collective-permute-start | bytes 294920 | tf_op jit(solution)/shard_map/ppermute | solution.py:30
  212.0 3.3 %collective-permute-done.10 = f32[2,16,768]{2,1,0:T(8,128)S(1)} collective-permute-done((f32[2,16,768]{2,1,0:T(8,128)S(1)}, f32[2,16,768]{2,1,0:T(8,128)S(1)}, u32[]{:S(2)}, u32[]{:S(2)}) %collective-permute-start.10) | collective-permute-done | bytes 98336 | tf_op jit(solution)/shard_map/ppermute | solution.py:30
  215.3 2.5 %collective-permute-done.9 = f32[2,16,768]{2,1,0:T(8,128)S(1)} collective-permute-done((f32[2,16,768]{2,1,0:T(8,128)S(1)}, f32[2,16,768]{2,1,0:T(8,128)S(1)}, u32[]{:S(2)}, u32[]{:S(2)}) %collective-permute-start.9) | collective-permute-done | bytes 98336 | tf_op jit(solution)/shard_map/ppermute | solution.py:30
  (75 shorter events, 7.9 us)
Async XLA Ops:
  13.1 12.2 %copy-start.3 = (bf16[4,128,1024]{2,1,0:T(8,128)(2,1)S(1)}, bf16[4,128,1024]{2,1,0:T(8,128)(2,1)}, u32[]{:S(2)}) copy-start(bf16[4,128,1024]{2,1,0:T(8,128)(2,1)} %param.10) | copy-start | bytes 3145732
  13.1 67.4 %all-to-all-start = ((bf16[64,16,1152]{2,1,0:T(8,128)(2,1)}), bf16[64,16,1152]{2,1,0:T(8,128)(2,1)S(1)}, u32[]{:S(2)}, u32[]{:S(2)}) async-start(bf16[64,16,1152]{2,1,0:T(8,128)(2,1)} %bitcast.81), calls=%async_computation | async-start | bytes 4718592 | tf_op jit(solution)/shard_map/all_to_all | solution.py:45
  25.3 130.7 %all-gather.2.cloned.1.call-start = ((), (), s32[]{:S(2)}) async-start(), calls=%async_computation.4 | async-start | bytes 5242880 | tf_op jit(solution)/shard_map/all_gather | solution.py:355
  27.0 35.3 %collective-permute-start = (bf16[512,1024]{1,0:T(8,128)(2,1)}, bf16[512,1024]{1,0:T(8,128)(2,1)}, u32[]{:S(2)}, u32[]{:S(2)}) collective-permute-start(bf16[512,1024]{1,0:T(8,128)(2,1)} %bitcast.78), channel_id=1, source_target_pairs={{0,64},{64,128},{128,192},{192,0},{1,65},{65,129},{129,193},{193,1... | collective-permute-start | bytes 3145736 | tf_op jit(solution)/shard_map/ppermute | solution.py:30
  28.6 35.1 %collective-permute-start.1 = (bf16[512,1024]{1,0:T(8,128)(2,1)}, bf16[512,1024]{1,0:T(8,128)(2,1)}, u32[]{:S(2)}, u32[]{:S(2)}) collective-permute-start(bf16[512,1024]{1,0:T(8,128)(2,1)} %bitcast.79), channel_id=1, source_target_pairs={{0,192},{64,0},{128,64},{192,128},{1,193},{65,1},{129,65},{193,129... | collective-permute-start | bytes 3145736 | tf_op jit(solution)/shard_map/ppermute | solution.py:30
  86.8 5.4 %collective-permute-start.3 = (f32[4,4,1024]{2,1,0:T(4,128)S(1)}, f32[4,4,1024]{2,1,0:T(4,128)S(1)}, u32[]{:S(2)}, u32[]{:S(2)}) collective-permute-start(f32[4,4,1024]{2,1,0:T(4,128)S(1)} %pad_maximum_fusion.2), channel_id=1, source_target_pairs={{1,0},{2,1},{3,2},{4,3},{5,4},{6,5},{7,6},{8,7},{9,8},{10,9},{11,1... | collective-permute-start | bytes 196616 | tf_op jit(solution)/shard_map/ppermute | solution.py:25
  89.9 7.7 %collective-permute-start.2 = (f32[4,4,1024]{2,1,0:T(4,128)S(1)}, f32[4,4,1024]{2,1,0:T(4,128)S(1)}, u32[]{:S(2)}, u32[]{:S(2)}) collective-permute-start(f32[4,4,1024]{2,1,0:T(4,128)S(1)} %pad_maximum_fusion.1), channel_id=1, source_target_pairs={{0,1},{1,2},{2,3},{3,4},{4,5},{5,6},{6,7},{7,8},{8,9},{9,10},{10,1... | collective-permute-start | bytes 196616 | tf_op jit(solution)/shard_map/ppermute | solution.py:25
  97.6 2.8 %copy-start.4 = (bf16[3,1024,1024]{2,1,0:T(8,128)(2,1)S(1)}, bf16[3,1024,1024]{2,1,0:T(8,128)(2,1)}, u32[]{:S(2)}) copy-start(bf16[3,1024,1024]{2,1,0:T(8,128)(2,1)} %taps_ref.1) | copy-start | bytes 18874372
  106.2 1.4 copy-start
  107.7 40.3 %all-to-all-start.1 = ((bf16[4,1056,256]{2,1,0:T(8,128)(2,1)}), bf16[4,1056,256]{2,1,0:T(8,128)(2,1)S(1)}, u32[]{:S(2)}, u32[]{:S(2)}) async-start(bf16[4,1056,256]{2,1,0:T(8,128)(2,1)} %bitcast.76), calls=%async_computation.1 | async-start | bytes 4325376 | tf_op jit(solution)/shard_map/all_to_all | solution.py:45
  112.1 35.8 %copy-start.6 = (bf16[4,128,1024]{2,1,0:T(8,128)(2,1)S(1)}, bf16[4,128,1024]{2,1,0:T(8,128)(2,1)}, u32[]{:S(2)}) copy-start(bf16[4,128,1024]{2,1,0:T(8,128)(2,1)} %param.9) | copy-start | bytes 3145732
  114.1 33.8 %collective-permute-start.4 = (bf16[256,1024]{1,0:T(8,128)(2,1)}, bf16[256,1024]{1,0:T(8,128)(2,1)}, u32[]{:S(2)}, u32[]{:S(2)}) collective-permute-start(bf16[256,1024]{1,0:T(8,128)(2,1)} %slice.89), channel_id=1, source_target_pairs={{0,64},{64,128},{128,192},{192,0},{1,65},{65,129},{129,193},{193,1... | collective-permute-start | bytes 1572872 | tf_op jit(solution)/shard_map/ppermute | solution.py:30
  118.0 29.9 %collective-permute-start.5 = (bf16[256,1024]{1,0:T(8,128)(2,1)}, bf16[256,1024]{1,0:T(8,128)(2,1)}, u32[]{:S(2)}, u32[]{:S(2)}) collective-permute-start(bf16[256,1024]{1,0:T(8,128)(2,1)} %slice.90), channel_id=1, source_target_pairs={{0,192},{64,0},{128,64},{192,128},{1,193},{65,1},{129,65},{193,129... | collective-permute-start | bytes 1572872 | tf_op jit(solution)/shard_map/ppermute | solution.py:30
  154.7 1.2 copy-start.1
  155.8 8.5 %collective-permute-start.6 = (bf16[32,16,768]{2,1,0:T(8,128)(2,1)}, bf16[32,16,768]{2,1,0:T(8,128)(2,1)S(1)}, u32[]{:S(2)}, u32[]{:S(2)}) collective-permute-start(bf16[32,16,768]{2,1,0:T(8,128)(2,1)} %get-tuple-element.7), channel_id=1, source_target_pairs={{0,1},{1,0},{2,3},{3,2},{4,5},{5,4},{6,7},{7,6},{8,9},{9,8},{10,11... | collective-permute-start | bytes 2359304 | tf_op jit(solution)/shard_map/ppermute | solution.py:30
  155.9 2.2 copy-start.5
  158.1 6.2 %copy-start.2 = (f32[32,16,768]{2,1,0:T(8,128)S(1)}, f32[32,16,768]{2,1,0:T(8,128)}, u32[]{:S(2)}) copy-start(f32[32,16,768]{2,1,0:T(8,128)} %copy-done.1) | copy-start | bytes 4718596
  163.7 2.5 %collective-permute-start.7 = (bf16[32,16,768]{2,1,0:T(8,128)(2,1)S(1)}, bf16[32,16,768]{2,1,0:T(8,128)(2,1)S(1)}, u32[]{:S(2)}, u32[]{:S(2)}) collective-permute-start(bf16[32,16,768]{2,1,0:T(8,128)(2,1)S(1)} %get-tuple-element.9), channel_id=1, source_target_pairs={{0,1},{1,0},{2,3},{3,2},{4,5},{5,4},{6,7},{7,6},{8,9},{9,8},{10,11... | collective-permute-start | bytes 2359304 | tf_op jit(solution)/shard_map/ppermute | solution.py:30
  208.4 6.9 %collective-permute-start.10 = (f32[2,16,768]{2,1,0:T(8,128)S(1)}, f32[2,16,768]{2,1,0:T(8,128)S(1)}, u32[]{:S(2)}, u32[]{:S(2)}) collective-permute-start(f32[2,16,768]{2,1,0:T(8,128)S(1)} %convert_reduce_fusion), channel_id=1, source_target_pairs={{0,64},{64,128},{128,192},{192,0},{1,65},{65,129},{129,193},{193,1... | collective-permute-start | bytes 294920 | tf_op jit(solution)/shard_map/ppermute | solution.py:30
  208.7 6.6 %collective-permute-start.8 = (f32[2,16,768]{2,1,0:T(8,128)S(1)}, f32[2,16,768]{2,1,0:T(8,128)S(1)}, u32[]{:S(2)}, u32[]{:S(2)}) collective-permute-start(f32[2,16,768]{2,1,0:T(8,128)S(1)} %convert_reduce_fusion), channel_id=1, source_target_pairs={{0,192},{64,0},{128,64},{192,128},{1,193},{65,1},{129,65},{193,129... | collective-permute-start | bytes 294920 | tf_op jit(solution)/shard_map/ppermute | solution.py:30
  211.7 6.1 %collective-permute-start.9 = (f32[2,16,768]{2,1,0:T(8,128)S(1)}, f32[2,16,768]{2,1,0:T(8,128)S(1)}, u32[]{:S(2)}, u32[]{:S(2)}) collective-permute-start(f32[2,16,768]{2,1,0:T(8,128)S(1)} %convert_reduce_fusion), channel_id=1, source_target_pairs={{0,128},{64,192},{128,0},{192,64},{1,129},{65,193},{129,1},{193,65... | collective-permute-start | bytes 294920 | tf_op jit(solution)/shard_map/ppermute | solution.py:30
Sparse Core Ops, SparseCore 0:
  27.9 59.8 all-gather.1

commit v8 on v7

--- a/solution.py
+++ b/solution.py
@@ -28,17 +28,6 @@
 def ring_shift(value, axis, shift):
     count = lax.axis_size(axis)
     return lax.ppermute(value, axis, [(i, (i + shift) % count) for i in range(count)])
-
-
-def around_video(rows):
-    count = lax.axis_size("video")
-    half = rows.shape[0] // 2
-    if count != 4:
-        held = [rows] + [ring_shift(rows, "video", shift) for shift in range(1, count)]
-        return [piece for part in held for piece in (part[:half], part[half:])]
-    below, above = ring_shift(rows, "video", 1), ring_shift(rows, "video", 3)
-    far = [ring_shift(below[:half], "video", 1), ring_shift(above[half:], "video", 3)]
-    return [rows, below] + far + [above]
 
 
 def exchange(value, axis):
@@ -353,14 +342,15 @@
     got = exchange(sent, TM)
 
     act_all = lax.all_gather(activation, "video", axis=0, tiled=True)
-    feature_all = around_video(features.reshape(main_rows, channels))
+    feature_all = lax.all_gather(
+        features.reshape(main_rows, channels), "video", axis=0, tiled=True
+    )
 
     partial = collect(got, channels, main_rows + 16)
     ends = partial[:main_rows].reshape(video_count, snip_count, channels)
     low = partial[main_rows : main_rows + video_count]
     high = partial[main_rows + video_count : main_rows + 2 * video_count]
-    begun = ((feature_all[1][0, 0] + feature_all[-1][0, 0]) * 0).astype(jnp.float32)
-    pre_ends = pre_values.reshape(ends.shape)[:, :: snip_count - 1] + begun
+    pre_ends = pre_values.reshape(ends.shape)[:, :: snip_count - 1]
     from_low = neighbours(jnp.stack([ends[:, -2], ends[:, -1], high, pre_ends[:, 1]]), True)
     from_high = neighbours(jnp.stack([low, ends[:, 0], ends[:, 1], pre_ends[:, 0]]), False)
     at = lax.axis_index(TM)
@@ -372,12 +362,11 @@
     shares = shares.reshape(quarters, 2, block, width)
 
     in_order = jnp.stack([core] + [jnp.int32(source) for source in range(quarters)])
-    around = jnp.stack([core] + [(place + quarters - source) % quarters for source in range(quarters)])
     second = share_by_core(
         *filter_terms([act_all], shares, 0, in_order, video_count, lag_count, each)
     )
     first = share_by_core(
-        *filter_terms(feature_all, shares, 1, around, video_count, lag_count, each)
+        *filter_terms([feature_all], shares, 1, in_order, video_count, lag_count, each)
     )
     x_total, z_total = lax.axis_size("x"), lax.axis_size("z")
     both = jnp.stack([part.reshape(x_total, -1, lag_count * width) for part in (first, second)], 1)

time: 228 us -> 224 us (0.982)
  starting transfers between devices: 32.6 us -> 26.1 us
  waiting for transfers between devices: 88 us -> 92.6 us
  local copies, waits for them, and re-layouts: 18 us -> 13.9 us
  blocking collectives: 41.3 us -> 45.3 us
    all_to_all x2, waiting for transfers between devices: 14.3 us -> 80 us  [exchange(): return lax.all_to_all(value, axis, split_axis=0, concat_axis=0, tiled=True)]
    ppermute x9 -> x5, waiting for transfers between devices: 68.2 us -> 6.39 us  [ring_shift(): lax.ppermute(value, axis, [(i, (i + shift) % count) for i in range(count)])]
    ppermute x9 -> x5, starting transfers between devices: 10.7 us -> 4.13 us  [ring_shift(): lax.ppermute(value, axis, [(i, (i + shift) % count) for i in range(count)])]
    slice x5 -> x2, local copies, waits for them, and re-layouts: 6.34 us -> 0.12 us  [the longest x1 0.1 us: on_device(): pre_ends = pre_values.reshape(ends.shape)[:, ::snip_count - 1]]
    all_to_all x2, blocking collectives: 41.3 us -> 45.3 us  [exchange(): return lax.all_to_all(value, axis, split_axis=0, concat_axis=0, tiled=True)]
    unnamed x24 -> x26, local copies, waits for them, and re-layouts: 9.98 us -> 12.2 us
  transfers between devices with their start and end apart: 14 -> 11, of which waited for: 8 -> 7; matrix products, arithmetic and copies ran while one was open for 4% -> 4% of each run, Pallas kernels for 11% -> 10%
where the time goes in v8:
time: 224 us
  waiting for transfers between devices  92.6 us (41%)
  blocking collectives  45.3 us (20%)
  starting transfers between devices  26.1 us (12%)
  Pallas kernels  23 us (10%)
  between operations  14.4 us (6%)
  local copies, waits for them, and re-layouts  13.9 us (6%)
  other arithmetic  4.82 us (2%)
  matrix products  3.41 us (2%)
    all_to_all x2, waiting for transfers between devices, exchange(): return lax.all_to_all(value, axis, split_axis=0, concat_axis=0, tiled=True)  80 us
    all_to_all x2, blocking collectives, exchange(): return lax.all_to_all(value, axis, split_axis=0, concat_axis=0, tiled=True)  45.3 us
    all_to_all x2, starting transfers between devices, exchange(): return lax.all_to_all(value, axis, split_axis=0, concat_axis=0, tiled=True)  16.6 us
    unnamed x26, local copies, waits for them, and re-layouts  12.2 us
    pallas_call x2, Pallas kernels, filter_terms(): pl.pallas_call(lambda *refs: terms_kernel(videos, layer, *refs), grid=(ch...  11.2 us
    ppermute x5, waiting for transfers between devices, ring_shift(): lax.ppermute(value, axis, [(i, (i + shift) % count) for i in range(count)])  6.39 us
    pallas_call x1, Pallas kernels, collect(): pl.pallas_call(collect_kernel, grid=(channels // step,), out_shape=jax.Sh...  6 us
    pallas_call x1, Pallas kernels, gradients(): pl.pallas_call(grads_kernel, grid=(quarters,), out_shape=share, in_specs=...  5.87 us
  transfers between devices with their start and end apart: 11, of which 7 were waited for; matrix products, arithmetic and copies ran while one was open for 4% of the time, Pallas kernels for 10%

profile of v8, /device:TPU:2, one launch (start us, length us, event | category | flops | bytes accessed | tf_op | source)
XLA Modules:
  0.0 223.6 jit_solution(8008692131283926669)
XLA Ops:
  7.2 0.7 all-gather.3.cloned.1.call-update
  7.9 0.7 slice_reduce_fusion
  8.7 0.7 copy.56
  10.5 3.4 %convolution_convert_fusion = bf16[1024,1152]{1,0:T(8,128)(2,1)} fusion(bf16[256,128]{1,0:T(8,128)(2,1)S(1)} %select_convert_fusion, bf16[256,1024]{1,0:T(8,128)(2,1)} %bitcast.81, s32[256]{0:T(256)S(1)} %get-tuple-element.48), kind=kOutput, calls=%fused_computation | convolution fusion | flops 606601216 | bytes 2950144 | tf_op jit(solution)/shard_map/dot_general | solution.py:103
  13.9 12.2 %all-to-all-start = ((bf16[64,16,1152]{2,1,0:T(8,128)(2,1)}), bf16[64,16,1152]{2,1,0:T(8,128)(2,1)S(1)}, u32[]{:S(2)}, u32[]{:S(2)}) async-start(bf16[64,16,1152]{2,1,0:T(8,128)(2,1)} %bitcast.74), calls=%async_computation | async-start | bytes 4718592 | tf_op jit(solution)/shard_map/all_to_all | solution.py:34
  26.1 1.6 fusion.3
  27.9 53.4 %all-to-all-done = bf16[64,16,1152]{2,1,0:T(8,128)(2,1)S(1)} async-done(((bf16[64,16,1152]{2,1,0:T(8,128)(2,1)}), bf16[64,16,1152]{2,1,0:T(8,128)(2,1)S(1)}, u32[]{:S(2)}, u32[]{:S(2)}) %all-to-all-start) | async-done | bytes 2359328 | tf_op jit(solution)/shard_map/all_to_all | solution.py:34
  81.3 6.0 %shard_map.77.part_ref = f32[528,1024]{1,0:T(8,128)S(1)} custom-call(bf16[1024,1152]{1,0:T(8,128)(2,1)S(1)} %bitcast.68, bf16[1024,1152]{1,0:T(8,128)(2,1)S(1)} %bitcast.69), custom_call_target="tpu_custom_call" | custom-call | flops 2214592512 | bytes 5242880 | tf_op jit(solution)/shard_map/pallas_call | solution.py:134
  87.6 3.0 %collective-permute-start.1 = (f32[4,4,1024]{2,1,0:T(4,128)S(1)}, f32[4,4,1024]{2,1,0:T(4,128)S(1)}, u32[]{:S(2)}, u32[]{:S(2)}) collective-permute-start(f32[4,4,1024]{2,1,0:T(4,128)S(1)} %pad_maximum_fusion.2), channel_id=1, source_target_pairs={{1,0},{2,1},{3,2},{4,3},{5,4},{6,5},{7,6},{8,7},{9,8},{10,9},{11,1... | collective-permute-start | bytes 196616 | tf_op jit(solution)/shard_map/ppermute | solution.py:25
  90.7 2.2 collective-permute-start
  92.9 5.4 %collective-permute-done.low_in_ref.pre_low_ref = f32[4,4,1024]{2,1,0:T(4,128)S(1)} collective-permute-done((f32[4,4,1024]{2,1,0:T(4,128)S(1)}, f32[4,4,1024]{2,1,0:T(4,128)S(1)}, u32[]{:S(2)}, u32[]{:S(2)}) %collective-permute-start) | collective-permute-done | bytes 65568 | tf_op jit(solution)/shard_map/ppermute | solution.py:25
  98.4 2.8 %copy-done.4 = bf16[3,1024,1024]{2,1,0:T(8,128)(2,1)S(1)} copy-done((bf16[3,1024,1024]{2,1,0:T(8,128)(2,1)S(1)}, bf16[3,1024,1024]{2,1,0:T(8,128)(2,1)}, u32[]{:S(2)}) %copy-start.4) | copy-done | bytes 6291480
  101.2 5.9 %shard_map.78 = bf16[4,2,528,256]{3,2,1,0:T(8,128)(2,1)S(1)} custom-call(s32[2]{0:T(128)S(1)} %add_convert_fusion.2.valid_ref, f32[528,1024]{1,0:T(8,128)S(1)} %shard_map.77.part_ref, f32[4,4,1024]{2,1,0:T(4,128)S(1)} %collective-permute-done.low_in_ref.pre_low_ref, f32[4,4,1024]{2,1,0:T(4,128)S(1)} %collective-permute-done.1.high_in_ref.pre_high_ref, ...), custom_call_target="tpu_custom_call" | custom-call | flops 3321888768 | bytes 12582912 | tf_op jit(solution)/shard_map/pallas_call | solution.py:229
  107.1 1.4 copy-done
  108.5 4.5 %all-to-all-start.1 = ((bf16[4,1056,256]{2,1,0:T(8,128)(2,1)}), bf16[4,1056,256]{2,1,0:T(8,128)(2,1)S(1)}, u32[]{:S(2)}, u32[]{:S(2)}) async-start(bf16[4,1056,256]{2,1,0:T(8,128)(2,1)} %bitcast.72), calls=%async_computation.1 | async-start | bytes 4325376 | tf_op jit(solution)/shard_map/all_to_all | solution.py:34
  113.0 26.7 %all-to-all-done.1 = bf16[4,1056,256]{2,1,0:T(8,128)(2,1)S(1)} async-done(((bf16[4,1056,256]{2,1,0:T(8,128)(2,1)}), bf16[4,1056,256]{2,1,0:T(8,128)(2,1)S(1)}, u32[]{:S(2)}, u32[]{:S(2)}) %all-to-all-start.1) | async-done | bytes 2162720 | tf_op jit(solution)/shard_map/all_to_all | solution.py:34
  139.7 2.2 copy-done.5
  141.9 5.6 %shard_map.79 = (f32[32,16,768]{2,1,0:T(8,128)S(1)}, bf16[32,16,768]{2,1,0:T(8,128)(2,1)S(1)}) custom-call(s32[5]{0:T(128)S(1)} %stack.31.refs_0_, bf16[4,2,528,256]{3,2,1,0:T(8,128)(2,1)S(1)} %bitcast.70, bf16[2048,1024]{1,0:T(8,128)(2,1)S(1)} %copy-done.5), custom_call_target="tpu_custom_call" | custom-call | flops 3221225472 | bytes 10485760 | tf_op jit(solution)/shard_map/pallas_call | solution.py:303
  147.5 1.2 copy-done.1
  148.7 2.2 copy-done.6
  150.9 5.6 %shard_map.80 = (f32[32,16,768]{2,1,0:T(8,128)S(1)}, bf16[32,16,768]{2,1,0:T(8,128)(2,1)S(1)}) custom-call(s32[5]{0:T(128)S(1)} %stack.31.refs_0_, bf16[4,2,528,256]{3,2,1,0:T(8,128)(2,1)S(1)} %bitcast.71, bf16[2048,1024]{1,0:T(8,128)(2,1)S(1)} %copy-done.6), custom_call_target="tpu_custom_call" | custom-call | flops 3221225472 | bytes 10485760 | tf_op jit(solution)/shard_map/pallas_call | solution.py:303
  156.5 0.8 collective-permute-start.3
  157.3 1.3 add_convert_fusion.1
  159.6 24.4 %all_to_all.20 = bf16[4,256,768]{2,1,0:T(8,128)(2,1)S(1)} all-to-all(bf16[4,256,768]{2,1,0:T(8,128)(2,1)S(1)} %bitcast.75), channel_id=1, replica_groups=mesh['video'=4,'x'=4,'z'=8,'core'=2] {'x'}, dimensions={0} | all-to-all | bytes 3145728 | tf_op jit(solution)/shard_map/all_to_all | solution.py:34
  184.4 20.9 %all_to_all.21 = bf16[8,2,16,768]{3,2,1,0:T(8,128)(2,1)S(1)} all-to-all(bf16[8,2,16,768]{3,2,1,0:T(8,128)(2,1)S(1)} %copy.64), channel_id=1, replica_groups=mesh['video'=4,'x'=4,'z'=8,'core'=2] {'z'}, dimensions={0} | all-to-all | bytes 786432 | tf_op jit(solution)/shard_map/all_to_all | solution.py:34
  205.4 1.8 collective-permute-start.4
  207.2 1.5 collective-permute-start.5
  208.7 1.7 collective-permute-done.4
  210.5 2.9 %collective-permute-done.5 = f32[2,16,768]{2,1,0:T(8,128)S(1)} collective-permute-done((f32[2,16,768]{2,1,0:T(8,128)S(1)}, f32[2,16,768]{2,1,0:T(8,128)S(1)}, u32[]{:S(2)}, u32[]{:S(2)}) %collective-permute-start.5) | collective-permute-done | bytes 98336 | tf_op jit(solution)/shard_map/ppermute | solution.py:30
  213.4 1.2 collective-permute-done.6
  215.1 0.8 copy.65
  215.9 0.8 copy.66
  (66 shorter events, 3.7 us)
Async XLA Ops:
  7.2 105.9 %all-gather.3.cloned.1.call-start = ((), (), s32[]{:S(2)}) async-start(), calls=%async_computation.4 | async-start | bytes 5242880 | tf_op jit(solution)/shard_map/all_gather | solution.py:345
  13.9 12.2 %copy-start.3 = (bf16[4,128,1024]{2,1,0:T(8,128)(2,1)S(1)}, bf16[4,128,1024]{2,1,0:T(8,128)(2,1)}, u32[]{:S(2)}) copy-start(bf16[4,128,1024]{2,1,0:T(8,128)(2,1)} %param.10) | copy-start | bytes 3145732
  13.9 67.4 %all-to-all-start = ((bf16[64,16,1152]{2,1,0:T(8,128)(2,1)}), bf16[64,16,1152]{2,1,0:T(8,128)(2,1)S(1)}, u32[]{:S(2)}, u32[]{:S(2)}) async-start(bf16[64,16,1152]{2,1,0:T(8,128)(2,1)} %bitcast.74), calls=%async_computation | async-start | bytes 4718592 | tf_op jit(solution)/shard_map/all_to_all | solution.py:34
  26.0 122.6 %all-gather.5.cloned.1.call-start = ((), (), s32[]{:S(2)}) async-start(), calls=%async_computation.5 | async-start | bytes 5242880 | tf_op jit(solution)/shard_map/all_gather | solution.py:344
  87.6 5.4 %collective-permute-start.1 = (f32[4,4,1024]{2,1,0:T(4,128)S(1)}, f32[4,4,1024]{2,1,0:T(4,128)S(1)}, u32[]{:S(2)}, u32[]{:S(2)}) collective-permute-start(f32[4,4,1024]{2,1,0:T(4,128)S(1)} %pad_maximum_fusion.2), channel_id=1, source_target_pairs={{1,0},{2,1},{3,2},{4,3},{5,4},{6,5},{7,6},{8,7},{9,8},{10,9},{11,1... | collective-permute-start | bytes 196616 | tf_op jit(solution)/shard_map/ppermute | solution.py:25
  90.7 7.7 %collective-permute-start = (f32[4,4,1024]{2,1,0:T(4,128)S(1)}, f32[4,4,1024]{2,1,0:T(4,128)S(1)}, u32[]{:S(2)}, u32[]{:S(2)}) collective-permute-start(f32[4,4,1024]{2,1,0:T(4,128)S(1)} %pad_maximum_fusion.1), channel_id=1, source_target_pairs={{0,1},{1,2},{2,3},{3,4},{4,5},{5,6},{6,7},{7,8},{8,9},{9,10},{10,1... | collective-permute-start | bytes 196616 | tf_op jit(solution)/shard_map/ppermute | solution.py:25
  98.4 2.8 %copy-start.4 = (bf16[3,1024,1024]{2,1,0:T(8,128)(2,1)S(1)}, bf16[3,1024,1024]{2,1,0:T(8,128)(2,1)}, u32[]{:S(2)}) copy-start(bf16[3,1024,1024]{2,1,0:T(8,128)(2,1)} %taps_ref.1) | copy-start | bytes 18874372
  107.0 1.4 copy-start
  108.5 31.2 %all-to-all-start.1 = ((bf16[4,1056,256]{2,1,0:T(8,128)(2,1)}), bf16[4,1056,256]{2,1,0:T(8,128)(2,1)S(1)}, u32[]{:S(2)}, u32[]{:S(2)}) async-start(bf16[4,1056,256]{2,1,0:T(8,128)(2,1)} %bitcast.72), calls=%async_computation.1 | async-start | bytes 4325376 | tf_op jit(solution)/shard_map/all_to_all | solution.py:34
  139.7 2.2 copy-start.5
  147.5 1.2 copy-start.1
  148.7 8.6 %collective-permute-start.2 = (bf16[32,16,768]{2,1,0:T(8,128)(2,1)S(1)}, bf16[32,16,768]{2,1,0:T(8,128)(2,1)}, u32[]{:S(2)}, u32[]{:S(2)}) collective-permute-start(bf16[32,16,768]{2,1,0:T(8,128)(2,1)S(1)} %get-tuple-element.7), channel_id=1, source_target_pairs={{0,1},{1,0},{2,3},{3,2},{4,5},{5,4},{6,7},{7,6},{8,9},{9,8},{10,11... | collective-permute-start | bytes 2359304 | tf_op jit(solution)/shard_map/ppermute | solution.py:30
  148.7 2.2 copy-start.6
  150.9 6.4 %copy-start.2 = (f32[32,16,768]{2,1,0:T(8,128)S(1)}, f32[32,16,768]{2,1,0:T(8,128)}, u32[]{:S(2)}) copy-start(f32[32,16,768]{2,1,0:T(8,128)} %copy-done.1) | copy-start | bytes 4718596
  156.5 2.7 %collective-permute-start.3 = (bf16[32,16,768]{2,1,0:T(8,128)(2,1)S(1)}, bf16[32,16,768]{2,1,0:T(8,128)(2,1)S(1)}, u32[]{:S(2)}, u32[]{:S(2)}) collective-permute-start(bf16[32,16,768]{2,1,0:T(8,128)(2,1)S(1)} %get-tuple-element.9), channel_id=1, source_target_pairs={{0,1},{1,0},{2,3},{3,2},{4,5},{5,4},{6,7},{7,6},{8,9},{9,8},{10,11... | collective-permute-start | bytes 2359304 | tf_op jit(solution)/shard_map/ppermute | solution.py:30
  205.4 5.1 %collective-permute-start.4 = (f32[2,16,768]{2,1,0:T(8,128)S(1)}, f32[2,16,768]{2,1,0:T(8,128)S(1)}, u32[]{:S(2)}, u32[]{:S(2)}) collective-permute-start(f32[2,16,768]{2,1,0:T(8,128)S(1)} %convert_reduce_fusion), channel_id=1, source_target_pairs={{0,192},{64,0},{128,64},{192,128},{1,193},{65,1},{129,65},{193,129... | collective-permute-start | bytes 294920 | tf_op jit(solution)/shard_map/ppermute | solution.py:30
  207.2 6.1 %collective-permute-start.5 = (f32[2,16,768]{2,1,0:T(8,128)S(1)}, f32[2,16,768]{2,1,0:T(8,128)S(1)}, u32[]{:S(2)}, u32[]{:S(2)}) collective-permute-start(f32[2,16,768]{2,1,0:T(8,128)S(1)} %convert_reduce_fusion), channel_id=1, source_target_pairs={{0,128},{64,192},{128,0},{192,64},{1,129},{65,193},{129,1},{193,65... | collective-permute-start | bytes 294920 | tf_op jit(solution)/shard_map/ppermute | solution.py:30
  208.7 5.8 %collective-permute-start.6 = (f32[2,16,768]{2,1,0:T(8,128)S(1)}, f32[2,16,768]{2,1,0:T(8,128)S(1)}, u32[]{:S(2)}, u32[]{:S(2)}) collective-permute-start(f32[2,16,768]{2,1,0:T(8,128)S(1)} %convert_reduce_fusion), channel_id=1, source_target_pairs={{0,64},{64,128},{128,192},{192,0},{1,65},{65,129},{129,193},{193,1... | collective-permute-start | bytes 294920 | tf_op jit(solution)/shard_map/ppermute | solution.py:30
Sparse Core Ops, SparseCore 0:
  9.8 53.7 all-gather.2
  65.4 52.3 all-gather.4
